TPU v7x, 128 devices: a whole 4x4x4 slice. The times are simulated.
128 devices in a mesh: dp: 8 (over y, core), cent: 16 (over x, z).
Axes of the slice: x: 4, y: 4, z: 4, core: 2. Of those that a mesh axis runs over, the one named last changes fastest.
Arguments:
- points: bfloat16 [32768, 1024], P(('dp', 'cent')), may hold values from -8 to 8
- assign: int32 [32768], P(('dp', 'cent')), may hold values from 0 to 65535, as said below
- parent_one: int32 [65536], P('cent'), may hold values from 0 to 4095, as said below
- parent_two: int32 [4096], replicated, may hold values from 0 to 255, as said below
- old_level_one: bfloat16 [65536, 1024], P('cent', 'dp'), may hold values from -6 to 6
Outputs:
- level_one: float32 [65536, 1024], P('cent', 'dp')
- level_two: float32 [4096, 1024], P('cent', 'dp')
- level_three: float32 [256, 1024], replicated
- residual: bfloat16 [32768, 1024], P(('dp', 'cent'))
Inputs may be any that keep to these rules, and one draw needn't show every extreme that they name: With 32 = 32: the 256 points of one device name at most 32 centroids of one block of 4096 level-1 centroids (block = assign // 4096); for every dp index one block is named by exactly 32 points of every device of that dp index. `parent_one`: every level-2 centroid is the parent of exactly 16 level-1 centroids. `parent_two`: every level-3 centroid is the parent of exactly 16 level-2 centroids.
All inputs are finite; a program needn't handle non-finite values.
Results may differ from a plain program's by a relative error of at most 0.013.
Values may be sent and summed in bfloat16 or wider, within the bound.
No kernel may reach another device: no remote copies, remote signals or barrier semaphores. Data moves between devices by JAX's collectives and lax.ppermute only.
A program may use at most 64 MiB of HBM per device.

v0:
```python
import math

import jax
import jax.numpy as jnp
from jax import lax
from jax.sharding import PartitionSpec as P

K2 = 4096
K3 = 256


HIGH = lax.Precision.HIGHEST


def first_contract(left, right):
    return lax.dot_general(
        left, right, (((0,), (0,)), ((), ())), precision=HIGH, preferred_element_type=jnp.float32
    )


def block_sums(slab, labels, centroid_count, block_rows):
    steps_count = slab.shape[0] // block_rows
    rows_blocks = slab.reshape(steps_count, block_rows, slab.shape[1])
    label_blocks = labels.reshape(steps_count, block_rows)
    columns = jnp.arange(centroid_count, dtype=jnp.int32)[None, :]

    def accumulate(carry, item):
        sums_now, counts_now = carry
        rows_block, labels_block = item
        table = labels_block[:, None] == columns
        added = lax.dot_general(
            table.astype(jnp.bfloat16),
            rows_block,
            (((0,), (0,)), ((), ())),
            preferred_element_type=jnp.float32,
        )
        return ((sums_now + added, counts_now + jnp.sum(table.astype(jnp.float32), axis=0)), None)

    start = (
        jnp.zeros((centroid_count, slab.shape[1]), jnp.float32),
        jnp.zeros((centroid_count,), jnp.float32),
    )
    totals, unused = lax.scan(accumulate, start, (rows_blocks, label_blocks))
    return totals


def block_residual(slab, labels, level_one, block_rows):
    steps_count = slab.shape[0] // block_rows
    rows_blocks = slab.reshape(steps_count, block_rows, slab.shape[1])
    label_blocks = labels.reshape(steps_count, block_rows)
    columns = jnp.arange(level_one.shape[0], dtype=jnp.int32)[None, :]

    def lookup(item):
        rows_block, labels_block = item
        table = (labels_block[:, None] == columns).astype(jnp.float32)
        looked = jnp.dot(table, level_one, precision=HIGH, preferred_element_type=jnp.float32)
        return (rows_block.astype(jnp.float32) - looked).astype(jnp.bfloat16)

    return lax.map(lookup, (rows_blocks, label_blocks)).reshape(slab.shape)


def on_device(points, assign, parent_one, parent_two, old_level_one):
    point_rows, width = points.shape
    owners_count = lax.axis_size("cent")
    groups_count = lax.axis_size("dp")
    capacity = point_rows // 8
    block_size = old_level_one.shape[0]
    slice_width = old_level_one.shape[1]
    slot_count = owners_count * capacity
    owner = assign // block_size
    owner_table = (owner[:, None] == jnp.arange(owners_count, dtype=jnp.int32)[None, :]).astype(
        jnp.float32
    )
    row_ids = jnp.arange(point_rows, dtype=jnp.int32)
    lower = (row_ids[:, None] >= row_ids[None, :]).astype(jnp.float32)
    running = jnp.dot(lower, owner_table, precision=HIGH, preferred_element_type=jnp.float32)
    position = (jnp.sum(running * owner_table, axis=1) - 1.0).astype(jnp.int32)
    slot = owner * capacity + position
    slot_table = jnp.arange(slot_count, dtype=jnp.int32)[:, None] == slot[None, :]
    slot_bf = slot_table.astype(jnp.bfloat16)
    slot_float = slot_table.astype(jnp.float32)
    buffer = jnp.dot(slot_bf, points, preferred_element_type=jnp.float32).astype(jnp.bfloat16)
    local_label = (assign - owner * block_size).astype(jnp.float32)
    label_values = jnp.dot(
        slot_float, local_label, precision=HIGH, preferred_element_type=jnp.float32
    )
    filled = jnp.sum(slot_float, axis=1)
    slot_labels = jnp.where(filled > 0.5, label_values, -1.0).astype(jnp.int32)
    rows_three = buffer.reshape(owners_count, capacity, width)
    labels_three = jnp.broadcast_to(
        slot_labels.reshape(owners_count, capacity, 1), (owners_count, capacity, groups_count)
    )
    moved_rows, moved_labels = (
        lax.all_to_all(
            lax.all_to_all(rows_three, "dp", split_axis=2, concat_axis=1, tiled=True),
            "cent",
            split_axis=0,
            concat_axis=1,
            tiled=True,
        ),
        lax.all_to_all(
            lax.all_to_all(labels_three, "dp", split_axis=2, concat_axis=1, tiled=True),
            "cent",
            split_axis=0,
            concat_axis=1,
            tiled=True,
        ),
    )
    slab_rows = groups_count * owners_count * capacity
    slab = moved_rows.reshape(slab_rows, slice_width)
    slab_labels = moved_labels.reshape(slab_rows)
    block_rows = math.gcd(slab_rows, 1024)
    sums_one, counts_one = block_sums(slab, slab_labels, block_size, block_rows)
    mass_one = sums_one + old_level_one.astype(jnp.float32)
    weight_one = counts_one + 1.0
    level_one = mass_one / weight_one[:, None]
    slab_residual = block_residual(slab, slab_labels, level_one, block_rows)
    shaped = slab_residual.reshape(owners_count, groups_count, capacity, slice_width)
    returned = lax.all_to_all(
        lax.all_to_all(shaped, "dp", split_axis=1, concat_axis=3, tiled=True),
        "cent",
        split_axis=0,
        concat_axis=1,
        tiled=True,
    )
    home_buffer = returned.reshape(owners_count * capacity, width)
    residual = lax.dot_general(
        slot_bf, home_buffer, (((0,), (0,)), ((), ())), preferred_element_type=jnp.float32
    ).astype(jnp.bfloat16)
    parent_table = (parent_one[:, None] == jnp.arange(K2, dtype=jnp.int32)[None, :]).astype(
        jnp.float32
    )
    mass_part = first_contract(parent_table, mass_one)
    weight_part = jnp.dot(
        weight_one, parent_table, precision=HIGH, preferred_element_type=jnp.float32
    )
    share_rows = K2 // owners_count
    share_start = lax.axis_index("cent") * share_rows
    mass_two, weight_two = (
        lax.psum(mass_part.astype(jnp.bfloat16), "cent").astype(jnp.float32),
        lax.psum(weight_part.astype(jnp.bfloat16), "cent").astype(jnp.float32),
    )
    level_all = mass_two / weight_two[:, None]
    level_two = lax.dynamic_slice_in_dim(level_all, share_start, share_rows, 0)
    top_table = (parent_two[:, None] == jnp.arange(K3, dtype=jnp.int32)[None, :]).astype(
        jnp.float32
    )
    mass_three = first_contract(top_table, mass_two)
    weight_three = jnp.dot(
        weight_two, top_table, precision=HIGH, preferred_element_type=jnp.float32
    )
    three_slice = mass_three / weight_three[:, None]
    level_three = lax.all_gather(three_slice, "dp", axis=1, tiled=True)
    return (level_one, level_two, level_three, residual)


def solution(mesh):
    in_specs = (P(("dp", "cent"), None), P(("dp", "cent")), P("cent"), P(), P("cent", "dp"))
    out_specs = (P("cent", "dp"), P("cent", "dp"), P(), P(("dp", "cent"), None))
    return jax.shard_map(
        on_device, mesh=mesh, in_specs=in_specs, out_specs=out_specs, check_vma=False
    )
```

profile of v0, /device:TPU:1, one launch (start us, length us, event | category | flops | bytes accessed | tf_op | source)
XLA Modules:
  0.0 323.9 jit_solution(2420821926642599736)
XLA Ops:
  9.4 6.0 %all-to-all-start = ((s32[8,1,512]{2,1,0:T(1,128)}), s32[8,1,512]{2,1,0:T(1,128)S(1)}, u32[]{:S(2)}, u32[]{:S(2)}) async-start(s32[8,1,512]{2,1,0:T(1,128)} %reshape.52), calls=%async_computation | async-start | bytes 32768 | tf_op jit(solution)/shard_map/all_to_all | solution.py:102
  15.9 4.8 %copy.31 = bf16[16,32,1024]{1,0,2:T(8,128)(2,1)} copy(bf16[16,32,1024]{2,1,0:T(8,128)(2,1)S(1)} %bitcast.72) | data formatting | bytes 2097152 | tf_op jit(solution)/shard_map/reshape | solution.py:89
  20.6 7.8 %reshape.54 = bf16[8,2,32768]{2,1,0:T(2,128)(2,1)} reshape(bf16[1024,16,32]{2,1,0:T(8,128)(2,1)} %bitcast.70) | data formatting | bytes 2097152
  28.5 4.8 %all-to-all-start.2 = ((bf16[8,2,32768]{2,1,0:T(2,128)(2,1)}), bf16[8,2,32768]{2,1,0:T(2,128)(2,1)S(1)}, u32[]{:S(2)}, u32[]{:S(2)}) async-start(bf16[8,2,32768]{2,1,0:T(2,128)(2,1)} %reshape.54), calls=%async_computation.2 | async-start | bytes 2097152 | tf_op jit(solution)/shard_map/all_to_all | solution.py:95
  35.3 13.1 %all-to-all-done.2 = bf16[8,2,32768]{2,1,0:T(2,128)(2,1)S(1)} async-done(((bf16[8,2,32768]{2,1,0:T(2,128)(2,1)}), bf16[8,2,32768]{2,1,0:T(2,128)(2,1)S(1)}, u32[]{:S(2)}, u32[]{:S(2)}) %all-to-all-start.2) | async-done | bytes 1048608 | tf_op jit(solution)/shard_map/all_to_all | solution.py:95
  48.4 7.6 %all-to-all-start.1 = ((s32[16,256,1]{1,2,0:T(1,128)}), s32[16,256,1]{1,2,0:T(1,128)S(1)}, u32[]{:S(2)}, u32[]{:S(2)}) async-start(s32[16,256,1]{1,2,0:T(1,128)} %all_to_all.75), calls=%async_computation.1 | async-start | bytes 32768 | tf_op jit(solution)/shard_map/all_to_all | solution.py:101
  56.0 4.5 %reshape.55 = bf16[1024,16,32]{2,1,0:T(8,128)(2,1)} reshape(bf16[8,2,32768]{2,1,0:T(2,128)(2,1)S(1)} %all-to-all-done.2) | data formatting | bytes 2097152
  60.5 5.3 %copy.33 = bf16[16,8,32,128]{3,2,1,0:T(8,128)(2,1)} copy(bf16[16,8,32,128]{2,0,3,1:T(8,128)(2,1)} %bitcast.71) | data formatting | bytes 2097152 | tf_op jit(solution)/shard_map/all_to_all | solution.py:95
  65.7 6.7 %all-to-all-start.3 = ((bf16[16,256,128]{2,1,0:T(8,128)(2,1)}), bf16[16,256,128]{2,1,0:T(8,128)(2,1)}, u32[]{:S(2)}, u32[]{:S(2)}) async-start(bf16[16,256,128]{2,1,0:T(8,128)(2,1)} %bitcast.8), calls=%async_computation.3 | async-start | bytes 2097152 | tf_op jit(solution)/shard_map/all_to_all | solution.py:94
  72.9 14.7 %all-to-all-done.3 = bf16[16,256,128]{2,1,0:T(8,128)(2,1)} async-done(((bf16[16,256,128]{2,1,0:T(8,128)(2,1)}), bf16[16,256,128]{2,1,0:T(8,128)(2,1)}, u32[]{:S(2)}, u32[]{:S(2)}) %all-to-all-start.3) | async-done | bytes 1048608 | tf_op jit(solution)/shard_map/all_to_all | solution.py:94
  87.6 37.4 %while.25 = (s32[]{:T(128)}, f32[4096,128]{1,0:T(8,128)S(1)}, f32[4096]{0:T(1024)S(1)}, s32[4,1024]{1,0:T(4,128)S(1)}, bf16[4,1024,128]{2,1,0:T(8,128)(2,1)}, /*index=5*/s32[]{:T(128)}, s32[]{:T(128)}) while((s32[]{:T(128)}, f32[4096,128]{1,0:T(8,128)S(1)}, f32[4096]{0:T(1024)S(1)}, s32[4,1024]{1,0:T(4,128)S(1)}, ...), condition=%wide.region_4.5_spmd.clone, body=%wide.region_2.4_spmd.clone.sunk | while | flops 1091571712 | bytes 4538472 | solution.py:43
  87.6 6.5 %fusion.52 = f32[4096,128]{1,0:T(8,128)S(1)} fusion(s32[1024]{0:T(1024)S(1)} %bitcast.75, f32[4096,128]{1,0:T(8,128)S(1)} %get-tuple-element.196, pred[]{:T(512)S(6)} %compare.5, bf16[4,1024,128]{2,1,0:T(8,128)(2,1)} %get-tuple-element.206, s32[]{:T(128)S(6)} %copy.45), kind=kOutput, calls=%fused_computation.15.clone.1 | convolution fusion | flops 1078984704 | bytes 4460549 | tf_op jit(solution)/shard_map/while/body/eval_jaxpr/dot_general | solution.py:31
  94.2 2.8 fusion.53
  97.0 6.5 %fusion.52 = f32[4096,128]{1,0:T(8,128)S(1)} fusion(s32[1024]{0:T(1024)S(1)} %bitcast.75, f32[4096,128]{1,0:T(8,128)S(1)} %get-tuple-element.196, pred[]{:T(512)S(6)} %compare.5, bf16[4,1024,128]{2,1,0:T(8,128)(2,1)} %get-tuple-element.206, s32[]{:T(128)S(6)} %copy.45), kind=kOutput, calls=%fused_computation.15.clone.1 | convolution fusion | flops 1078984704 | bytes 4460549 | tf_op jit(solution)/shard_map/while/body/eval_jaxpr/dot_general | solution.py:31
  103.5 2.8 fusion.53
  106.3 6.5 %fusion.52 = f32[4096,128]{1,0:T(8,128)S(1)} fusion(s32[1024]{0:T(1024)S(1)} %bitcast.75, f32[4096,128]{1,0:T(8,128)S(1)} %get-tuple-element.196, pred[]{:T(512)S(6)} %compare.5, bf16[4,1024,128]{2,1,0:T(8,128)(2,1)} %get-tuple-element.206, s32[]{:T(128)S(6)} %copy.45), kind=kOutput, calls=%fused_computation.15.clone.1 | convolution fusion | flops 1078984704 | bytes 4460549 | tf_op jit(solution)/shard_map/while/body/eval_jaxpr/dot_general | solution.py:31
  112.8 2.8 fusion.53
  115.6 6.5 %fusion.52 = f32[4096,128]{1,0:T(8,128)S(1)} fusion(s32[1024]{0:T(1024)S(1)} %bitcast.75, f32[4096,128]{1,0:T(8,128)S(1)} %get-tuple-element.196, pred[]{:T(512)S(6)} %compare.5, bf16[4,1024,128]{2,1,0:T(8,128)(2,1)} %get-tuple-element.206, s32[]{:T(128)S(6)} %copy.45), kind=kOutput, calls=%fused_computation.15.clone.1 | convolution fusion | flops 1078984704 | bytes 4460549 | tf_op jit(solution)/shard_map/while/body/eval_jaxpr/dot_general | solution.py:31
  122.2 2.8 fusion.53
  128.2 56.5 %fusion.22 = bf16[4096,128]{1,0:T(8,128)(2,1)} fusion(s32[4096]{0:T(1024)S(1)} %copy-done.3, f32[4096,128]{1,0:T(8,128)S(1)} %convert_add_fusion.6), kind=kOutput, calls=%fused_computation.26 | convolution fusion | flops 25787105280 | bytes 3162112 | tf_op jit(solution)/shard_map/dot_general | solution.py:16
  184.8 36.8 %while.24 = (s32[]{:T(128)}, bf16[4,1024,128]{2,1,0:T(8,128)(2,1)}, bf16[4,1024,128]{2,1,0:T(8,128)(2,1)}, s32[4,1024]{1,0:T(4,128)S(1)}, f32[4096,128]{1,0:T(8,128)S(1)}, /*index=5*/s32[]{:T(128)}) while((s32[]{:T(128)}, bf16[4,1024,128]{2,1,0:T(8,128)(2,1)}, bf16[4,1024,128]{2,1,0:T(8,128)(2,1)}, s32[4,1024]{1,0:T(4,128)S(1)}, ...), condition=%wide.region_8.9_spmd.clone, body=%wide.region_7.8_spmd.clone.sunk | while | flops 6447038464 | bytes 2633813 | solution.py:59
  184.8 9.2 %fusion.50 = bf16[4,1024,128]{2,1,0:T(8,128)(2,1)} fusion(bf16[4,1024,128]{2,1,0:T(8,128)(2,1)} %get-tuple-element.216, s32[]{:T(128)S(6)} %copy.54, f32[4096,128]{1,0:T(8,128)S(1)} %get-tuple-element.225, s32[1024]{0:T(1024)S(1)} %bitcast.77, bf16[4,1024,128]{2,1,0:T(8,128)(2,1)} %get-tuple-element.223), kind=kOutput, calls=%fused_computation.8.clone.1 | convolution fusion | flops 6447038464 | bytes 2625540 | tf_op jit(solution)/shard_map/while/body/eval_jaxpr/dot_general | solution.py:56
  194.0 9.2 %fusion.50 = bf16[4,1024,128]{2,1,0:T(8,128)(2,1)} fusion(bf16[4,1024,128]{2,1,0:T(8,128)(2,1)} %get-tuple-element.216, s32[]{:T(128)S(6)} %copy.54, f32[4096,128]{1,0:T(8,128)S(1)} %get-tuple-element.225, s32[1024]{0:T(1024)S(1)} %bitcast.77, bf16[4,1024,128]{2,1,0:T(8,128)(2,1)} %get-tuple-element.223), kind=kOutput, calls=%fused_computation.8.clone.1 | convolution fusion | flops 6447038464 | bytes 2625540 | tf_op jit(solution)/shard_map/while/body/eval_jaxpr/dot_general | solution.py:56
  203.2 9.2 %fusion.50 = bf16[4,1024,128]{2,1,0:T(8,128)(2,1)} fusion(bf16[4,1024,128]{2,1,0:T(8,128)(2,1)} %get-tuple-element.216, s32[]{:T(128)S(6)} %copy.54, f32[4096,128]{1,0:T(8,128)S(1)} %get-tuple-element.225, s32[1024]{0:T(1024)S(1)} %bitcast.77, bf16[4,1024,128]{2,1,0:T(8,128)(2,1)} %get-tuple-element.223), kind=kOutput, calls=%fused_computation.8.clone.1 | convolution fusion | flops 6447038464 | bytes 2625540 | tf_op jit(solution)/shard_map/while/body/eval_jaxpr/dot_general | solution.py:56
  212.4 9.2 %fusion.50 = bf16[4,1024,128]{2,1,0:T(8,128)(2,1)} fusion(bf16[4,1024,128]{2,1,0:T(8,128)(2,1)} %get-tuple-element.216, s32[]{:T(128)S(6)} %copy.54, f32[4096,128]{1,0:T(8,128)S(1)} %get-tuple-element.225, s32[1024]{0:T(1024)S(1)} %bitcast.77, bf16[4,1024,128]{2,1,0:T(8,128)(2,1)} %get-tuple-element.223), kind=kOutput, calls=%fused_computation.8.clone.1 | convolution fusion | flops 6447038464 | bytes 2625540 | tf_op jit(solution)/shard_map/while/body/eval_jaxpr/dot_general | solution.py:56
  223.9 6.6 %all-to-all-start.4 = ((bf16[16,8,32,128]{3,2,0,1:T(8,128)(2,1)}), bf16[16,8,32,128]{3,2,0,1:T(8,128)(2,1)S(1)}, u32[]{:S(2)}, u32[]{:S(2)}) async-start(bf16[16,8,32,128]{3,2,0,1:T(8,128)(2,1)} %copy.34), calls=%async_computation.4 | async-start | bytes 2097152 | tf_op jit(solution)/shard_map/all_to_all | solution.py:120
  230.5 21.7 %fusion.18 = f32[1,4096]{1,0:T(1,128)S(1)} fusion(f32[4096,1]{0,1:T(1,128)S(1)} %bitcast.78, s32[4096]{0:T(1024)S(1)} %copy-done.3), kind=kOutput, calls=%fused_computation.22 | convolution fusion | flops 218103808 | bytes 49152 | tf_op jit(solution)/shard_map/dot_general | solution.py:134
  252.2 30.1 %psum.15 = bf16[4096]{0:T(1024)(128)(2,1)S(1)} all-reduce(bf16[4096]{0:T(1024)(128)(2,1)S(1)} %convert_element_type.60), channel_id=1, replica_groups=mesh['dp'=8,'cent'=16] {'cent'}, use_global_device_ids=true, to_apply=%region_6.7 | all-reduce | flops 4096 | bytes 16384 | tf_op jit(solution)/shard_map/psum | solution.py:141
  283.1 3.8 %fusion.28 = f32[256,128]{1,0:T(8,128)} fusion(bf16[4096,128]{1,0:T(8,128)(2,1)} %all-reduce.2.cloned.1.call-done, s32[4096]{0:T(1024)S(1)} %copy-done.4, f32[256]{0:T(256)S(1)} %bitcast.82), kind=kOutput, calls=%fused_computation.36 | convolution fusion | flops 269516800 | bytes 1197056 | tf_op jit(solution)/shard_map/dot_general | solution.py:16
  288.1 3.7 %all-to-all-start.5 = ((bf16[16,1,32,1024]{3,2,1,0:T(8,128)(2,1)}), bf16[16,1,32,1024]{3,2,1,0:T(8,128)(2,1)S(1)}, u32[]{:S(2)}, u32[]{:S(2)}) async-start(bf16[16,1,32,1024]{3,2,1,0:T(8,128)(2,1)} %bitcast_bitcast_fusion), calls=%async_computation.5 | async-start | bytes 2097152 | tf_op jit(solution)/shard_map/all_to_all | solution.py:119
  293.4 10.1 %all-to-all-done.5 = bf16[16,1,32,1024]{3,2,1,0:T(8,128)(2,1)S(1)} async-done(((bf16[16,1,32,1024]{3,2,1,0:T(8,128)(2,1)}), bf16[16,1,32,1024]{3,2,1,0:T(8,128)(2,1)S(1)}, u32[]{:S(2)}, u32[]{:S(2)}) %all-to-all-start.5) | async-done | bytes 1048608 | tf_op jit(solution)/shard_map/all_to_all | solution.py:119
  304.8 9.8 %all-gather.2.cloned.1.call-done = f32[256,1024]{1,0:T(8,128)} async-done(((f32[256,128]{1,0:T(8,128)}), f32[256,1024]{1,0:T(8,128)}) %all-gather.2.cloned.1.call-update) | async-done | bytes 1048592 | tf_op jit(solution)/shard_map/all_gather | solution.py:153
  (63 shorter events, 18.0 us)
Async XLA Ops:
  7.2 8.2 %copy-start = (bf16[256,1024]{1,0:T(8,128)(2,1)S(1)}, bf16[256,1024]{1,0:T(8,128)(2,1)}, u32[]{:S(2)}) copy-start(bf16[256,1024]{1,0:T(8,128)(2,1)} %param.9) | copy-start | bytes 1572868
  9.4 19.0 %all-to-all-start = ((s32[8,1,512]{2,1,0:T(1,128)}), s32[8,1,512]{2,1,0:T(1,128)S(1)}, u32[]{:S(2)}, u32[]{:S(2)}) async-start(s32[8,1,512]{2,1,0:T(1,128)} %reshape.52), calls=%async_computation | async-start | bytes 32768 | tf_op jit(solution)/shard_map/all_to_all | solution.py:102
  28.5 19.9 %all-to-all-start.2 = ((bf16[8,2,32768]{2,1,0:T(2,128)(2,1)}), bf16[8,2,32768]{2,1,0:T(2,128)(2,1)S(1)}, u32[]{:S(2)}, u32[]{:S(2)}) async-start(bf16[8,2,32768]{2,1,0:T(2,128)(2,1)} %reshape.54), calls=%async_computation.2 | async-start | bytes 2097152 | tf_op jit(solution)/shard_map/all_to_all | solution.py:95
  48.4 17.3 %all-to-all-start.1 = ((s32[16,256,1]{1,2,0:T(1,128)}), s32[16,256,1]{1,2,0:T(1,128)S(1)}, u32[]{:S(2)}, u32[]{:S(2)}) async-start(s32[16,256,1]{1,2,0:T(1,128)} %all_to_all.75), calls=%async_computation.1 | async-start | bytes 32768 | tf_op jit(solution)/shard_map/all_to_all | solution.py:101
  65.7 21.9 %all-to-all-start.3 = ((bf16[16,256,128]{2,1,0:T(8,128)(2,1)}), bf16[16,256,128]{2,1,0:T(8,128)(2,1)}, u32[]{:S(2)}, u32[]{:S(2)}) async-start(bf16[16,256,128]{2,1,0:T(8,128)(2,1)} %bitcast.8), calls=%async_computation.3 | async-start | bytes 2097152 | tf_op jit(solution)/shard_map/all_to_all | solution.py:94
  72.4 210.7 %all-reduce.2.cloned.1.call-start = ((), (), s32[]{:S(2)}) async-start(), calls=%async_computation.6 | async-start | bytes 2097152 | tf_op jit(solution)/shard_map/psum | solution.py:140
  125.0 1.5 copy-start.1
  126.5 1.7 copy-start.3
  128.2 56.6 %copy-start.2 = (f32[4096,128]{1,0:T(8,128)S(1)}, f32[4096,128]{1,0:T(8,128)}, u32[]{:S(2)}) copy-start(f32[4096,128]{1,0:T(8,128)} %fusion.27) | copy-start | bytes 6291460
  223.9 63.1 %all-to-all-start.4 = ((bf16[16,8,32,128]{3,2,0,1:T(8,128)(2,1)}), bf16[16,8,32,128]{3,2,0,1:T(8,128)(2,1)S(1)}, u32[]{:S(2)}, u32[]{:S(2)}) async-start(bf16[16,8,32,128]{3,2,0,1:T(8,128)(2,1)} %copy.34), calls=%async_computation.4 | async-start | bytes 2097152 | tf_op jit(solution)/shard_map/all_to_all | solution.py:120
  230.5 84.1 %all-gather.2.cloned.1.call-start = ((), (), s32[]{:S(2)}) async-start(), calls=%async_computation.7 | async-start | bytes 1179648 | tf_op jit(solution)/shard_map/all_gather | solution.py:153
  230.5 51.8 %copy-start.4 = (s32[4096]{0:T(1024)S(1)}, s32[4096]{0:T(1024)}, u32[]{:S(2)}) copy-start(s32[4096]{0:T(1024)} %param.12) | copy-start | bytes 49156
  288.1 15.4 %all-to-all-start.5 = ((bf16[16,1,32,1024]{3,2,1,0:T(8,128)(2,1)}), bf16[16,1,32,1024]{3,2,1,0:T(8,128)(2,1)S(1)}, u32[]{:S(2)}, u32[]{:S(2)}) async-start(bf16[16,1,32,1024]{3,2,1,0:T(8,128)(2,1)} %bitcast_bitcast_fusion), calls=%async_computation.5 | async-start | bytes 2097152 | tf_op jit(solution)/shard_map/all_to_all | solution.py:119
Sparse Core Ops, SparseCore 0:
  184.9 84.1 all-reduce.1
  287.1 27.4 all-gather.1
where the time goes:
time: 329 us; the launch traced here: 324 us
  matrix products  148 us (45%)
  waiting for transfers between devices  47.7 us (14%)
  starting transfers between devices  35.6 us (11%)
  local copies, waits for them, and re-layouts  30.5 us (9%)
  blocking collectives  30.1 us (9%)
  other arithmetic  17.5 us (5%)
  between operations  14.5 us (4%)
    dot_general x2, matrix products, first_contract(): lax.dot_general(left, right, (((0,), (0,)), ((), ())), precision=HIGH, pr...  60.4 us
    dot_general x4, matrix products, lookup(): jnp.dot(table, level_one, precision=HIGH, preferred_element_type=jnp.floa...  36.7 us
    psum x1, blocking collectives, on_device(): lax.psum(weight_part.astype(jnp.bfloat16), 'cent').astype(jnp.float32)  30.1 us
    dot_general x4, matrix products, accumulate(): lax.dot_general(table.astype(jnp.bfloat16), rows_block, (((0,), (0,)), ((...  26.1 us
    dot_general x1, matrix products, on_device(): jnp.dot(weight_one, parent_table, precision=HIGH, preferred_element_type=...  21.7 us
    unnamed x16, local copies, waits for them, and re-layouts  15.5 us
    all_to_all x1, waiting for transfers between devices, on_device(): lax.all_to_all(lax.all_to_all(rows_three, 'dp', split_axis=2, concat_axis...  14.7 us
    all_to_all x1, waiting for transfers between devices, on_device(): lax.all_to_all(rows_three, 'dp', split_axis=2, concat_axis=1, tiled=True)  13.1 us
  transfers between devices with their start and end apart: 8, of which 4 were waited for; matrix products, arithmetic and copies ran while one was open for 29% of the time, Pallas kernels for 0%

commit v1 on v0

v1 whole, which is shorter than its diff:
```python
import jax
import jax.numpy as jnp
from jax import lax
from jax.experimental import pallas as pl
from jax.experimental.pallas import tpu as pltpu
from jax.sharding import PartitionSpec as P

F32 = jnp.float32
BF16 = jnp.bfloat16
I32 = jnp.int32
LANES = 128
CHUNK = 512
LOW = 512
HIGHS = 8
CAP = 32
EXTRA = 8
BOTH = ("dp", "cent")


def iota(shape, axis):
    return lax.broadcasted_iota(I32, shape, axis)


def dot(left, right):
    return jnp.dot(left, right, preferred_element_type=F32)


def dot_nt(left, right):
    return lax.dot_general(left, right, (((1,), (1,)), ((), ())), preferred_element_type=F32)


def call(body, out_shape, scratch=(), flops=0, size=4 << 20, vmem=24 << 20):
    return pl.pallas_call(
        body,
        out_shape=out_shape,
        scratch_shapes=list(scratch),
        compiler_params=pltpu.CompilerParams(vmem_limit_bytes=vmem),
        cost_estimate=pl.CostEstimate(flops=flops, bytes_accessed=size, transcendentals=0),
    )


def pack_kernel(assign_ref, points_ref, send_ref, back_ref):
    count = assign_ref.shape[1]
    owners = send_ref.shape[1]
    label = assign_ref[...]
    owner = lax.shift_right_logical(label, 12)
    local = label & 4095
    mine = iota((owners, count), 0) == owner
    mine_f = jnp.where(mine, 1.0, 0.0)
    before = jnp.where(iota((count, count), 0) <= iota((count, count), 1), 1.0, 0.0).astype(BF16)
    running = dot(mine_f.astype(BF16), before)
    place = jnp.sum(running * mine_f, axis=0, keepdims=True).astype(I32) - 1
    slot = owner * CAP + place
    table = jnp.where(iota((owners * CAP, count), 0) == slot, 1.0, 0.0).astype(BF16)
    same = jnp.where(iota((count, count), 0) == iota((count, count), 1), 1.0, 0.0).astype(BF16)
    back_ref[...] = dot_nt(same, table).astype(BF16)
    shift = (lax.axis_index("cent") % 4) * CAP
    lane_table = jnp.where(iota((LANES, count), 0) == place + shift, 1.0, 0.0).astype(BF16)
    high = (lax.shift_right_logical(local, 6) + 1).astype(F32)
    low = ((local & 63) + 1).astype(F32)
    high_rows = dot_nt((mine_f * high).astype(BF16), lane_table)
    low_rows = dot_nt((mine_f * low).astype(BF16), lane_table)
    row = iota((owners, EXTRA, LANES), 1)
    extra = jnp.where(row == 0, high_rows[:, None, :], jnp.where(row == 1, low_rows[:, None, :], 0.0))
    extra = extra.astype(BF16)
    for part in range(send_ref.shape[0]):
        rows = dot(table, points_ref[:, part * LANES : (part + 1) * LANES]).astype(BF16)
        send_ref[part, :, 0:CAP, :] = rows.reshape(owners, CAP, LANES)
        send_ref[part, :, CAP : CAP + EXTRA, :] = extra


def slot_digits(slab_ref, digits_ref):
    rows = slab_ref[:, CAP : CAP + EXTRA, :].astype(F32).reshape(-1, LANES).astype(BF16)
    shape = (64, rows.shape[0])
    column, line = iota(shape, 1), iota(shape, 0)
    pick = (lax.shift_right_logical(column, 5) == (line & 31)) & (
        (column & 7) == lax.shift_right_logical(line, 5)
    )
    digits_ref[...] = dot(jnp.where(pick, 1.0, 0.0).astype(BF16), rows)


def digit_rows(digits_ref, at):
    return digits_ref[pl.ds(at, 1), :], digits_ref[pl.ds(at + 32, 1), :]


def across_lanes(digits_ref, step):
    found = []
    for part in range(CHUNK // LANES):
        high, low = digit_rows(digits_ref, step * (CHUNK // LANES) + part)
        found.append((high * 64.0 + low).astype(I32) - 65)
    return found


def down_rows(digits_ref, step):
    same = iota((LANES, LANES), 0) == iota((LANES, LANES), 1)
    parts = []
    for part in range(CHUNK // LANES):
        high, low = digit_rows(digits_ref, step * (CHUNK // LANES) + part)
        parts.append(
            jnp.concatenate([jnp.where(same, high, 0.0), jnp.where(same, low, 0.0)], axis=1)
        )
    left = jnp.concatenate(parts, axis=0).astype(BF16)
    right = jnp.where(iota((2 * LANES, LANES), 0) < LANES, 64.0, 1.0).astype(BF16)
    return dot(left, right).astype(I32) - 65


def add_segments(total_ref, digits_ref, step, rows):
    line = iota((LOW, LANES), 0)
    left = jnp.concatenate(
        [
            jnp.where(line == (label & (LOW - 1)), 1.0, 0.0).astype(BF16)
            for label in across_lanes(digits_ref, step)
        ],
        axis=1,
    )
    high = lax.shift_right_arithmetic(down_rows(digits_ref, step), 9)
    wide = rows.astype(F32)
    for pair in range(HIGHS // 2):
        right = jnp.concatenate(
            [jnp.where(high == 2 * pair + side, wide, 0.0).astype(BF16) for side in range(2)], axis=1
        )
        at = slice(2 * pair * LANES, (2 * pair + 2) * LANES)
        total_ref[:, at] += dot(left, right)
    lane = iota((CHUNK, LANES), 1)
    ones = jnp.where((high == (lane & 7)) & (lane < 16), 1.0, 0.0).astype(BF16)
    total_ref[:, HIGHS * LANES :] += dot(left, ones)


def parent_kernel(parent_ref, old_ref, total_ref, digits_ref):
    parent = parent_ref[...]
    digits_ref[0:32, :] = (lax.shift_right_logical(parent, 6) + 1).astype(F32)
    digits_ref[32:64, :] = ((parent & 63) + 1).astype(F32)
    total_ref[...] = jnp.zeros_like(total_ref)

    def step(at, carry):
        rows = old_ref[pl.ds(pl.multiple_of(at * CHUNK, CHUNK), CHUNK), :]
        add_segments(total_ref, digits_ref, at, rows)
        return carry

    lax.fori_loop(0, old_ref.shape[0] // CHUNK, step, 0)


def slab_rows(slab_ref, at):
    sources = CHUNK // CAP
    return slab_ref[pl.ds(at * sources, sources), 0:CAP, :].reshape(CHUNK, LANES)


def upper_kernel(slab_ref, table_ref, top_ref, start_ref, send_ref, digits_ref, parents_ref, total_ref):
    slot_digits(slab_ref, digits_ref)
    total_ref[...] = start_ref[...]
    steps = slab_ref.shape[0] * CAP // CHUNK
    line = iota((LANES, LANES), 0)

    def step(at, carry):
        for part in range(CHUNK // LANES):
            row = at * (CHUNK // LANES) + part
            high, low = digit_rows(digits_ref, row)
            left = jnp.where(line == high.astype(I32) - 1, 1.0, 0.0).astype(BF16)
            found = dot(table_ref[...], left)
            found = jnp.where((line & 63) == low.astype(I32) - 1, found, 0.0)
            parents_ref[pl.ds(row, 1), :] = jnp.sum(found[0:64], axis=0, keepdims=True)
            parents_ref[pl.ds(row + 32, 1), :] = jnp.sum(found[64:128], axis=0, keepdims=True)
        add_segments(total_ref, parents_ref, at, slab_rows(slab_ref, at))
        return carry

    lax.fori_loop(0, steps, step, 0)
    weights = total_ref[:, HIGHS * LANES :]
    coarse = weights.astype(BF16).astype(F32)
    fine = weights - coarse
    lane = iota((LOW, LANES), 1)
    tops = jnp.zeros((256, 2 * LANES), F32)
    for high in range(HIGHS):
        mass = total_ref[:, high * LANES : (high + 1) * LANES].astype(BF16)
        for half in range(2):
            send_ref[2 * high + half, 0:256, :] = mass[half * 256 : (half + 1) * 256]
        heavy = jnp.where(lane == high, coarse, jnp.where(lane == high + 8, fine, 0.0)).astype(BF16)
        left = jnp.concatenate(
            [
                jnp.where(
                    iota((256, LANES), 0) == top_ref[high * 4 + part : high * 4 + part + 1, :], 1.0, 0.0
                ).astype(BF16)
                for part in range(4)
            ],
            axis=1,
        )
        tops += dot(left, jnp.concatenate([mass, heavy], axis=1))
    top_mass = tops[:, :LANES].astype(BF16)
    top_weight = jnp.sum(tops[:, LANES:].T[0:16], axis=0, keepdims=True)
    top_coarse = top_weight.astype(BF16).astype(F32)
    top_fine = top_weight - top_coarse
    coarse_t, fine_t = coarse.T, fine.T
    for owner in range(send_ref.shape[0]):
        send_ref[owner, 256:272, :] = top_mass[owner * 16 : (owner + 1) * 16]
        high, from_lane = owner // 2, (owner % 2) * 256
        rows = []
        for source, line_at, lane_at in (
            (coarse_t, high, from_lane),
            (fine_t, high, from_lane),
            (top_coarse, 0, 0),
            (top_fine, 0, 0),
        ):
            for half in range(2):
                first = lane_at + half * LANES
                rows.append(source[line_at : line_at + 1, first : first + LANES])
        send_ref[owner, 272:280, :] = jnp.concatenate(rows, axis=0).astype(BF16)


def level_kernel(slab_ref, old_ref, level_ref, residual_ref, digits_ref, total_ref, table_ref):
    slot_digits(slab_ref, digits_ref)
    total_ref[...] = jnp.zeros_like(total_ref)
    steps = slab_ref.shape[0] * CAP // CHUNK

    def gather(at, carry):
        add_segments(total_ref, digits_ref, at, slab_rows(slab_ref, at))
        return carry

    lax.fori_loop(0, steps, gather, 0)
    inverse = 1.0 / (total_ref[:, HIGHS * LANES :] + 1.0)
    for high in range(HIGHS):
        lines = slice(high * LOW, (high + 1) * LOW)
        lanes = slice(high * LANES, (high + 1) * LANES)
        mass = total_ref[:, lanes] + old_ref[lines, :].astype(F32)
        level = mass * jnp.broadcast_to(inverse[:, high : high + 1], mass.shape)
        level_ref[lines, :] = level
        table_ref[:, lanes] = level.astype(BF16)

    def subtract(at, carry):
        label = down_rows(digits_ref, at)
        low = label & (LOW - 1)
        high = lax.shift_right_arithmetic(label, 9)
        lane = iota((CHUNK, LANES), 1)
        left = jnp.concatenate(
            [
                jnp.where(low == lane + part * LANES, 1.0, 0.0).astype(BF16)
                for part in range(LOW // LANES)
            ],
            axis=1,
        )
        rows = slab_rows(slab_ref, at).astype(F32)
        for pair in range(HIGHS // 2):
            found = dot(left, table_ref[:, 2 * pair * LANES : (2 * pair + 2) * LANES])
            for side in range(2):
                chosen = found[:, side * LANES : (side + 1) * LANES]
                rows -= jnp.where(high == 2 * pair + side, chosen, 0.0)
        sources = CHUNK // CAP
        residual_ref[pl.ds(at * sources, sources), :, :] = rows.astype(BF16).reshape(
            sources, CAP, LANES
        )
        return carry

    lax.fori_loop(0, steps, subtract, 0)


def finish_kernel(parts_ref, level_ref, send_ref, column_ref):
    total = parts_ref[0].astype(F32)
    for source in range(1, parts_ref.shape[0]):
        total += parts_ref[source].astype(F32)
    tail = total[272:280].T
    for half in range(2):
        weight = tail[:, half : half + 1] + tail[:, half + 2 : half + 3]
        lines = slice(half * LANES, (half + 1) * LANES)
        level_ref[lines, :] = total[lines] / jnp.broadcast_to(weight, (LANES, LANES))
    me = lax.axis_index("cent")
    first = tail[:, 4:5] + tail[:, 6:7]
    second = tail[:, 5:6] + tail[:, 7:8]
    chosen = jnp.where(me < 8, first, second)
    column_ref[...] = jnp.broadcast_to(chosen, (LANES, LANES))
    weight = column_ref[pl.ds(pl.multiple_of((me % 8) * 16, 16), 16), :]
    top = (total[256:272] / weight).astype(BF16)
    send_ref[...] = jnp.broadcast_to(top[None], send_ref.shape)


def unpack_kernel(back_ref, returned_ref, residual_ref):
    owners, cap, lanes = returned_ref.shape[1:]
    for pair in range(returned_ref.shape[0] // 2):
        right = jnp.concatenate(
            [returned_ref[2 * pair + side].reshape(owners * cap, lanes) for side in range(2)], axis=1
        )
        residual_ref[:, 2 * pair * lanes : (2 * pair + 2) * lanes] = dot(back_ref[...], right).astype(BF16)


def top_kernel(parts_ref, level_ref):
    for part in range(parts_ref.shape[0]):
        rows = parts_ref[part].reshape(level_ref.shape[0], LANES)
        level_ref[:, part * LANES : (part + 1) * LANES] = rows.astype(F32)


def shape(dims, kind):
    return jax.ShapeDtypeStruct(dims, kind)


def swap(value, axes):
    return lax.all_to_all(value, axes, split_axis=0, concat_axis=0, tiled=True)


def on_device(points, assign, parent_one, parent_two, old_level_one):
    count, width = points.shape
    owners = lax.axis_size("cent")
    groups = lax.axis_size("dp")
    devices = owners * groups
    block, lanes = old_level_one.shape
    slots = owners * CAP
    rows = CAP + EXTRA
    total_shape = shape((LOW, (HIGHS + 1) * LANES), F32)
    work = 2 * LOW * block * (HIGHS + 1) * LANES

    send, back = call(
        pack_kernel,
        (shape((groups, owners, rows, lanes), BF16), shape((count, slots), BF16)),
        flops=2 * slots * count * width,
    )(assign.reshape(1, count), points)
    slab = swap(send.reshape(devices, rows, lanes), BOTH)

    start = call(
        parent_kernel, total_shape, [pltpu.VMEM((64, LANES), F32)], flops=work
    )(parent_one.reshape(block // LANES, LANES), old_level_one)
    grid = parent_one.reshape(64, 64).T
    table = jnp.concatenate([lax.shift_right_logical(grid, 6), grid & 63], axis=0) + 1
    table = jnp.pad(table, ((0, 0), (0, 64))).astype(BF16)

    share = call(
        upper_kernel,
        shape((owners, 280, lanes), BF16),
        [
            pltpu.VMEM((64, LANES), F32),
            pltpu.VMEM((64, LANES), F32),
            pltpu.VMEM(total_shape.shape, F32),
        ],
        flops=work,
    )(slab, table, parent_two.reshape(-1, LANES), start)
    shares = swap(share, "cent")

    level_one, slab_residual = call(
        level_kernel,
        (shape((block, lanes), F32), shape((devices, CAP, lanes), BF16)),
        [
            pltpu.VMEM((64, LANES), F32),
            pltpu.VMEM(total_shape.shape, F32),
            pltpu.VMEM((LOW, HIGHS * LANES), BF16),
        ],
        flops=2 * work,
    )(slab, old_level_one)
    returned = swap(slab_residual, BOTH)

    level_two, top = call(
        finish_kernel,
        (shape((256, lanes), F32), shape((devices, 16, lanes), BF16)),
        [pltpu.VMEM((LANES, LANES), F32)],
    )(shares)
    tops = swap(top, BOTH)
    residual = call(unpack_kernel, shape((count, width), BF16), flops=2 * slots * count * width)(
        back, returned.reshape(groups, owners, CAP, lanes)
    )
    level_three = call(top_kernel, shape((owners * 16, width), F32))(
        tops.reshape(groups, owners, 16, lanes)
    )
    return (level_one, level_two, level_three, residual)


def solution(mesh):
    in_specs = (P(("dp", "cent"), None), P(("dp", "cent")), P("cent"), P(), P("cent", "dp"))
    out_specs = (P("cent", "dp"), P("cent", "dp"), P(), P(("dp", "cent"), None))
    return jax.shard_map(
        on_device, mesh=mesh, in_specs=in_specs, out_specs=out_specs, check_vma=False
    )
```

time: 329 us -> 121 us (0.37); the launches traced: 324 us -> 120 us
  matrix products: 148 us -> 0 us
  Pallas kernels: 0 us -> 42.8 us
  blocking collectives: 30.1 us -> 0 us
  local copies, waits for them, and re-layouts: 30.5 us -> 7.37 us
  other arithmetic: 17.5 us -> 0.04 us
  between operations: 14.5 us -> 0.77 us
  waiting for transfers between devices: 47.7 us -> 40.5 us
  starting transfers between devices: 35.6 us -> 28.8 us
    dot_general x16 -> x0, matrix products: 148 us -> none  [the longest x2 60.4 us: first_contract(): lax.dot_general(left, right, (((0,), (0,)), ((), ())), precision=HIGH, pr...]
    pallas_call x0 -> x7, Pallas kernels: none -> 42.8 us  [the longest x1 17.5 us: on_device(): call(level_kernel, (shape((block, lanes), F32), shape((devices, CAP, lane...]
    psum x1 -> x0, blocking collectives: 30.1 us -> none  [on_device(): lax.psum(weight_part.astype(jnp.bfloat16), 'cent').astype(jnp.float32)]
    reduce_sum x5 -> x0, other arithmetic: 11.2 us -> none  [the longest x4 11 us: accumulate(): jnp.sum(table.astype(jnp.float32), axis=0)]
    all_gather x1 -> x0, waiting for transfers between devices: 9.77 us -> none  [on_device(): level_three = lax.all_gather(three_slice, 'dp', axis=1, tiled=True)]
    unnamed x16 -> x18, local copies, waits for them, and re-layouts: 15.5 us -> 7.06 us
    all_to_all x6 -> x0, local copies, waits for them, and re-layouts: 7.63 us -> none  [the longest x1 5.25 us: on_device(): lax.all_to_all(rows_three, 'dp', split_axis=2, concat_axis=1, tiled=True)]
    all_to_all x6 -> x4, starting transfers between devices: 35.3 us -> 28.8 us  [swap(): return lax.all_to_all(value, axes, split_axis=0, concat_axis=0, tiled=True)]
  transfers between devices with their start and end apart: 8 -> 4, of which waited for: 4 -> 3; matrix products, arithmetic and copies ran while one was open for 29% -> 0% of each run, Pallas kernels for 0% -> 24%
where the time goes in v1:
time: 121 us; the launch traced here: 120 us
  Pallas kernels  42.8 us (35%)
  waiting for transfers between devices  40.5 us (33%)
  starting transfers between devices  28.8 us (24%)
  local copies, waits for them, and re-layouts  7.37 us (6%)
    all_to_all x4, waiting for transfers between devices, swap(): return lax.all_to_all(value, axes, split_axis=0, concat_axis=0, tiled=True)  40.5 us
    all_to_all x4, starting transfers between devices, swap(): return lax.all_to_all(value, axes, split_axis=0, concat_axis=0, tiled=True)  28.8 us
    pallas_call x1, Pallas kernels, on_device(): call(level_kernel, (shape((block, lanes), F32), shape((devices, CAP, lane...  17.5 us
    pallas_call x1, Pallas kernels, on_device(): call(upper_kernel, shape((owners, 280, lanes), BF16), [pltpu.VMEM((64, LA...  10.9 us
    pallas_call x1, Pallas kernels, on_device(): call(parent_kernel, total_shape, [pltpu.VMEM((64, LANES), F32)], flops=work)  8.75 us
    unnamed x18, local copies, waits for them, and re-layouts  7.06 us
  transfers between devices with their start and end apart: 4, of which 3 were waited for; matrix products, arithmetic and copies ran while one was open for 0% of the time, Pallas kernels for 24%

profile of v1, /device:TPU:1, one launch (start us, length us, event | category | flops | bytes accessed | tf_op | source)
XLA Modules:
  0.0 120.3 jit_solution(8447821737190856234)
XLA Ops:
  0.6 0.0 copy-start.4
  0.6 1.0 copy-done.4
  1.7 0.7 copy-done.6
  2.4 2.1 %shard_map.84 = (bf16[8,16,40,128]{3,2,1,0:T(8,128)(2,1)}, bf16[256,512]{1,0:T(8,128)(2,1)S(1)}) custom-call(s32[1,256]{1,0:T(1,128)S(1)} %bitcast.12, bf16[256,1024]{1,0:T(8,128)(2,1)S(1)} %copy-done.4), custom_call_target="tpu_custom_call" | custom-call | flops 268435456 | bytes 4194304 | tf_op jit(solution)/shard_map/pallas_call | solution.py:307
  4.5 11.5 %all-to-all-start = ((bf16[128,40,128]{2,1,0:T(8,128)(2,1)}), bf16[128,40,128]{2,1,0:T(8,128)(2,1)S(1)}, u32[]{:S(2)}, u32[]{:S(2)}) async-start(bf16[128,40,128]{2,1,0:T(8,128)(2,1)} %bitcast.1), calls=%async_computation | async-start | bytes 2621440 | tf_op jit(solution)/shard_map/all_to_all | solution.py:293
  16.0 0.0 copy-done.1
  16.0 0.1 shift_right_logical.14
  16.1 0.1 copy.9
  16.2 0.1 and.14
  16.3 0.1 copy.10
  16.4 0.0 copy-done.2
  16.4 0.0 copy-start.5
  16.4 8.8 %shard_map.86.start_ref = f32[512,1152]{1,0:T(8,128)S(1)} custom-call(s32[32,128]{1,0:T(8,128)S(1)} %bitcast.10, bf16[4096,128]{1,0:T(8,128)(2,1)S(1)} %copy-done.2), custom_call_target="tpu_custom_call" | custom-call | flops 4831838208 | bytes 4194304 | tf_op jit(solution)/shard_map/pallas_call | solution.py:314
  25.2 0.0 copy-start.7
  25.2 1.4 %copy-done.7 = f32[512,1152]{1,0:T(8,128)} copy-done((f32[512,1152]{1,0:T(8,128)}, f32[512,1152]{1,0:T(8,128)S(1)}, u32[]{:S(2)}) %copy-start.7) | copy-done | bytes 2359320
  26.6 10.8 %all-to-all-done.slab_ref = bf16[128,40,128]{2,1,0:T(8,128)(2,1)S(1)} async-done(((bf16[128,40,128]{2,1,0:T(8,128)(2,1)}), bf16[128,40,128]{2,1,0:T(8,128)(2,1)S(1)}, u32[]{:S(2)}, u32[]{:S(2)}) %all-to-all-start) | async-done | bytes 1310752 | tf_op jit(solution)/shard_map/all_to_all | solution.py:293
  37.4 0.0 copy-done.5
  37.4 1.7 %copy-done.8 = f32[512,1152]{1,0:T(8,128)S(1)} copy-done((f32[512,1152]{1,0:T(8,128)S(1)}, f32[512,1152]{1,0:T(8,128)}, u32[]{:S(2)}) %copy-start.8) | copy-done | bytes 2359320
  39.0 10.9 %shard_map.87 = bf16[16,280,128]{2,1,0:T(8,128)(2,1)S(1)} custom-call(bf16[128,40,128]{2,1,0:T(8,128)(2,1)S(1)} %all-to-all-done.slab_ref, bf16[128,128]{1,0:T(8,128)(2,1)S(1)} %pad.5.table_ref, s32[32,128]{1,0:T(8,128)S(1)} %bitcast.11, f32[512,1152]{1,0:T(8,128)S(1)} %copy-done.8), custom_call_target="tpu_custom_call" | custom-call | flops 4831838208 | bytes 4194304 | tf_op jit(solution)/shard_map/pallas_call | solution.py:321
  49.9 1.0 copy-done
  51.0 3.7 %all-to-all-start.1 = ((bf16[16,280,128]{2,1,0:T(8,128)(2,1)}), bf16[16,280,128]{2,1,0:T(8,128)(2,1)S(1)}, u32[]{:S(2)}, u32[]{:S(2)}) async-start(bf16[16,280,128]{2,1,0:T(8,128)(2,1)} %copy-done), calls=%async_computation.1 | async-start | bytes 2293760 | tf_op jit(solution)/shard_map/all_to_all | solution.py:293
  54.7 0.0 copy-start.3
  54.7 1.2 %copy-done.3 = bf16[4096,128]{1,0:T(8,128)(2,1)S(1)} copy-done((bf16[4096,128]{1,0:T(8,128)(2,1)S(1)}, bf16[4096,128]{1,0:T(8,128)(2,1)}, u32[]{:S(2)}) %copy-start.3) | copy-done | bytes 1048600
  55.9 17.5 %shard_map.85 = (f32[4096,128]{1,0:T(8,128)}, bf16[128,32,128]{2,1,0:T(8,128)(2,1)}) custom-call(bf16[128,40,128]{2,1,0:T(8,128)(2,1)S(1)} %all-to-all-done.slab_ref, bf16[4096,128]{1,0:T(8,128)(2,1)S(1)} %copy-done.3), custom_call_target="tpu_custom_call" | custom-call | flops 9663676416 | bytes 4194304 | tf_op jit(solution)/shard_map/pallas_call | solution.py:333
  73.4 0.0 all-to-all-done.1.parts_ref
  73.4 8.7 %all-to-all-start.3 = ((bf16[128,32,128]{2,1,0:T(8,128)(2,1)}), bf16[128,32,128]{2,1,0:T(8,128)(2,1)S(1)}, u32[]{:S(2)}, u32[]{:S(2)}) async-start(bf16[128,32,128]{2,1,0:T(8,128)(2,1)} %get-tuple-element.15), calls=%async_computation.3 | async-start | bytes 2097152 | tf_op jit(solution)/shard_map/all_to_all | solution.py:293
  82.1 1.2 shard_map.88
  83.3 17.4 %all-to-all-done.3 = bf16[128,32,128]{2,1,0:T(8,128)(2,1)S(1)} async-done(((bf16[128,32,128]{2,1,0:T(8,128)(2,1)}), bf16[128,32,128]{2,1,0:T(8,128)(2,1)S(1)}, u32[]{:S(2)}, u32[]{:S(2)}) %all-to-all-start.3) | async-done | bytes 1048608 | tf_op jit(solution)/shard_map/all_to_all | solution.py:293
  100.7 4.9 %all-to-all-start.2 = ((bf16[128,16,128]{2,1,0:T(8,128)(2,1)}), bf16[128,16,128]{2,1,0:T(8,128)(2,1)S(1)}, u32[]{:S(2)}, u32[]{:S(2)}) async-start(bf16[128,16,128]{2,1,0:T(8,128)(2,1)} %get-tuple-element.13), calls=%async_computation.2 | async-start | bytes 1048576 | tf_op jit(solution)/shard_map/all_to_all | solution.py:293
  105.6 1.2 %shard_map.90 = bf16[256,1024]{1,0:T(8,128)(2,1)} custom-call(bf16[256,512]{1,0:T(8,128)(2,1)S(1)} %get-tuple-element.14.back_ref, bf16[8,16,32,128]{3,2,1,0:T(8,128)(2,1)S(1)} %bitcast.8), custom_call_target="tpu_custom_call" | custom-call | flops 268435456 | bytes 4194304 | tf_op jit(solution)/shard_map/pallas_call | solution.py:351
  106.9 12.3 %all-to-all-done.2 = bf16[128,16,128]{2,1,0:T(8,128)(2,1)S(1)} async-done(((bf16[128,16,128]{2,1,0:T(8,128)(2,1)}), bf16[128,16,128]{2,1,0:T(8,128)(2,1)S(1)}, u32[]{:S(2)}, u32[]{:S(2)}) %all-to-all-start.2) | async-done | bytes 524320 | tf_op jit(solution)/shard_map/all_to_all | solution.py:293
  119.2 1.1 shard_map.89
  (8 shorter events, 0.1 us)
Async XLA Ops:
  0.6 1.0 copy-start.4
  1.7 0.7 copy-start.6
  4.5 11.5 %copy-start.1 = (s32[4096]{0:T(1024)S(1)}, s32[4096]{0:T(1024)}, u32[]{:S(2)}) copy-start(s32[4096]{0:T(1024)} %param.7) | copy-start | bytes 49156
  4.5 11.9 %copy-start.2 = (bf16[4096,128]{1,0:T(8,128)(2,1)S(1)}, bf16[4096,128]{1,0:T(8,128)(2,1)}, u32[]{:S(2)}) copy-start(bf16[4096,128]{1,0:T(8,128)(2,1)} %old_ref.3) | copy-start | bytes 3145732
  4.5 32.9 %all-to-all-start = ((bf16[128,40,128]{2,1,0:T(8,128)(2,1)}), bf16[128,40,128]{2,1,0:T(8,128)(2,1)S(1)}, u32[]{:S(2)}, u32[]{:S(2)}) async-start(bf16[128,40,128]{2,1,0:T(8,128)(2,1)} %bitcast.1), calls=%async_computation | async-start | bytes 2621440 | tf_op jit(solution)/shard_map/all_to_all | solution.py:293
  16.4 21.0 %copy-start.5 = (s32[4096]{0:T(1024)S(1)}, s32[4096]{0:T(1024)}, u32[]{:S(2)}) copy-start(s32[4096]{0:T(1024)} %param.8) | copy-start | bytes 49156
  25.2 1.4 %copy-start.7 = (f32[512,1152]{1,0:T(8,128)}, f32[512,1152]{1,0:T(8,128)S(1)}, u32[]{:S(2)}) copy-start(f32[512,1152]{1,0:T(8,128)S(1)} %shard_map.86.start_ref) | copy-start | bytes 7077892
  37.4 1.7 %copy-start.8 = (f32[512,1152]{1,0:T(8,128)S(1)}, f32[512,1152]{1,0:T(8,128)}, u32[]{:S(2)}) copy-start(f32[512,1152]{1,0:T(8,128)} %copy-done.7) | copy-start | bytes 7077892
  49.9 1.0 copy-start
  51.0 22.5 %all-to-all-start.1 = ((bf16[16,280,128]{2,1,0:T(8,128)(2,1)}), bf16[16,280,128]{2,1,0:T(8,128)(2,1)S(1)}, u32[]{:S(2)}, u32[]{:S(2)}) async-start(bf16[16,280,128]{2,1,0:T(8,128)(2,1)} %copy-done), calls=%async_computation.1 | async-start | bytes 2293760 | tf_op jit(solution)/shard_map/all_to_all | solution.py:293
  54.7 1.2 %copy-start.3 = (bf16[4096,128]{1,0:T(8,128)(2,1)S(1)}, bf16[4096,128]{1,0:T(8,128)(2,1)}, u32[]{:S(2)}) copy-start(bf16[4096,128]{1,0:T(8,128)(2,1)} %old_ref.3) | copy-start | bytes 3145732
  73.4 27.3 %all-to-all-start.3 = ((bf16[128,32,128]{2,1,0:T(8,128)(2,1)}), bf16[128,32,128]{2,1,0:T(8,128)(2,1)S(1)}, u32[]{:S(2)}, u32[]{:S(2)}) async-start(bf16[128,32,128]{2,1,0:T(8,128)(2,1)} %get-tuple-element.15), calls=%async_computation.3 | async-start | bytes 2097152 | tf_op jit(solution)/shard_map/all_to_all | solution.py:293
  100.7 18.4 %all-to-all-start.2 = ((bf16[128,16,128]{2,1,0:T(8,128)(2,1)}), bf16[128,16,128]{2,1,0:T(8,128)(2,1)S(1)}, u32[]{:S(2)}, u32[]{:S(2)}) async-start(bf16[128,16,128]{2,1,0:T(8,128)(2,1)} %get-tuple-element.13), calls=%async_computation.2 | async-start | bytes 1048576 | tf_op jit(solution)/shard_map/all_to_all | solution.py:293

commit v2 on v1

v2 whole, which is shorter than its diff:
```python
import jax
import jax.numpy as jnp
from jax import lax
from jax.experimental import pallas as pl
from jax.experimental.pallas import tpu as pltpu
from jax.sharding import PartitionSpec as P

F32 = jnp.float32
BF16 = jnp.bfloat16
I32 = jnp.int32
LANES = 128
LOW = 512
HIGHS = 8
CAP = 32
HALF = 16
EXTRA = 8
TOP = 16
BOTH = ("dp", "cent")


def iota(shape, axis):
    return lax.broadcasted_iota(I32, shape, axis)


def dot(left, right):
    return jnp.dot(left, right, preferred_element_type=F32)


def dot_nt(left, right):
    return lax.dot_general(left, right, (((1,), (1,)), ((), ())), preferred_element_type=F32)


def lane_slice(at, width=LANES):
    return slice(at * width, (at + 1) * width)


HBM = pl.BlockSpec(memory_space=pltpu.HBM)
VMEM = pl.BlockSpec(memory_space=pltpu.VMEM)


def call(body, out_shape, ins, outs, scratch=(), flops=0, size=4 << 20, vmem=32 << 20, alias=None):
    return pl.pallas_call(
        body,
        out_shape=out_shape,
        in_specs=ins,
        out_specs=outs,
        scratch_shapes=list(scratch),
        input_output_aliases=alias or {},
        compiler_params=pltpu.CompilerParams(vmem_limit_bytes=vmem),
        cost_estimate=pl.CostEstimate(flops=flops, bytes_accessed=size, transcendentals=0),
    )


def pack_kernel(assign_hbm, points_hbm, send_hbm, back_ref, assign_ref, points_ref, send_ref, sems):
    owners = send_ref.shape[1]
    parts = send_ref.shape[0]
    count = points_ref.shape[0]
    load = pltpu.make_async_copy(assign_hbm, assign_ref, sems.at[0])
    load.start()
    loads = []
    for pair in range(parts // 2):
        at = lane_slice(pair, 2 * LANES)
        loads.append(
            pltpu.make_async_copy(points_hbm.at[:, at], points_ref.at[:, at], sems.at[1 + pair])
        )
        loads[-1].start()
    before = jnp.where(iota((count, count), 0) <= iota((count, count), 1), 1.0, 0.0).astype(BF16)
    same = jnp.where(iota((count, count), 0) == iota((count, count), 1), 1.0, 0.0).astype(BF16)
    load.wait()
    label = assign_ref[...]
    owner = lax.shift_right_logical(label, 12)
    local = label & 4095
    mine = iota((owners, count), 0) == owner
    mine_f = jnp.where(mine, 1.0, 0.0)
    running = dot(mine_f.astype(BF16), before)
    place = jnp.sum(running * mine_f, axis=0, keepdims=True).astype(I32) - 1
    slot = owner * CAP + place
    table = jnp.where(iota((owners * CAP, count), 0) == slot, 1.0, 0.0).astype(BF16)
    shift = (lax.axis_index("cent") % 8) * HALF
    line = iota((LANES, count), 0)
    row = iota((owners, EXTRA, LANES), 1)
    digits = [(lax.shift_right_logical(local, 6) + 1).astype(F32), ((local & 63) + 1).astype(F32)]
    digits = [(mine_f * digit).astype(BF16) for digit in digits]
    extra = jnp.zeros((owners, EXTRA, LANES), F32)
    for half in range(2):
        first = half * HALF
        inside = (place >= first) & (place < first + HALF)
        lane = jnp.where(inside, place - first + shift, -1)
        lane_table = jnp.where(line == lane, 1.0, 0.0).astype(BF16)
        for kind in range(2):
            found = dot_nt(digits[kind], lane_table)
            extra = jnp.where(row == 2 * kind + half, found[:, None, :], extra)
    extra = extra.astype(BF16)
    stores = []
    for part in range(parts):
        if part % 2 == 0:
            loads[part // 2].wait()
            both = dot(table, points_ref[:, lane_slice(part // 2, 2 * LANES)]).astype(BF16)
        rows = both[:, lane_slice(part % 2)]
        send_ref[part, :, 0:CAP, :] = rows.reshape(owners, CAP, LANES)
        send_ref[part, :, CAP : CAP + EXTRA, :] = extra
        stores.append(
            pltpu.make_async_copy(send_ref.at[part], send_hbm.at[part], sems.at[1 + parts // 2 + part])
        )
        stores[-1].start()
    back_ref[...] = dot_nt(same, table).astype(BF16)
    for store in stores:
        store.wait()


def slot_digits(slab_ref, digits_ref):
    rows = slab_ref[:, CAP : CAP + EXTRA, :].astype(F32).reshape(-1, LANES).astype(BF16)
    shape = (64, rows.shape[0])
    column, line = iota(shape, 1), iota(shape, 0)
    pick = (lax.shift_right_logical(column, 6) == (line & 15)) & (
        (column & 7) == lax.shift_right_logical(line, 4)
    )
    digits_ref[...] = dot(jnp.where(pick, 1.0, 0.0).astype(BF16), rows)


def across_lanes(digits_ref, at, count):
    found = []
    for part in range(count):
        high, low = digits_ref[pl.ds(at + part, 1), :], digits_ref[pl.ds(at + part + 32, 1), :]
        found.append((high * 64.0 + low).astype(I32) - 65)
    return found


def down_rows(digits_ref, at, count):
    same = iota((LANES, LANES), 0) == iota((LANES, LANES), 1)
    parts = []
    for part in range(count):
        high, low = digits_ref[pl.ds(at + part, 1), :], digits_ref[pl.ds(at + part + 32, 1), :]
        parts.append(
            jnp.concatenate([jnp.where(same, high, 0.0), jnp.where(same, low, 0.0)], axis=1)
        )
    left = jnp.concatenate(parts, axis=0).astype(BF16)
    right = jnp.where(iota((2 * LANES, LANES), 0) < LANES, 64.0, 1.0).astype(BF16)
    return dot(left, right).astype(I32) - 65


def low_table(labels):
    line = iota((LOW, LANES), 0)
    return jnp.concatenate(
        [jnp.where(line == (label & (LOW - 1)), 1.0, 0.0).astype(BF16) for label in labels], axis=1
    )


def masked(rows, high, which):
    return jnp.where(high == which, rows, 0.0).astype(BF16)


def counting(high):
    lane = iota(high.shape, 1)
    return jnp.where((high == (lane & 7)) & (lane < 16), 1.0, 0.0).astype(BF16)


def segments(total_ref, left_ref, high_ref, rows_of, digits_ref, steps):
    for step in range(steps):
        left_ref[:, lane_slice(step, 512)] = low_table(across_lanes(digits_ref, 4 * step, 4))
        high_ref[lane_slice(step, 512), :] = lax.shift_right_arithmetic(
            down_rows(digits_ref, 4 * step, 4), 9
        )
    left = left_ref[:, 0 : steps * 512]
    for pair in range(HIGHS // 2):
        right = []
        for step in range(steps):
            high, rows = high_ref[lane_slice(step, 512), :], rows_of(step)
            right.append(
                jnp.concatenate([masked(rows, high, 2 * pair + side) for side in range(2)], axis=1)
            )
        total_ref[:, lane_slice(pair, 2 * LANES)] = dot(left, jnp.concatenate(right, axis=0))
    total_ref[:, HIGHS * LANES :] = dot(left, counting(high_ref[0 : steps * 512, :]))


def add_segments(total_ref, digits_ref, at, rows):
    left = low_table(across_lanes(digits_ref, at, 2))
    high = lax.shift_right_arithmetic(down_rows(digits_ref, at, 2), 9)
    for pair in range(HIGHS // 2):
        right = jnp.concatenate([masked(rows, high, 2 * pair + side) for side in range(2)], axis=1)
        total_ref[:, lane_slice(pair, 2 * LANES)] += dot(left, right)
    total_ref[:, HIGHS * LANES :] += dot(left, counting(high))


def lower_rows(slab_ref, step):
    return slab_ref[lane_slice(step, 32), 0:HALF, :].reshape(512, LANES).astype(F32)


def upper_rows(slab_ref, group):
    return slab_ref[pl.ds(group * 16, 16), HALF:CAP, :].reshape(256, LANES).astype(F32)


def any_label(digits_ref, group):
    return jnp.max(digits_ref[pl.ds(16 + 2 * group, 2), :]) > 0.0


def parent_kernel(parent_ref, old_ref, total_ref, digits_ref):
    parent = parent_ref[...]
    digits_ref[0:32, :] = (lax.shift_right_logical(parent, 6) + 1).astype(F32)
    digits_ref[32:64, :] = ((parent & 63) + 1).astype(F32)
    total_ref[...] = jnp.zeros_like(total_ref)

    def step(at, carry):
        rows = old_ref[pl.ds(pl.multiple_of(at * 256, 256), 256), :].astype(F32)
        add_segments(total_ref, digits_ref, 2 * at, rows)
        return carry

    lax.fori_loop(0, old_ref.shape[0] // 256, step, 0)


def find_parents(digits_ref, parents_ref, table_ref, at, count):
    line = iota((LANES, LANES), 0)
    rows = [(digits_ref[pl.ds(at + n, 1), :], digits_ref[pl.ds(at + n + 32, 1), :]) for n in range(count)]
    left = [jnp.where(line == high.astype(I32) - 1, 1.0, 0.0).astype(BF16) for high, _ in rows]
    found = dot(table_ref[...], jnp.concatenate(left, axis=1))
    for n in range(count):
        chosen = jnp.where((line & 63) == rows[n][1].astype(I32) - 1, found[:, lane_slice(n)], 0.0)
        parents_ref[pl.ds(at + n, 1), :] = jnp.sum(chosen[0:64], axis=0, keepdims=True)
        parents_ref[pl.ds(at + n + 32, 1), :] = jnp.sum(chosen[64:128], axis=0, keepdims=True)


def upper_kernel(
    slab_ref, table_ref, top_ref, start_hbm, send_hbm,
    digits_ref, parents_ref, total_ref, left_ref, high_ref, start_ref, send_ref, right_ref, sems,
):
    load = pltpu.make_async_copy(start_hbm, start_ref, sems.at[0])
    load.start()
    slot_digits(slab_ref, digits_ref)
    for step in range(4):
        find_parents(digits_ref, parents_ref, table_ref, 4 * step, 4)
    segments(total_ref, left_ref, high_ref, lambda step: lower_rows(slab_ref, step), parents_ref, 4)

    def more(group, carry):
        @pl.when(any_label(digits_ref, group))
        def _():
            find_parents(digits_ref, parents_ref, table_ref, 16 + 2 * group, 2)
            add_segments(total_ref, parents_ref, 16 + 2 * group, upper_rows(slab_ref, group))

        return carry

    lax.fori_loop(0, slab_ref.shape[0] // 16, more, 0)
    load.wait()
    at = slice(HIGHS * LANES, (HIGHS + 1) * LANES)
    weights = total_ref[:, at] + start_ref[:, at]
    coarse = weights.astype(BF16).astype(F32)
    fine = weights - coarse
    lane = iota((LOW, LANES), 1)
    tops = []
    for high in range(HIGHS):
        mass = (total_ref[:, lane_slice(high)] + start_ref[:, lane_slice(high)]).astype(BF16)
        for half in range(2):
            send_ref[2 * high + half, 0:256, :] = mass[half * 256 : (half + 1) * 256]
        right_ref[lane_slice(high, LOW), 0:LANES] = mass
        right_ref[lane_slice(high, LOW), LANES:] = jnp.where(
            lane == high, coarse, jnp.where(lane == high + 8, fine, 0.0)
        ).astype(BF16)
        for part in range(4):
            hit = iota((256, LANES), 0) == top_ref[high * 4 + part : high * 4 + part + 1, :]
            tops.append(jnp.where(hit, 1.0, 0.0).astype(BF16))
    tops = dot(jnp.concatenate(tops, axis=1), right_ref[...])
    top_mass = tops[:, :LANES].astype(BF16)
    top_weight = jnp.sum(tops[:, LANES:].T[0:16], axis=0, keepdims=True)
    top_coarse = top_weight.astype(BF16).astype(F32)
    top_fine = top_weight - top_coarse
    coarse_t, fine_t = coarse.T, fine.T
    stores = []
    for owner in range(send_ref.shape[0]):
        send_ref[owner, 256:272, :] = top_mass[owner * TOP : (owner + 1) * TOP]
        high, from_lane = owner // 2, (owner % 2) * 256
        rows = []
        for source, line_at, lane_at in (
            (coarse_t, high, from_lane),
            (fine_t, high, from_lane),
            (top_coarse, 0, 0),
            (top_fine, 0, 0),
        ):
            for half in range(2):
                first = lane_at + half * LANES
                rows.append(source[line_at : line_at + 1, first : first + LANES])
        send_ref[owner, 272:280, :] = jnp.concatenate(rows, axis=0).astype(BF16)
        if owner % 4 == 3:
            part = pl.ds(owner - 3, 4)
            stores.append(
                pltpu.make_async_copy(send_ref.at[part], send_hbm.at[part], sems.at[1 + owner // 4])
            )
            stores[-1].start()
    for store in stores:
        store.wait()


def level_kernel(
    slab_ref, old_hbm, level_hbm, residual_hbm,
    digits_ref, total_ref, table_ref, left_ref, high_ref, old_ref, level_ref, residual_ref,
    load_sem, level_sems, low_sems, up_sems,
):
    load = pltpu.make_async_copy(old_hbm, old_ref, load_sem)
    load.start()
    slot_digits(slab_ref, digits_ref)
    segments(total_ref, left_ref, high_ref, lambda step: lower_rows(slab_ref, step), digits_ref, 4)
    groups = slab_ref.shape[0] // 16

    def more(group, carry):
        @pl.when(any_label(digits_ref, group))
        def _():
            add_segments(total_ref, digits_ref, 16 + 2 * group, upper_rows(slab_ref, group))

        return carry

    lax.fori_loop(0, groups, more, 0)
    load.wait()
    inverse = 1.0 / (total_ref[:, HIGHS * LANES :] + 1.0)
    stores = []
    for high in range(HIGHS):
        lines = lane_slice(high, LOW)
        mass = total_ref[:, lane_slice(high)] + old_ref[lines, :].astype(F32)
        level = mass * jnp.broadcast_to(inverse[:, high : high + 1], mass.shape)
        level_ref[lines, :] = level
        table_ref[:, lane_slice(high)] = level.astype(BF16)
        stores.append(
            pltpu.make_async_copy(level_ref.at[lines], level_hbm.at[lines], level_sems.at[high])
        )
        stores[-1].start()

    def subtract(at, count, rows):
        label = down_rows(digits_ref, at, count)
        low = label & (LOW - 1)
        high = lax.shift_right_arithmetic(label, 9)
        lane = iota(label.shape, 1)
        left = jnp.concatenate(
            [
                jnp.where(low == lane + part * LANES, 1.0, 0.0).astype(BF16)
                for part in range(LOW // LANES)
            ],
            axis=1,
        )
        for pair in range(HIGHS // 2):
            found = dot(left, table_ref[:, lane_slice(pair, 2 * LANES)])
            for side in range(2):
                rows -= jnp.where(high == 2 * pair + side, found[:, lane_slice(side)], 0.0)
        return rows.astype(BF16)

    for step in range(4):
        sources = lane_slice(step, 32)
        residual_ref[sources, 0:HALF, :] = subtract(
            4 * step, 4, lower_rows(slab_ref, step)
        ).reshape(32, HALF, LANES)
        part = (sources, slice(0, HALF))
        stores.append(
            pltpu.make_async_copy(residual_ref.at[part], residual_hbm.at[part], low_sems.at[step])
        )
        stores[-1].start()

    def upper_copy(group):
        part = (pl.ds(group * 16, 16), pl.ds(HALF, HALF))
        return pltpu.make_async_copy(residual_ref.at[part], residual_hbm.at[part], up_sems.at[group])

    def finish(group, carry):
        sources = pl.ds(group * 16, 16)
        live = any_label(digits_ref, group)

        @pl.when(live)
        def _():
            residual_ref[sources, HALF:CAP, :] = subtract(
                16 + 2 * group, 2, upper_rows(slab_ref, group)
            ).reshape(16, HALF, LANES)

        @pl.when(jnp.logical_not(live))
        def _():
            residual_ref[sources, HALF:CAP, :] = slab_ref[sources, HALF:CAP, :]

        upper_copy(group).start()
        return carry

    lax.fori_loop(0, groups, finish, 0)
    for store in stores:
        store.wait()

    def settle(group, carry):
        upper_copy(group).wait()
        return carry

    lax.fori_loop(0, groups, settle, 0)


def finish_kernel(parts_ref, send_in, level_ref, send_hbm, column_ref, top_ref, sem):
    total = parts_ref[0].astype(F32)
    for source in range(1, parts_ref.shape[0]):
        total += parts_ref[source].astype(F32)
    tail = total[272:280].T
    me = lax.axis_index("cent")
    chosen = jnp.where(me < 8, tail[:, 4:5] + tail[:, 6:7], tail[:, 5:6] + tail[:, 7:8])
    column_ref[...] = jnp.broadcast_to(chosen, (LANES, LANES))
    weight = column_ref[pl.ds(pl.multiple_of((me % 8) * TOP, TOP), TOP), :]
    top = (total[256:272] / weight).astype(BF16)
    top_ref[...] = jnp.broadcast_to(top[None], top_ref.shape)
    store = pltpu.make_async_copy(top_ref, send_hbm.at[:, pl.ds(CAP, TOP), :], sem)
    store.start()
    for half in range(2):
        weight = tail[:, half : half + 1] + tail[:, half + 2 : half + 3]
        lines = slice(half * LANES, (half + 1) * LANES)
        level_ref[lines, :] = total[lines] / jnp.broadcast_to(weight, (LANES, LANES))
    store.wait()


def unpack_kernel(back_ref, returned_ref, residual_ref, level_ref):
    groups, owners, rows, lanes = returned_ref.shape
    for pair in range(groups // 2):
        right = jnp.concatenate(
            [
                returned_ref[2 * pair + side, :, 0:CAP, :].reshape(owners * CAP, lanes)
                for side in range(2)
            ],
            axis=1,
        )
        residual_ref[:, lane_slice(pair, 2 * lanes)] = dot(back_ref[...], right).astype(BF16)
    for group in range(groups):
        top = returned_ref[group, :, CAP:rows, :].astype(F32)
        level_ref[:, lane_slice(group)] = top.reshape(owners * TOP, lanes)


def shape(dims, kind):
    return jax.ShapeDtypeStruct(dims, kind)


def swap(value, axes):
    return lax.all_to_all(value, axes, split_axis=0, concat_axis=0, tiled=True)


def on_device(points, assign, parent_one, parent_two, old_level_one):
    count, width = points.shape
    owners = lax.axis_size("cent")
    groups = lax.axis_size("dp")
    devices = owners * groups
    block, lanes = old_level_one.shape
    slots = owners * CAP
    rows = CAP + EXTRA
    total_dims = (LOW, (HIGHS + 1) * LANES)
    work = 2 * LOW * block * (HIGHS + 1) * LANES

    send, back = call(
        pack_kernel,
        (shape((groups, owners, rows, lanes), BF16), shape((count, slots), BF16)),
        [HBM, HBM],
        (HBM, VMEM),
        [
            pltpu.VMEM((1, count), I32),
            pltpu.VMEM((count, width), BF16),
            pltpu.VMEM((groups, owners, rows, lanes), BF16),
            pltpu.SemaphoreType.DMA((1 + groups // 2 + groups,)),
        ],
        flops=2 * slots * count * width,
    )(assign.reshape(1, count), points)
    slab = swap(send.reshape(devices, rows, lanes), BOTH)

    start = call(
        parent_kernel,
        shape(total_dims, F32),
        [VMEM, VMEM],
        VMEM,
        [pltpu.VMEM((64, LANES), F32)],
        flops=work,
    )(parent_one.reshape(block // LANES, LANES), old_level_one)
    grid = parent_one.reshape(64, 64).T
    table = jnp.concatenate([lax.shift_right_logical(grid, 6), grid & 63], axis=0) + 1
    table = jnp.pad(table, ((0, 0), (0, 64))).astype(BF16)

    share = call(
        upper_kernel,
        shape((owners, 280, lanes), BF16),
        [VMEM, VMEM, VMEM, HBM],
        HBM,
        [
            pltpu.VMEM((64, LANES), F32),
            pltpu.VMEM((64, LANES), F32),
            pltpu.VMEM(total_dims, F32),
            pltpu.VMEM((LOW, 2048), BF16),
            pltpu.VMEM((2048, LANES), I32),
            pltpu.VMEM(total_dims, F32),
            pltpu.VMEM((owners, 280, lanes), BF16),
            pltpu.VMEM((HIGHS * LOW, 2 * LANES), BF16),
            pltpu.SemaphoreType.DMA((5,)),
        ],
        flops=work,
    )(slab, table, parent_two.reshape(-1, LANES), start)
    shares = swap(share, "cent")

    level_one, answer = call(
        level_kernel,
        (shape((block, lanes), F32), shape((devices, CAP + TOP, lanes), BF16)),
        [VMEM, HBM],
        (HBM, HBM),
        [
            pltpu.VMEM((64, LANES), F32),
            pltpu.VMEM(total_dims, F32),
            pltpu.VMEM((LOW, HIGHS * LANES), BF16),
            pltpu.VMEM((LOW, 2048), BF16),
            pltpu.VMEM((2048, LANES), I32),
            pltpu.VMEM((block, lanes), BF16),
            pltpu.VMEM((block, lanes), F32),
            pltpu.VMEM((devices, CAP, lanes), BF16),
            pltpu.SemaphoreType.DMA(()),
            pltpu.SemaphoreType.DMA((HIGHS,)),
            pltpu.SemaphoreType.DMA((4,)),
            pltpu.SemaphoreType.DMA((groups,)),
        ],
        flops=2 * work,
    )(slab, old_level_one)

    level_two, answer = call(
        finish_kernel,
        (shape((256, lanes), F32), shape((devices, CAP + TOP, lanes), BF16)),
        [VMEM, HBM],
        (VMEM, HBM),
        [
            pltpu.VMEM((LANES, LANES), F32),
            pltpu.VMEM((devices, TOP, lanes), BF16),
            pltpu.SemaphoreType.DMA(()),
        ],
        alias={1: 1},
    )(shares, answer)
    returned = swap(answer, BOTH)
    residual, level_three = call(
        unpack_kernel,
        (shape((count, width), BF16), shape((owners * TOP, width), F32)),
        [VMEM, VMEM],
        (VMEM, VMEM),
        flops=2 * slots * count * width,
    )(back, returned.reshape(groups, owners, CAP + TOP, lanes))
    return (level_one, level_two, level_three, residual)


def solution(mesh):
    in_specs = (P(("dp", "cent"), None), P(("dp", "cent")), P("cent"), P(), P("cent", "dp"))
    out_specs = (P("cent", "dp"), P("cent", "dp"), P(), P(("dp", "cent"), None))
    return jax.shard_map(
        on_device, mesh=mesh, in_specs=in_specs, out_specs=out_specs, check_vma=False
    )
```

time: 121 us -> 103 us (0.85)
  blocking collectives: 0 us -> 31.2 us
  waiting for transfers between devices: 40.5 us -> 9.94 us
  starting transfers between devices: 28.8 us -> 15.4 us
  Pallas kernels: 42.8 us -> 35.9 us
  local copies, waits for them, and re-layouts: 7.37 us -> 9.16 us
    all_to_all x0 -> x1, blocking collectives: none -> 31.2 us  [swap(): return lax.all_to_all(value, axes, split_axis=0, concat_axis=0, tiled=True)]
    all_to_all x4 -> x2, waiting for transfers between devices: 40.5 us -> 9.94 us  [swap(): return lax.all_to_all(value, axes, split_axis=0, concat_axis=0, tiled=True)]
    all_to_all x4 -> x2, starting transfers between devices: 28.8 us -> 15.4 us  [swap(): return lax.all_to_all(value, axes, split_axis=0, concat_axis=0, tiled=True)]
    pallas_call x6 -> x5, Pallas kernels: 40.7 us -> 33.3 us  [the longest x1 11.9 us: on_device(): call(parent_kernel, shape(total_dims, F32), [VMEM, VMEM], VMEM, [pltpu.VM...]
    unnamed x18 -> x22, local copies, waits for them, and re-layouts: 7.06 us -> 8.85 us
  transfers between devices with their start and end apart: 4 -> 2, of which waited for: 3 -> 2; matrix products, arithmetic and copies ran while one was open for 0% -> 0% of each run, Pallas kernels for 24% -> 23%
where the time goes in v2:
time: 103 us; the launch traced here: 102 us
  Pallas kernels  35.9 us (35%)
  blocking collectives  31.2 us (30%)
  starting transfers between devices  15.4 us (15%)
  waiting for transfers between devices  9.94 us (10%)
  local copies, waits for them, and re-layouts  9.16 us (9%)
    all_to_all x1, blocking collectives, swap(): return lax.all_to_all(value, axes, split_axis=0, concat_axis=0, tiled=True)  31.2 us
    all_to_all x2, starting transfers between devices, swap(): return lax.all_to_all(value, axes, split_axis=0, concat_axis=0, tiled=True)  15.4 us
    pallas_call x1, Pallas kernels, on_device(): call(parent_kernel, shape(total_dims, F32), [VMEM, VMEM], VMEM, [pltpu.VM...  11.9 us
    pallas_call x1, Pallas kernels, on_device(): call(level_kernel, (shape((block, lanes), F32), shape((devices, CAP + TOP...  11.2 us
    all_to_all x2, waiting for transfers between devices, swap(): return lax.all_to_all(value, axes, split_axis=0, concat_axis=0, tiled=True)  9.94 us
    unnamed x22, local copies, waits for them, and re-layouts  8.85 us
    pallas_call x1, Pallas kernels, on_device(): call(upper_kernel, shape((owners, 280, lanes), BF16), [VMEM, VMEM, VMEM,...  7.33 us
    pallas_call x1, Pallas kernels, on_device(): call(pack_kernel, (shape((groups, owners, rows, lanes), BF16), shape((cou...  2.55 us
  transfers between devices with their start and end apart: 2, of which 2 were waited for; matrix products, arithmetic and copies ran while one was open for 0% of the time, Pallas kernels for 23%

profile of v2, /device:TPU:1, one launch (start us, length us, event | category | flops | bytes accessed | tf_op | source)
XLA Modules:
  0.0 102.4 jit_solution(11798157978319241257)
XLA Ops:
  0.6 0.0 copy-start.6
  0.6 1.0 %copy-done.6 = bf16[256,1024]{1,0:T(8,128)(2,1)S(1)} copy-done((bf16[256,1024]{1,0:T(8,128)(2,1)S(1)}, bf16[256,1024]{1,0:T(8,128)(2,1)}, u32[]{:S(2)}) %copy-start.6) | copy-done | bytes 524312
  1.7 0.7 copy-done.8
  2.4 2.6 %shard_map.84 = (bf16[8,16,40,128]{3,2,1,0:T(8,128)(2,1)}, bf16[256,512]{1,0:T(8,128)(2,1)S(1)}) custom-call(s32[1,256]{1,0:T(1,128)S(1)} %bitcast.10, bf16[256,1024]{1,0:T(8,128)(2,1)S(1)} %copy-done.6), custom_call_target="tpu_custom_call" | custom-call | flops 268435456 | bytes 4194304 | tf_op jit(solution)/shard_map/pallas_call | solution.py:440
  4.9 0.0 copy-start.4
  4.9 11.5 %all-to-all-start = ((bf16[128,40,128]{2,1,0:T(8,128)(2,1)}), bf16[128,40,128]{2,1,0:T(8,128)(2,1)S(1)}, u32[]{:S(2)}, u32[]{:S(2)}) async-start(bf16[128,40,128]{2,1,0:T(8,128)(2,1)} %bitcast.1), calls=%async_computation | async-start | bytes 2621440 | tf_op jit(solution)/shard_map/all_to_all | solution.py:426
  16.4 0.0 copy-done.3
  16.5 0.1 shift_right_logical.14
  16.5 0.1 copy.10
  16.6 0.1 and.14
  16.7 0.1 copy.11
  16.8 0.0 copy-done.4
  16.8 0.0 copy-start.7
  16.8 11.9 %shard_map.86.start_hbm = f32[512,1152]{1,0:T(8,128)S(1)} custom-call(s32[32,128]{1,0:T(8,128)S(1)} %bitcast.8, bf16[4096,128]{1,0:T(8,128)(2,1)S(1)} %copy-done.4), custom_call_target="tpu_custom_call" | custom-call | flops 4831838208 | bytes 4194304 | tf_op jit(solution)/shard_map/pallas_call | solution.py:455
  28.7 0.0 copy-start.9
  28.7 1.4 %copy-done.9 = f32[512,1152]{1,0:T(8,128)} copy-done((f32[512,1152]{1,0:T(8,128)}, f32[512,1152]{1,0:T(8,128)S(1)}, u32[]{:S(2)}) %copy-start.9) | copy-done | bytes 2359320
  30.2 7.6 %all-to-all-done.slab_ref = bf16[128,40,128]{2,1,0:T(8,128)(2,1)S(1)} async-done(((bf16[128,40,128]{2,1,0:T(8,128)(2,1)}), bf16[128,40,128]{2,1,0:T(8,128)(2,1)S(1)}, u32[]{:S(2)}, u32[]{:S(2)}) %all-to-all-start) | async-done | bytes 1310752 | tf_op jit(solution)/shard_map/all_to_all | solution.py:426
  37.8 0.0 copy-done.7
  37.8 2.1 %copy-done.10 = f32[512,1152]{1,0:T(8,128)S(1)} copy-done((f32[512,1152]{1,0:T(8,128)S(1)}, f32[512,1152]{1,0:T(8,128)}, u32[]{:S(2)}) %copy-start.10) | copy-done | bytes 2359320
  39.9 7.3 %shard_map.87 = bf16[16,280,128]{2,1,0:T(8,128)(2,1)S(1)} custom-call(bf16[128,40,128]{2,1,0:T(8,128)(2,1)S(1)} %all-to-all-done.slab_ref, bf16[128,128]{1,0:T(8,128)(2,1)S(1)} %pad.5.table_ref, s32[32,128]{1,0:T(8,128)S(1)} %bitcast.9, f32[512,1152]{1,0:T(8,128)S(1)} %copy-done.10), custom_call_target="tpu_custom_call" | custom-call | flops 4831838208 | bytes 4194304 | tf_op jit(solution)/shard_map/pallas_call | solution.py:467
  47.3 0.0 copy-done
  47.3 0.0 copy-start.2
  47.3 1.0 %copy-done.2 = bf16[16,280,128]{2,1,0:T(8,128)(2,1)} copy-done((bf16[16,280,128]{2,1,0:T(8,128)(2,1)}, bf16[16,280,128]{2,1,0:T(8,128)(2,1)S(1)}, u32[]{:S(2)}) %copy-start.2) | copy-done | bytes 1146904
  48.3 3.9 %all-to-all-start.1 = ((bf16[16,280,128]{2,1,0:T(8,128)(2,1)}), bf16[16,280,128]{2,1,0:T(8,128)(2,1)S(1)}, u32[]{:S(2)}, u32[]{:S(2)}) async-start(bf16[16,280,128]{2,1,0:T(8,128)(2,1)} %copy-done.2), calls=%async_computation.1 | async-start | bytes 2293760 | tf_op jit(solution)/shard_map/all_to_all | solution.py:426
  52.2 0.0 copy-start.1
  52.2 1.3 %copy-done.1 = bf16[128,40,128]{2,1,0:T(8,128)(2,1)S(1)} copy-done((bf16[128,40,128]{2,1,0:T(8,128)(2,1)S(1)}, bf16[128,40,128]{2,1,0:T(8,128)(2,1)}, u32[]{:S(2)}) %copy-start.1) | copy-done | bytes 1310744
  53.5 1.2 %copy-done.5 = bf16[4096,128]{1,0:T(8,128)(2,1)S(1)} copy-done((bf16[4096,128]{1,0:T(8,128)(2,1)S(1)}, bf16[4096,128]{1,0:T(8,128)(2,1)}, u32[]{:S(2)}) %copy-start.5) | copy-done | bytes 1048600
  54.7 11.2 %shard_map.85 = (f32[4096,128]{1,0:T(8,128)}, bf16[128,48,128]{2,1,0:T(8,128)(2,1)S(1)}) custom-call(bf16[128,40,128]{2,1,0:T(8,128)(2,1)S(1)} %copy-done.1, bf16[4096,128]{1,0:T(8,128)(2,1)S(1)} %copy-done.5), custom_call_target="tpu_custom_call" | custom-call | flops 9663676416 | bytes 4194304 | tf_op jit(solution)/shard_map/pallas_call | solution.py:487
  65.9 2.3 %all-to-all-done.1.parts_ref = bf16[16,280,128]{2,1,0:T(8,128)(2,1)S(1)} async-done(((bf16[16,280,128]{2,1,0:T(8,128)(2,1)}), bf16[16,280,128]{2,1,0:T(8,128)(2,1)S(1)}, u32[]{:S(2)}, u32[]{:S(2)}) %all-to-all-start.1) | async-done | bytes 1146912 | tf_op jit(solution)/shard_map/all_to_all | solution.py:426
  68.3 1.3 %shard_map.88 = (f32[256,128]{1,0:T(8,128)}, bf16[128,48,128]{2,1,0:T(8,128)(2,1)S(1)}) custom-call(bf16[16,280,128]{2,1,0:T(8,128)(2,1)S(1)} %all-to-all-done.1.parts_ref, bf16[128,48,128]{2,1,0:T(8,128)(2,1)S(1)} %get-tuple-element.14.send_in), custom_call_target="tpu_custom_call", output_to_operand_aliasing={{1}: (1, {})} | custom-call | bytes 4194304 | tf_op jit(solution)/shard_map/pallas_call | solution.py:509
  69.6 31.2 %all_to_all.15 = bf16[128,48,128]{2,1,0:T(8,128)(2,1)S(1)} all-to-all(bf16[128,48,128]{2,1,0:T(8,128)(2,1)S(1)} %get-tuple-element.17), channel_id=1, replica_groups=mesh['dp'=8,'cent'=16] {'dp','cent'}, dimensions={0} | all-to-all | bytes 3145728 | tf_op jit(solution)/shard_map/all_to_all | solution.py:426
  100.7 1.6 %shard_map.89 = (bf16[256,1024]{1,0:T(8,128)(2,1)}, f32[256,1024]{1,0:T(8,128)}) custom-call(bf16[256,512]{1,0:T(8,128)(2,1)S(1)} %get-tuple-element.16.back_ref, bf16[8,16,48,128]{3,2,1,0:T(8,128)(2,1)S(1)} %bitcast.7), custom_call_target="tpu_custom_call" | custom-call | flops 268435456 | bytes 4194304 | tf_op jit(solution)/shard_map/pallas_call | solution.py:522
  (8 shorter events, 0.1 us)
Async XLA Ops:
  0.6 1.0 %copy-start.6 = (bf16[256,1024]{1,0:T(8,128)(2,1)S(1)}, bf16[256,1024]{1,0:T(8,128)(2,1)}, u32[]{:S(2)}) copy-start(bf16[256,1024]{1,0:T(8,128)(2,1)} %points_hbm.1) | copy-start | bytes 1572868
  1.7 0.7 copy-start.8
  2.4 14.1 %copy-start.3 = (s32[4096]{0:T(1024)S(1)}, s32[4096]{0:T(1024)}, u32[]{:S(2)}) copy-start(s32[4096]{0:T(1024)} %param.7) | copy-start | bytes 49156
  4.9 11.9 %copy-start.4 = (bf16[4096,128]{1,0:T(8,128)(2,1)S(1)}, bf16[4096,128]{1,0:T(8,128)(2,1)}, u32[]{:S(2)}) copy-start(bf16[4096,128]{1,0:T(8,128)(2,1)} %old_ref.1) | copy-start | bytes 3145732
  4.9 32.9 %all-to-all-start = ((bf16[128,40,128]{2,1,0:T(8,128)(2,1)}), bf16[128,40,128]{2,1,0:T(8,128)(2,1)S(1)}, u32[]{:S(2)}, u32[]{:S(2)}) async-start(bf16[128,40,128]{2,1,0:T(8,128)(2,1)} %bitcast.1), calls=%async_computation | async-start | bytes 2621440 | tf_op jit(solution)/shard_map/all_to_all | solution.py:426
  16.8 21.0 %copy-start.7 = (s32[4096]{0:T(1024)S(1)}, s32[4096]{0:T(1024)}, u32[]{:S(2)}) copy-start(s32[4096]{0:T(1024)} %param.8) | copy-start | bytes 49156
  28.7 1.4 %copy-start.9 = (f32[512,1152]{1,0:T(8,128)}, f32[512,1152]{1,0:T(8,128)S(1)}, u32[]{:S(2)}) copy-start(f32[512,1152]{1,0:T(8,128)S(1)} %shard_map.86.start_hbm) | copy-start | bytes 7077892
  37.8 9.5 %copy-start = (bf16[128,40,128]{2,1,0:T(8,128)(2,1)}, bf16[128,40,128]{2,1,0:T(8,128)(2,1)S(1)}, u32[]{:S(2)}) copy-start(bf16[128,40,128]{2,1,0:T(8,128)(2,1)S(1)} %all-to-all-done.slab_ref) | copy-start | bytes 3932164
  37.8 2.1 %copy-start.10 = (f32[512,1152]{1,0:T(8,128)S(1)}, f32[512,1152]{1,0:T(8,128)}, u32[]{:S(2)}) copy-start(f32[512,1152]{1,0:T(8,128)} %copy-done.9) | copy-start | bytes 7077892
  47.3 1.0 %copy-start.2 = (bf16[16,280,128]{2,1,0:T(8,128)(2,1)}, bf16[16,280,128]{2,1,0:T(8,128)(2,1)S(1)}, u32[]{:S(2)}) copy-start(bf16[16,280,128]{2,1,0:T(8,128)(2,1)S(1)} %shard_map.87) | copy-start | bytes 3440644
  48.3 19.9 %all-to-all-start.1 = ((bf16[16,280,128]{2,1,0:T(8,128)(2,1)}), bf16[16,280,128]{2,1,0:T(8,128)(2,1)S(1)}, u32[]{:S(2)}, u32[]{:S(2)}) async-start(bf16[16,280,128]{2,1,0:T(8,128)(2,1)} %copy-done.2), calls=%async_computation.1 | async-start | bytes 2293760 | tf_op jit(solution)/shard_map/all_to_all | solution.py:426
  52.2 1.3 %copy-start.1 = (bf16[128,40,128]{2,1,0:T(8,128)(2,1)S(1)}, bf16[128,40,128]{2,1,0:T(8,128)(2,1)}, u32[]{:S(2)}) copy-start(bf16[128,40,128]{2,1,0:T(8,128)(2,1)} %copy-done) | copy-start | bytes 3932164
  53.5 1.2 %copy-start.5 = (bf16[4096,128]{1,0:T(8,128)(2,1)S(1)}, bf16[4096,128]{1,0:T(8,128)(2,1)}, u32[]{:S(2)}) copy-start(bf16[4096,128]{1,0:T(8,128)(2,1)} %old_ref.1) | copy-start | bytes 3145732

commit v3 on v2

--- a/solution.py
+++ b/solution.py
@@ -38,7 +38,7 @@
 VMEM = pl.BlockSpec(memory_space=pltpu.VMEM)
 
 
-def call(body, out_shape, ins, outs, scratch=(), flops=0, size=4 << 20, vmem=32 << 20, alias=None):
+def call(body, out_shape, ins, outs, scratch=(), flops=0, size=4 << 20, vmem=60 << 20, alias=None):
     return pl.pallas_call(
         body,
         out_shape=out_shape,

time: 103 us -> 108 us (1.049)
  Pallas kernels: 35.9 us -> 46.6 us
  local copies, waits for them, and re-layouts: 9.16 us -> 3.04 us
    unnamed x22 -> x6, local copies, waits for them, and re-layouts: 8.85 us -> 2.12 us
    pallas_call x1, Pallas kernels: 11.9 us -> 14.5 us  [on_device(): call(parent_kernel, shape(total_dims, F32), [VMEM, VMEM], VMEM, [pltpu.VM...]
    pallas_call x1, Pallas kernels: 7.33 us -> 9.3 us  [on_device(): call(upper_kernel, shape((owners, 280, lanes), BF16), [VMEM, VMEM, VMEM,...]
    pallas_call x1, Pallas kernels: 1.28 us -> 3.18 us  [on_device(): call(finish_kernel, (shape((256, lanes), F32), shape((devices, CAP + TOP,...]
    pallas_call x1, Pallas kernels: 1.62 us -> 3.12 us  [on_device(): call(unpack_kernel, (shape((count, width), BF16), shape((owners * TOP, wi...]
    pallas_call x1, Pallas kernels: 11.2 us -> 12.6 us  [on_device(): call(level_kernel, (shape((block, lanes), F32), shape((devices, CAP + TOP...]
    pallas_call x1, Pallas kernels: 2.55 us -> 3.84 us  [on_device(): call(pack_kernel, (shape((groups, owners, rows, lanes), BF16), shape((cou...]
  transfers between devices with their start and end apart: 2 -> 2, of which waited for: 2 -> 2; matrix products, arithmetic and copies ran while one was open for 0% -> 1% of each run, Pallas kernels for 23% -> 25%
where the time goes in v3:
time: 108 us; the launch traced here: 107 us
  Pallas kernels  46.6 us (43%)
  blocking collectives  32 us (30%)
  starting transfers between devices  15.4 us (14%)
  waiting for transfers between devices  9.36 us (9%)
  local copies, waits for them, and re-layouts  3.04 us (3%)
    all_to_all x1, blocking collectives, swap(): return lax.all_to_all(value, axes, split_axis=0, concat_axis=0, tiled=True)  32 us
    all_to_all x2, starting transfers between devices, swap(): return lax.all_to_all(value, axes, split_axis=0, concat_axis=0, tiled=True)  15.4 us
    pallas_call x1, Pallas kernels, on_device(): call(parent_kernel, shape(total_dims, F32), [VMEM, VMEM], VMEM, [pltpu.VM...  14.5 us
    pallas_call x1, Pallas kernels, on_device(): call(level_kernel, (shape((block, lanes), F32), shape((devices, CAP + TOP...  12.6 us
    all_to_all x2, waiting for transfers between devices, swap(): return lax.all_to_all(value, axes, split_axis=0, concat_axis=0, tiled=True)  9.36 us
    pallas_call x1, Pallas kernels, on_device(): call(upper_kernel, shape((owners, 280, lanes), BF16), [VMEM, VMEM, VMEM,...  9.3 us
    pallas_call x1, Pallas kernels, on_device(): call(pack_kernel, (shape((groups, owners, rows, lanes), BF16), shape((cou...  3.84 us
    pallas_call x1, Pallas kernels, on_device(): call(finish_kernel, (shape((256, lanes), F32), shape((devices, CAP + TOP,...  3.18 us
  transfers between devices with their start and end apart: 2, of which 2 were waited for; matrix products, arithmetic and copies ran while one was open for 1% of the time, Pallas kernels for 25%

profile of v3, /device:TPU:1, one launch (start us, length us, event | category | flops | bytes accessed | tf_op | source)
XLA Modules:
  0.0 107.2 jit_solution(13243855714917701764)
XLA Ops:
  0.6 0.0 copy-start.2
  0.6 3.8 %shard_map.84 = (bf16[8,16,40,128]{3,2,1,0:T(8,128)(2,1)}, bf16[256,512]{1,0:T(8,128)(2,1)}) custom-call(s32[1,256]{1,0:T(1,128)} %bitcast.13, bf16[256,1024]{1,0:T(8,128)(2,1)} %points_hbm.1), custom_call_target="tpu_custom_call" | custom-call | flops 268435456 | bytes 4194304 | tf_op jit(solution)/shard_map/pallas_call | solution.py:440
  4.5 11.5 %all-to-all-start = ((bf16[128,40,128]{2,1,0:T(8,128)(2,1)}), bf16[128,40,128]{2,1,0:T(8,128)(2,1)S(1)}, u32[]{:S(2)}, u32[]{:S(2)}) async-start(bf16[128,40,128]{2,1,0:T(8,128)(2,1)} %bitcast.8), calls=%async_computation | async-start | bytes 2621440 | tf_op jit(solution)/shard_map/all_to_all | solution.py:426
  16.0 0.0 copy-done.2
  16.0 0.1 shift_right_logical.14
  16.1 0.1 copy.10
  16.2 0.1 and.14
  16.2 0.1 copy.11
  16.4 0.6 pad.5.table_ref
  17.0 14.5 %shard_map.86.start_hbm = f32[512,1152]{1,0:T(8,128)} custom-call(s32[32,128]{1,0:T(8,128)} %bitcast.11, bf16[4096,128]{1,0:T(8,128)(2,1)} %old_ref.1), custom_call_target="tpu_custom_call" | custom-call | flops 4831838208 | bytes 4194304 | tf_op jit(solution)/shard_map/pallas_call | solution.py:455
  31.5 5.8 %all-to-all-done.slab_ref = bf16[128,40,128]{2,1,0:T(8,128)(2,1)S(1)} async-done(((bf16[128,40,128]{2,1,0:T(8,128)(2,1)}), bf16[128,40,128]{2,1,0:T(8,128)(2,1)S(1)}, u32[]{:S(2)}, u32[]{:S(2)}) %all-to-all-start) | async-done | bytes 1310752 | tf_op jit(solution)/shard_map/all_to_all | solution.py:426
  37.3 0.0 copy-start.1
  37.3 1.1 %copy-done.1 = bf16[128,40,128]{2,1,0:T(8,128)(2,1)} copy-done((bf16[128,40,128]{2,1,0:T(8,128)(2,1)}, bf16[128,40,128]{2,1,0:T(8,128)(2,1)S(1)}, u32[]{:S(2)}) %copy-start.1) | copy-done | bytes 1310744
  38.4 9.3 %shard_map.87 = bf16[16,280,128]{2,1,0:T(8,128)(2,1)} custom-call(bf16[128,40,128]{2,1,0:T(8,128)(2,1)} %copy-done.1, bf16[128,128]{1,0:T(8,128)(2,1)} %pad.5.table_ref, s32[32,128]{1,0:T(8,128)} %bitcast.12, f32[512,1152]{1,0:T(8,128)} %shard_map.86.start_hbm), custom_call_target="tpu_custom_call" | custom-call | flops 4831838208 | bytes 4194304 | tf_op jit(solution)/shard_map/pallas_call | solution.py:467
  47.7 3.9 %all-to-all-start.1 = ((bf16[16,280,128]{2,1,0:T(8,128)(2,1)}), bf16[16,280,128]{2,1,0:T(8,128)(2,1)S(1)}, u32[]{:S(2)}, u32[]{:S(2)}) async-start(bf16[16,280,128]{2,1,0:T(8,128)(2,1)} %shard_map.87), calls=%async_computation.1 | async-start | bytes 2293760 | tf_op jit(solution)/shard_map/all_to_all | solution.py:426
  51.7 12.6 %shard_map.85 = (f32[4096,128]{1,0:T(8,128)}, bf16[128,48,128]{2,1,0:T(8,128)(2,1)}) custom-call(bf16[128,40,128]{2,1,0:T(8,128)(2,1)} %copy-done.1, bf16[4096,128]{1,0:T(8,128)(2,1)} %old_ref.1), custom_call_target="tpu_custom_call" | custom-call | flops 9663676416 | bytes 4194304 | tf_op jit(solution)/shard_map/pallas_call | solution.py:487
  64.3 3.5 %all-to-all-done.1.parts_ref = bf16[16,280,128]{2,1,0:T(8,128)(2,1)S(1)} async-done(((bf16[16,280,128]{2,1,0:T(8,128)(2,1)}), bf16[16,280,128]{2,1,0:T(8,128)(2,1)S(1)}, u32[]{:S(2)}, u32[]{:S(2)}) %all-to-all-start.1) | async-done | bytes 1146912 | tf_op jit(solution)/shard_map/all_to_all | solution.py:426
  67.8 0.0 copy-start
  67.8 1.0 copy-done
  68.9 3.2 %shard_map.88 = (f32[256,128]{1,0:T(8,128)}, bf16[128,48,128]{2,1,0:T(8,128)(2,1)}) custom-call(bf16[16,280,128]{2,1,0:T(8,128)(2,1)} %copy-done, bf16[128,48,128]{2,1,0:T(8,128)(2,1)} %get-tuple-element.14.send_in), custom_call_target="tpu_custom_call", output_to_operand_aliasing={{1}: (1, {})} | custom-call | bytes 4194304 | tf_op jit(solution)/shard_map/pallas_call | solution.py:509
  72.1 32.0 %all_to_all.15 = bf16[128,48,128]{2,1,0:T(8,128)(2,1)} all-to-all(bf16[128,48,128]{2,1,0:T(8,128)(2,1)} %get-tuple-element.17), channel_id=1, replica_groups=mesh['dp'=8,'cent'=16] {'dp','cent'}, dimensions={0} | all-to-all | bytes 3145728 | tf_op jit(solution)/shard_map/all_to_all | solution.py:426
  104.0 3.1 %shard_map.89 = (bf16[256,1024]{1,0:T(8,128)(2,1)}, f32[256,1024]{1,0:T(8,128)}) custom-call(bf16[256,512]{1,0:T(8,128)(2,1)} %get-tuple-element.16.back_ref, bf16[8,16,48,128]{3,2,1,0:T(8,128)(2,1)} %bitcast.7), custom_call_target="tpu_custom_call" | custom-call | flops 268435456 | bytes 4194304 | tf_op jit(solution)/shard_map/pallas_call | solution.py:522
  (2 shorter events, 0.0 us)
Async XLA Ops:
  0.6 15.4 %copy-start.2 = (s32[4096]{0:T(1024)S(1)}, s32[4096]{0:T(1024)}, u32[]{:S(2)}) copy-start(s32[4096]{0:T(1024)} %param.7) | copy-start | bytes 49156
  4.5 32.9 %all-to-all-start = ((bf16[128,40,128]{2,1,0:T(8,128)(2,1)}), bf16[128,40,128]{2,1,0:T(8,128)(2,1)S(1)}, u32[]{:S(2)}, u32[]{:S(2)}) async-start(bf16[128,40,128]{2,1,0:T(8,128)(2,1)} %bitcast.8), calls=%async_computation | async-start | bytes 2621440 | tf_op jit(solution)/shard_map/all_to_all | solution.py:426
  37.3 1.1 %copy-start.1 = (bf16[128,40,128]{2,1,0:T(8,128)(2,1)}, bf16[128,40,128]{2,1,0:T(8,128)(2,1)S(1)}, u32[]{:S(2)}) copy-start(bf16[128,40,128]{2,1,0:T(8,128)(2,1)S(1)} %all-to-all-done.slab_ref) | copy-start | bytes 3932164
  47.7 20.1 %all-to-all-start.1 = ((bf16[16,280,128]{2,1,0:T(8,128)(2,1)}), bf16[16,280,128]{2,1,0:T(8,128)(2,1)S(1)}, u32[]{:S(2)}, u32[]{:S(2)}) async-start(bf16[16,280,128]{2,1,0:T(8,128)(2,1)} %shard_map.87), calls=%async_computation.1 | async-start | bytes 2293760 | tf_op jit(solution)/shard_map/all_to_all | solution.py:426
  67.8 1.0 copy-start

commit v4 on v3

--- a/solution.py
+++ b/solution.py
@@ -38,7 +38,12 @@
 VMEM = pl.BlockSpec(memory_space=pltpu.VMEM)
 
 
-def call(body, out_shape, ins, outs, scratch=(), flops=0, size=4 << 20, vmem=60 << 20, alias=None):
+FULL = 62_900_000
+LESS = 62_100_000
+LEAST = 61_100_000
+
+
+def call(body, out_shape, ins, outs, vmem, scratch=(), flops=0, size=4 << 20, alias=None):
     return pl.pallas_call(
         body,
         out_shape=out_shape,
@@ -51,7 +56,9 @@
     )
 
 
-def pack_kernel(assign_hbm, points_hbm, send_hbm, back_ref, assign_ref, points_ref, send_ref, sems):
+def pack_kernel(
+    assign_hbm, points_hbm, send_hbm, back_hbm, assign_ref, points_ref, send_ref, back_ref, sems
+):
     owners = send_ref.shape[1]
     parts = send_ref.shape[0]
     count = points_ref.shape[0]
@@ -103,7 +110,10 @@
             pltpu.make_async_copy(send_ref.at[part], send_hbm.at[part], sems.at[1 + parts // 2 + part])
         )
         stores[-1].start()
-    back_ref[...] = dot_nt(same, table).astype(BF16)
+        if part == 0:
+            back_ref[...] = dot_nt(same, table).astype(BF16)
+            stores.append(pltpu.make_async_copy(back_ref, back_hbm, sems.at[1 + parts // 2 + parts]))
+            stores[-1].start()
     for store in stores:
         store.wait()
 
@@ -190,22 +200,24 @@
     return slab_ref[pl.ds(group * 16, 16), HALF:CAP, :].reshape(256, LANES).astype(F32)
 
 
-def any_label(digits_ref, group):
-    return jnp.max(digits_ref[pl.ds(16 + 2 * group, 2), :]) > 0.0
-
-
-def parent_kernel(parent_ref, old_ref, total_ref, digits_ref):
+def mark_live(digits_ref, live_ref):
+    for group in range(live_ref.shape[0]):
+        most = jnp.max(digits_ref[16 + 2 * group : 18 + 2 * group, :])
+        live_ref[group] = jnp.where(most > 0.0, 1, 0)
+
+
+def parent_kernel(parent_ref, old_ref, total_ref, digits_ref, left_ref, high_ref):
     parent = parent_ref[...]
     digits_ref[0:32, :] = (lax.shift_right_logical(parent, 6) + 1).astype(F32)
     digits_ref[32:64, :] = ((parent & 63) + 1).astype(F32)
-    total_ref[...] = jnp.zeros_like(total_ref)
-
-    def step(at, carry):
-        rows = old_ref[pl.ds(pl.multiple_of(at * 256, 256), 256), :].astype(F32)
-        add_segments(total_ref, digits_ref, 2 * at, rows)
-        return carry
-
-    lax.fori_loop(0, old_ref.shape[0] // 256, step, 0)
+    segments(
+        total_ref,
+        left_ref,
+        high_ref,
+        lambda step: old_ref[lane_slice(step, 512), :].astype(F32),
+        digits_ref,
+        old_ref.shape[0] // 512,
+    )
 
 
 def find_parents(digits_ref, parents_ref, table_ref, at, count):
@@ -221,17 +233,18 @@
 
 def upper_kernel(
     slab_ref, table_ref, top_ref, start_hbm, send_hbm,
-    digits_ref, parents_ref, total_ref, left_ref, high_ref, start_ref, send_ref, right_ref, sems,
+    digits_ref, parents_ref, total_ref, left_ref, high_ref, start_ref, send_ref, right_ref, live_ref, sems,
 ):
     load = pltpu.make_async_copy(start_hbm, start_ref, sems.at[0])
     load.start()
     slot_digits(slab_ref, digits_ref)
+    mark_live(digits_ref, live_ref)
     for step in range(4):
         find_parents(digits_ref, parents_ref, table_ref, 4 * step, 4)
     segments(total_ref, left_ref, high_ref, lambda step: lower_rows(slab_ref, step), parents_ref, 4)
 
     def more(group, carry):
-        @pl.when(any_label(digits_ref, group))
+        @pl.when(live_ref[group] > 0)
         def _():
             find_parents(digits_ref, parents_ref, table_ref, 16 + 2 * group, 2)
             add_segments(total_ref, parents_ref, 16 + 2 * group, upper_rows(slab_ref, group))
@@ -290,17 +303,18 @@
 
 def level_kernel(
     slab_ref, old_hbm, level_hbm, residual_hbm,
-    digits_ref, total_ref, table_ref, left_ref, high_ref, old_ref, level_ref, residual_ref,
+    digits_ref, total_ref, table_ref, left_ref, high_ref, old_ref, level_ref, residual_ref, live_ref,
     load_sem, level_sems, low_sems, up_sems,
 ):
     load = pltpu.make_async_copy(old_hbm, old_ref, load_sem)
     load.start()
     slot_digits(slab_ref, digits_ref)
+    mark_live(digits_ref, live_ref)
     segments(total_ref, left_ref, high_ref, lambda step: lower_rows(slab_ref, step), digits_ref, 4)
     groups = slab_ref.shape[0] // 16
 
     def more(group, carry):
-        @pl.when(any_label(digits_ref, group))
+        @pl.when(live_ref[group] > 0)
         def _():
             add_segments(total_ref, digits_ref, 16 + 2 * group, upper_rows(slab_ref, group))
 
@@ -356,15 +370,13 @@
 
     def finish(group, carry):
         sources = pl.ds(group * 16, 16)
-        live = any_label(digits_ref, group)
-
-        @pl.when(live)
+        @pl.when(live_ref[group] > 0)
         def _():
             residual_ref[sources, HALF:CAP, :] = subtract(
                 16 + 2 * group, 2, upper_rows(slab_ref, group)
             ).reshape(16, HALF, LANES)
 
-        @pl.when(jnp.logical_not(live))
+        @pl.when(live_ref[group] == 0)
         def _():
             residual_ref[sources, HALF:CAP, :] = slab_ref[sources, HALF:CAP, :]
 
@@ -441,12 +453,14 @@
         pack_kernel,
         (shape((groups, owners, rows, lanes), BF16), shape((count, slots), BF16)),
         [HBM, HBM],
-        (HBM, VMEM),
+        (HBM, HBM),
+        FULL,
         [
             pltpu.VMEM((1, count), I32),
             pltpu.VMEM((count, width), BF16),
             pltpu.VMEM((groups, owners, rows, lanes), BF16),
-            pltpu.SemaphoreType.DMA((1 + groups // 2 + groups,)),
+            pltpu.VMEM((count, slots), BF16),
+            pltpu.SemaphoreType.DMA((2 + groups // 2 + groups,)),
         ],
         flops=2 * slots * count * width,
     )(assign.reshape(1, count), points)
@@ -457,7 +471,12 @@
         shape(total_dims, F32),
         [VMEM, VMEM],
         VMEM,
-        [pltpu.VMEM((64, LANES), F32)],
+        FULL,
+        [
+            pltpu.VMEM((64, LANES), F32),
+            pltpu.VMEM((LOW, block), BF16),
+            pltpu.VMEM((block, LANES), I32),
+        ],
         flops=work,
     )(parent_one.reshape(block // LANES, LANES), old_level_one)
     grid = parent_one.reshape(64, 64).T
@@ -469,6 +488,7 @@
         shape((owners, 280, lanes), BF16),
         [VMEM, VMEM, VMEM, HBM],
         HBM,
+        LESS,
         [
             pltpu.VMEM((64, LANES), F32),
             pltpu.VMEM((64, LANES), F32),
@@ -478,6 +498,7 @@
             pltpu.VMEM(total_dims, F32),
             pltpu.VMEM((owners, 280, lanes), BF16),
             pltpu.VMEM((HIGHS * LOW, 2 * LANES), BF16),
+            pltpu.SMEM((groups,), I32),
             pltpu.SemaphoreType.DMA((5,)),
         ],
         flops=work,
@@ -489,6 +510,7 @@
         (shape((block, lanes), F32), shape((devices, CAP + TOP, lanes), BF16)),
         [VMEM, HBM],
         (HBM, HBM),
+        LEAST,
         [
             pltpu.VMEM((64, LANES), F32),
             pltpu.VMEM(total_dims, F32),
@@ -498,6 +520,7 @@
             pltpu.VMEM((block, lanes), BF16),
             pltpu.VMEM((block, lanes), F32),
             pltpu.VMEM((devices, CAP, lanes), BF16),
+            pltpu.SMEM((groups,), I32),
             pltpu.SemaphoreType.DMA(()),
             pltpu.SemaphoreType.DMA((HIGHS,)),
             pltpu.SemaphoreType.DMA((4,)),
@@ -511,6 +534,7 @@
         (shape((256, lanes), F32), shape((devices, CAP + TOP, lanes), BF16)),
         [VMEM, HBM],
         (VMEM, HBM),
+        LESS,
         [
             pltpu.VMEM((LANES, LANES), F32),
             pltpu.VMEM((devices, TOP, lanes), BF16),
@@ -524,6 +548,7 @@
         (shape((count, width), BF16), shape((owners * TOP, width), F32)),
         [VMEM, VMEM],
         (VMEM, VMEM),
+        LESS,
         flops=2 * slots * count * width,
     )(back, returned.reshape(groups, owners, CAP + TOP, lanes))
     return (level_one, level_two, level_three, residual)

time: 108 us -> 106 us (0.981)
  Pallas kernels: 46.6 us -> 38 us
  waiting for transfers between devices: 9.36 us -> 16.5 us
    all_to_all x2, waiting for transfers between devices: 9.36 us -> 16.5 us  [swap(): return lax.all_to_all(value, axes, split_axis=0, concat_axis=0, tiled=True)]
    pallas_call x1, Pallas kernels: 14.5 us -> 9.29 us  [on_device(): call(parent_kernel, shape(total_dims, F32), [VMEM, VMEM], VMEM, FULL, [pl...]
    pallas_call x1, Pallas kernels: 12.6 us -> 10.8 us  [on_device(): call(level_kernel, (shape((block, lanes), F32), shape((devices, CAP + TOP...]
  transfers between devices with their start and end apart: 2 -> 2, of which waited for: 2 -> 2; matrix products, arithmetic and copies ran while one was open for 1% -> 1% of each run, Pallas kernels for 25% -> 19%
where the time goes in v4:
time: 106 us
  Pallas kernels  38 us (36%)
  blocking collectives  32 us (30%)
  waiting for transfers between devices  16.5 us (16%)
  starting transfers between devices  15.5 us (15%)
  local copies, waits for them, and re-layouts  3.04 us (3%)
    all_to_all x1, blocking collectives, swap(): return lax.all_to_all(value, axes, split_axis=0, concat_axis=0, tiled=True)  32 us
    all_to_all x2, waiting for transfers between devices, swap(): return lax.all_to_all(value, axes, split_axis=0, concat_axis=0, tiled=True)  16.5 us
    all_to_all x2, starting transfers between devices, swap(): return lax.all_to_all(value, axes, split_axis=0, concat_axis=0, tiled=True)  15.5 us
    pallas_call x1, Pallas kernels, on_device(): call(level_kernel, (shape((block, lanes), F32), shape((devices, CAP + TOP...  10.8 us
    pallas_call x1, Pallas kernels, on_device(): call(parent_kernel, shape(total_dims, F32), [VMEM, VMEM], VMEM, FULL, [pl...  9.29 us
    pallas_call x1, Pallas kernels, on_device(): call(upper_kernel, shape((owners, 280, lanes), BF16), [VMEM, VMEM, VMEM,...  8.39 us
    pallas_call x1, Pallas kernels, on_device(): call(pack_kernel, (shape((groups, owners, rows, lanes), BF16), shape((cou...  3.19 us
    pallas_call x1, Pallas kernels, on_device(): call(finish_kernel, (shape((256, lanes), F32), shape((devices, CAP + TOP,...  3.18 us
  transfers between devices with their start and end apart: 2, of which 2 were waited for; matrix products, arithmetic and copies ran while one was open for 1% of the time, Pallas kernels for 19%

profile of v4, /device:TPU:1, one launch (start us, length us, event | category | flops | bytes accessed | tf_op | source)
XLA Modules:
  0.0 105.8 jit_solution(1694150820816377818)
XLA Ops:
  0.6 0.0 copy-start.2
  0.6 3.2 %shard_map.84 = (bf16[8,16,40,128]{3,2,1,0:T(8,128)(2,1)}, bf16[256,512]{1,0:T(8,128)(2,1)}) custom-call(s32[1,256]{1,0:T(1,128)} %bitcast.13, bf16[256,1024]{1,0:T(8,128)(2,1)} %points_hbm.1), custom_call_target="tpu_custom_call" | custom-call | flops 268435456 | bytes 4194304 | tf_op jit(solution)/shard_map/pallas_call | solution.py:452
  3.8 11.5 %all-to-all-start = ((bf16[128,40,128]{2,1,0:T(8,128)(2,1)}), bf16[128,40,128]{2,1,0:T(8,128)(2,1)S(1)}, u32[]{:S(2)}, u32[]{:S(2)}) async-start(bf16[128,40,128]{2,1,0:T(8,128)(2,1)} %bitcast.8), calls=%async_computation | async-start | bytes 2621440 | tf_op jit(solution)/shard_map/all_to_all | solution.py:438
  15.4 0.0 copy-done.2
  15.4 0.1 shift_right_logical.14
  15.5 0.1 copy.10
  15.5 0.1 and.14
  15.6 0.1 copy.11
  15.7 0.6 pad.5.table_ref
  16.3 9.3 %shard_map.86.start_hbm = f32[512,1152]{1,0:T(8,128)} custom-call(s32[32,128]{1,0:T(8,128)} %bitcast.11, bf16[4096,128]{1,0:T(8,128)(2,1)} %old_ref.1), custom_call_target="tpu_custom_call" | custom-call | flops 4831838208 | bytes 4194304 | tf_op jit(solution)/shard_map/pallas_call | solution.py:469
  25.6 11.1 %all-to-all-done.slab_ref = bf16[128,40,128]{2,1,0:T(8,128)(2,1)S(1)} async-done(((bf16[128,40,128]{2,1,0:T(8,128)(2,1)}), bf16[128,40,128]{2,1,0:T(8,128)(2,1)S(1)}, u32[]{:S(2)}, u32[]{:S(2)}) %all-to-all-start) | async-done | bytes 1310752 | tf_op jit(solution)/shard_map/all_to_all | solution.py:438
  36.7 0.0 copy-start.1
  36.7 1.1 %copy-done.1 = bf16[128,40,128]{2,1,0:T(8,128)(2,1)} copy-done((bf16[128,40,128]{2,1,0:T(8,128)(2,1)}, bf16[128,40,128]{2,1,0:T(8,128)(2,1)S(1)}, u32[]{:S(2)}) %copy-start.1) | copy-done | bytes 1310744
  37.8 8.4 %shard_map.87 = bf16[16,280,128]{2,1,0:T(8,128)(2,1)} custom-call(bf16[128,40,128]{2,1,0:T(8,128)(2,1)} %copy-done.1, bf16[128,128]{1,0:T(8,128)(2,1)} %pad.5.table_ref, s32[32,128]{1,0:T(8,128)} %bitcast.12, f32[512,1152]{1,0:T(8,128)} %shard_map.86.start_hbm), custom_call_target="tpu_custom_call" | custom-call | flops 4831838208 | bytes 4194304 | tf_op jit(solution)/shard_map/pallas_call | solution.py:486
  46.2 4.0 %all-to-all-start.1 = ((bf16[16,280,128]{2,1,0:T(8,128)(2,1)}), bf16[16,280,128]{2,1,0:T(8,128)(2,1)S(1)}, u32[]{:S(2)}, u32[]{:S(2)}) async-start(bf16[16,280,128]{2,1,0:T(8,128)(2,1)} %shard_map.87), calls=%async_computation.1 | async-start | bytes 2293760 | tf_op jit(solution)/shard_map/all_to_all | solution.py:438
  50.2 10.8 %shard_map.85 = (f32[4096,128]{1,0:T(8,128)}, bf16[128,48,128]{2,1,0:T(8,128)(2,1)}) custom-call(bf16[128,40,128]{2,1,0:T(8,128)(2,1)} %copy-done.1, bf16[4096,128]{1,0:T(8,128)(2,1)} %old_ref.1), custom_call_target="tpu_custom_call" | custom-call | flops 9663676416 | bytes 4194304 | tf_op jit(solution)/shard_map/pallas_call | solution.py:508
  61.1 5.4 %all-to-all-done.1.parts_ref = bf16[16,280,128]{2,1,0:T(8,128)(2,1)S(1)} async-done(((bf16[16,280,128]{2,1,0:T(8,128)(2,1)}), bf16[16,280,128]{2,1,0:T(8,128)(2,1)S(1)}, u32[]{:S(2)}, u32[]{:S(2)}) %all-to-all-start.1) | async-done | bytes 1146912 | tf_op jit(solution)/shard_map/all_to_all | solution.py:438
  66.4 0.0 copy-start
  66.4 1.0 copy-done
  67.5 3.2 %shard_map.88 = (f32[256,128]{1,0:T(8,128)}, bf16[128,48,128]{2,1,0:T(8,128)(2,1)}) custom-call(bf16[16,280,128]{2,1,0:T(8,128)(2,1)} %copy-done, bf16[128,48,128]{2,1,0:T(8,128)(2,1)} %get-tuple-element.14.send_in), custom_call_target="tpu_custom_call", output_to_operand_aliasing={{1}: (1, {})} | custom-call | bytes 4194304 | tf_op jit(solution)/shard_map/pallas_call | solution.py:532
  70.7 32.0 %all_to_all.15 = bf16[128,48,128]{2,1,0:T(8,128)(2,1)} all-to-all(bf16[128,48,128]{2,1,0:T(8,128)(2,1)} %get-tuple-element.17), channel_id=1, replica_groups=mesh['dp'=8,'cent'=16] {'dp','cent'}, dimensions={0} | all-to-all | bytes 3145728 | tf_op jit(solution)/shard_map/all_to_all | solution.py:438
  102.6 3.1 %shard_map.89 = (bf16[256,1024]{1,0:T(8,128)(2,1)}, f32[256,1024]{1,0:T(8,128)}) custom-call(bf16[256,512]{1,0:T(8,128)(2,1)} %get-tuple-element.16.back_ref, bf16[8,16,48,128]{3,2,1,0:T(8,128)(2,1)} %bitcast.7), custom_call_target="tpu_custom_call" | custom-call | flops 268435456 | bytes 4194304 | tf_op jit(solution)/shard_map/pallas_call | solution.py:546
  (2 shorter events, 0.0 us)
Async XLA Ops:
  0.6 14.7 %copy-start.2 = (s32[4096]{0:T(1024)S(1)}, s32[4096]{0:T(1024)}, u32[]{:S(2)}) copy-start(s32[4096]{0:T(1024)} %param.7) | copy-start | bytes 49156
  3.8 32.9 %all-to-all-start = ((bf16[128,40,128]{2,1,0:T(8,128)(2,1)}), bf16[128,40,128]{2,1,0:T(8,128)(2,1)S(1)}, u32[]{:S(2)}, u32[]{:S(2)}) async-start(bf16[128,40,128]{2,1,0:T(8,128)(2,1)} %bitcast.8), calls=%async_computation | async-start | bytes 2621440 | tf_op jit(solution)/shard_map/all_to_all | solution.py:438
  36.7 1.1 %copy-start.1 = (bf16[128,40,128]{2,1,0:T(8,128)(2,1)}, bf16[128,40,128]{2,1,0:T(8,128)(2,1)S(1)}, u32[]{:S(2)}) copy-start(bf16[128,40,128]{2,1,0:T(8,128)(2,1)S(1)} %all-to-all-done.slab_ref) | copy-start | bytes 3932164
  46.2 20.3 %all-to-all-start.1 = ((bf16[16,280,128]{2,1,0:T(8,128)(2,1)}), bf16[16,280,128]{2,1,0:T(8,128)(2,1)S(1)}, u32[]{:S(2)}, u32[]{:S(2)}) async-start(bf16[16,280,128]{2,1,0:T(8,128)(2,1)} %shard_map.87), calls=%async_computation.1 | async-start | bytes 2293760 | tf_op jit(solution)/shard_map/all_to_all | solution.py:438
  66.4 1.0 copy-start

commit v5 on v4

--- a/solution.py
+++ b/solution.py
@@ -39,8 +39,9 @@
 
 
 FULL = 62_900_000
-LESS = 62_100_000
-LEAST = 61_100_000
+UPPER = 61_000_000
+LEVEL = 58_600_000
+SMALL = 16_000_000
 
 
 def call(body, out_shape, ins, outs, vmem, scratch=(), flops=0, size=4 << 20, alias=None):
@@ -488,7 +489,7 @@
         shape((owners, 280, lanes), BF16),
         [VMEM, VMEM, VMEM, HBM],
         HBM,
-        LESS,
+        UPPER,
         [
             pltpu.VMEM((64, LANES), F32),
             pltpu.VMEM((64, LANES), F32),
@@ -510,7 +511,7 @@
         (shape((block, lanes), F32), shape((devices, CAP + TOP, lanes), BF16)),
         [VMEM, HBM],
         (HBM, HBM),
-        LEAST,
+        LEVEL,
         [
             pltpu.VMEM((64, LANES), F32),
             pltpu.VMEM(total_dims, F32),
@@ -534,7 +535,7 @@
         (shape((256, lanes), F32), shape((devices, CAP + TOP, lanes), BF16)),
         [VMEM, HBM],
         (VMEM, HBM),
-        LESS,
+        SMALL,
         [
             pltpu.VMEM((LANES, LANES), F32),
             pltpu.VMEM((devices, TOP, lanes), BF16),
@@ -548,7 +549,7 @@
         (shape((count, width), BF16), shape((owners * TOP, width), F32)),
         [VMEM, VMEM],
         (VMEM, VMEM),
-        LESS,
+        SMALL,
         flops=2 * slots * count * width,
     )(back, returned.reshape(groups, owners, CAP + TOP, lanes))
     return (level_one, level_two, level_three, residual)

time: 106 us -> 105 us (level)
  Pallas kernels: 38 us -> 32.5 us
  waiting for transfers between devices: 16.5 us -> 19.7 us
  local copies, waits for them, and re-layouts: 3.04 us -> 4.59 us
  blocking collectives: 32 us -> 30.5 us
  starting transfers between devices: 15.5 us -> 17 us
    all_to_all x2, waiting for transfers between devices: 16.5 us -> 19.7 us  [swap(): return lax.all_to_all(value, axes, split_axis=0, concat_axis=0, tiled=True)]
    pallas_call x1, Pallas kernels: 3.18 us -> 1.28 us  [on_device(): call(finish_kernel, (shape((256, lanes), F32), shape((devices, CAP + TOP,...]
    unnamed x6 -> x10, local copies, waits for them, and re-layouts: 2.12 us -> 3.66 us
    pallas_call x1, Pallas kernels: 3.12 us -> 1.62 us  [on_device(): call(unpack_kernel, (shape((count, width), BF16), shape((owners * TOP, wi...]
    all_to_all x1, blocking collectives: 32 us -> 30.5 us  [swap(): return lax.all_to_all(value, axes, split_axis=0, concat_axis=0, tiled=True)]
    all_to_all x2, starting transfers between devices: 15.5 us -> 17 us  [swap(): return lax.all_to_all(value, axes, split_axis=0, concat_axis=0, tiled=True)]
    pallas_call x1, Pallas kernels: 10.8 us -> 9.61 us  [on_device(): call(level_kernel, (shape((block, lanes), F32), shape((devices, CAP + TOP...]
  transfers between devices with their start and end apart: 2 -> 2, of which waited for: 2 -> 2; matrix products, arithmetic and copies ran while one was open for 1% -> 1% of each run, Pallas kernels for 19% -> 18%
where the time goes in v5:
time: 105 us
  Pallas kernels  32.5 us (31%)
  blocking collectives  30.5 us (29%)
  waiting for transfers between devices  19.7 us (19%)
  starting transfers between devices  17 us (16%)
  local copies, waits for them, and re-layouts  4.59 us (4%)
    all_to_all x1, blocking collectives, swap(): return lax.all_to_all(value, axes, split_axis=0, concat_axis=0, tiled=True)  30.5 us
    all_to_all x2, waiting for transfers between devices, swap(): return lax.all_to_all(value, axes, split_axis=0, concat_axis=0, tiled=True)  19.7 us
    all_to_all x2, starting transfers between devices, swap(): return lax.all_to_all(value, axes, split_axis=0, concat_axis=0, tiled=True)  17 us
    pallas_call x1, Pallas kernels, on_device(): call(level_kernel, (shape((block, lanes), F32), shape((devices, CAP + TOP...  9.61 us
    pallas_call x1, Pallas kernels, on_device(): call(parent_kernel, shape(total_dims, F32), [VMEM, VMEM], VMEM, FULL, [pl...  9.29 us
    pallas_call x1, Pallas kernels, on_device(): call(upper_kernel, shape((owners, 280, lanes), BF16), [VMEM, VMEM, VMEM,...  7.5 us
    unnamed x10, local copies, waits for them, and re-layouts  3.66 us
    pallas_call x1, Pallas kernels, on_device(): call(pack_kernel, (shape((groups, owners, rows, lanes), BF16), shape((cou...  3.19 us
  transfers between devices with their start and end apart: 2, of which 2 were waited for; matrix products, arithmetic and copies ran while one was open for 1% of the time, Pallas kernels for 18%

profile of v5, /device:TPU:1, one launch (start us, length us, event | category | flops | bytes accessed | tf_op | source)
XLA Modules:
  0.0 105.1 jit_solution(2104121666226635179)
XLA Ops:
  0.6 0.0 copy-start.4
  0.6 3.2 %shard_map.84 = (bf16[8,16,40,128]{3,2,1,0:T(8,128)(2,1)}, bf16[256,512]{1,0:T(8,128)(2,1)}) custom-call(s32[1,256]{1,0:T(1,128)} %bitcast.13, bf16[256,1024]{1,0:T(8,128)(2,1)} %points_hbm.1), custom_call_target="tpu_custom_call" | custom-call | flops 268435456 | bytes 4194304 | tf_op jit(solution)/shard_map/pallas_call | solution.py:453
  3.8 11.5 %all-to-all-start = ((bf16[128,40,128]{2,1,0:T(8,128)(2,1)}), bf16[128,40,128]{2,1,0:T(8,128)(2,1)S(1)}, u32[]{:S(2)}, u32[]{:S(2)}) async-start(bf16[128,40,128]{2,1,0:T(8,128)(2,1)} %bitcast.8), calls=%async_computation | async-start | bytes 2621440 | tf_op jit(solution)/shard_map/all_to_all | solution.py:439
  15.4 0.0 copy-done.4
  15.4 0.1 shift_right_logical.14
  15.5 0.1 copy.10
  15.5 0.1 and.14
  15.6 0.1 copy.11
  15.7 0.6 pad.5.table_ref
  16.3 9.3 %shard_map.86.start_hbm = f32[512,1152]{1,0:T(8,128)} custom-call(s32[32,128]{1,0:T(8,128)} %bitcast.11, bf16[4096,128]{1,0:T(8,128)(2,1)} %old_ref.1), custom_call_target="tpu_custom_call" | custom-call | flops 4831838208 | bytes 4194304 | tf_op jit(solution)/shard_map/pallas_call | solution.py:470
  25.6 11.1 %all-to-all-done.slab_ref = bf16[128,40,128]{2,1,0:T(8,128)(2,1)S(1)} async-done(((bf16[128,40,128]{2,1,0:T(8,128)(2,1)}), bf16[128,40,128]{2,1,0:T(8,128)(2,1)S(1)}, u32[]{:S(2)}, u32[]{:S(2)}) %all-to-all-start) | async-done | bytes 1310752 | tf_op jit(solution)/shard_map/all_to_all | solution.py:439
  36.7 0.0 copy-start.3
  36.7 1.1 %copy-done.3 = bf16[128,40,128]{2,1,0:T(8,128)(2,1)} copy-done((bf16[128,40,128]{2,1,0:T(8,128)(2,1)}, bf16[128,40,128]{2,1,0:T(8,128)(2,1)S(1)}, u32[]{:S(2)}) %copy-start.3) | copy-done | bytes 1310744
  37.8 7.5 %shard_map.87 = bf16[16,280,128]{2,1,0:T(8,128)(2,1)} custom-call(bf16[128,40,128]{2,1,0:T(8,128)(2,1)} %copy-done.3, bf16[128,128]{1,0:T(8,128)(2,1)} %pad.5.table_ref, s32[32,128]{1,0:T(8,128)} %bitcast.12, f32[512,1152]{1,0:T(8,128)} %shard_map.86.start_hbm), custom_call_target="tpu_custom_call" | custom-call | flops 4831838208 | bytes 4194304 | tf_op jit(solution)/shard_map/pallas_call | solution.py:487
  45.3 5.5 %all-to-all-start.1 = ((bf16[16,280,128]{2,1,0:T(8,128)(2,1)}), bf16[16,280,128]{2,1,0:T(8,128)(2,1)S(1)}, u32[]{:S(2)}, u32[]{:S(2)}) async-start(bf16[16,280,128]{2,1,0:T(8,128)(2,1)} %shard_map.87), calls=%async_computation.1 | async-start | bytes 2293760 | tf_op jit(solution)/shard_map/all_to_all | solution.py:439
  50.8 9.6 %shard_map.85 = (f32[4096,128]{1,0:T(8,128)}, bf16[128,48,128]{2,1,0:T(8,128)(2,1)}) custom-call(bf16[128,40,128]{2,1,0:T(8,128)(2,1)} %copy-done.3, bf16[4096,128]{1,0:T(8,128)(2,1)} %old_ref.1), custom_call_target="tpu_custom_call" | custom-call | flops 9663676416 | bytes 4194304 | tf_op jit(solution)/shard_map/pallas_call | solution.py:509
  60.4 8.7 %all-to-all-done.1.parts_ref = bf16[16,280,128]{2,1,0:T(8,128)(2,1)S(1)} async-done(((bf16[16,280,128]{2,1,0:T(8,128)(2,1)}), bf16[16,280,128]{2,1,0:T(8,128)(2,1)S(1)}, u32[]{:S(2)}, u32[]{:S(2)}) %all-to-all-start.1) | async-done | bytes 1146912 | tf_op jit(solution)/shard_map/all_to_all | solution.py:439
  69.1 0.0 copy-start
  69.1 1.4 %copy-done = bf16[128,48,128]{2,1,0:T(8,128)(2,1)S(1)} copy-done((bf16[128,48,128]{2,1,0:T(8,128)(2,1)S(1)}, bf16[128,48,128]{2,1,0:T(8,128)(2,1)}, u32[]{:S(2)}) %copy-start) | copy-done | bytes 1572888
  70.5 1.3 %shard_map.88 = (f32[256,128]{1,0:T(8,128)}, bf16[128,48,128]{2,1,0:T(8,128)(2,1)S(1)}) custom-call(bf16[16,280,128]{2,1,0:T(8,128)(2,1)S(1)} %all-to-all-done.1.parts_ref, bf16[128,48,128]{2,1,0:T(8,128)(2,1)S(1)} %copy-done), custom_call_target="tpu_custom_call", output_to_operand_aliasing={{1}: (1, {})} | custom-call | bytes 4194304 | tf_op jit(solution)/shard_map/pallas_call | solution.py:533
  71.8 0.0 copy-start.1
  71.8 1.2 %copy-done.1 = bf16[128,48,128]{2,1,0:T(8,128)(2,1)} copy-done((bf16[128,48,128]{2,1,0:T(8,128)(2,1)}, bf16[128,48,128]{2,1,0:T(8,128)(2,1)S(1)}, u32[]{:S(2)}) %copy-start.1) | copy-done | bytes 1572888
  73.0 0.0 copy-start.2
  73.0 30.5 %all_to_all.15 = bf16[128,48,128]{2,1,0:T(8,128)(2,1)S(1)} all-to-all(bf16[128,48,128]{2,1,0:T(8,128)(2,1)} %copy-done.1), channel_id=1, replica_groups=mesh['dp'=8,'cent'=16] {'dp','cent'}, dimensions={0} | all-to-all | bytes 3145728 | tf_op jit(solution)/shard_map/all_to_all | solution.py:439
  103.5 0.0 copy-done.2
  103.5 1.6 %shard_map.89 = (bf16[256,1024]{1,0:T(8,128)(2,1)}, f32[256,1024]{1,0:T(8,128)}) custom-call(bf16[256,512]{1,0:T(8,128)(2,1)S(1)} %copy-done.2, bf16[8,16,48,128]{3,2,1,0:T(8,128)(2,1)S(1)} %bitcast.7), custom_call_target="tpu_custom_call" | custom-call | flops 268435456 | bytes 4194304 | tf_op jit(solution)/shard_map/pallas_call | solution.py:547
  (2 shorter events, 0.0 us)
Async XLA Ops:
  0.6 14.7 %copy-start.4 = (s32[4096]{0:T(1024)S(1)}, s32[4096]{0:T(1024)}, u32[]{:S(2)}) copy-start(s32[4096]{0:T(1024)} %param.7) | copy-start | bytes 49156
  3.8 32.9 %all-to-all-start = ((bf16[128,40,128]{2,1,0:T(8,128)(2,1)}), bf16[128,40,128]{2,1,0:T(8,128)(2,1)S(1)}, u32[]{:S(2)}, u32[]{:S(2)}) async-start(bf16[128,40,128]{2,1,0:T(8,128)(2,1)} %bitcast.8), calls=%async_computation | async-start | bytes 2621440 | tf_op jit(solution)/shard_map/all_to_all | solution.py:439
  36.7 1.1 %copy-start.3 = (bf16[128,40,128]{2,1,0:T(8,128)(2,1)}, bf16[128,40,128]{2,1,0:T(8,128)(2,1)S(1)}, u32[]{:S(2)}) copy-start(bf16[128,40,128]{2,1,0:T(8,128)(2,1)S(1)} %all-to-all-done.slab_ref) | copy-start | bytes 3932164
  45.3 23.8 %all-to-all-start.1 = ((bf16[16,280,128]{2,1,0:T(8,128)(2,1)}), bf16[16,280,128]{2,1,0:T(8,128)(2,1)S(1)}, u32[]{:S(2)}, u32[]{:S(2)}) async-start(bf16[16,280,128]{2,1,0:T(8,128)(2,1)} %shard_map.87), calls=%async_computation.1 | async-start | bytes 2293760 | tf_op jit(solution)/shard_map/all_to_all | solution.py:439
  69.1 1.4 %copy-start = (bf16[128,48,128]{2,1,0:T(8,128)(2,1)S(1)}, bf16[128,48,128]{2,1,0:T(8,128)(2,1)}, u32[]{:S(2)}) copy-start(bf16[128,48,128]{2,1,0:T(8,128)(2,1)} %get-tuple-element.14.send_in) | copy-start | bytes 4718596
  71.8 1.2 %copy-start.1 = (bf16[128,48,128]{2,1,0:T(8,128)(2,1)}, bf16[128,48,128]{2,1,0:T(8,128)(2,1)S(1)}, u32[]{:S(2)}) copy-start(bf16[128,48,128]{2,1,0:T(8,128)(2,1)S(1)} %get-tuple-element.17) | copy-start | bytes 4718596
  73.0 30.5 %copy-start.2 = (bf16[256,512]{1,0:T(8,128)(2,1)S(1)}, bf16[256,512]{1,0:T(8,128)(2,1)}, u32[]{:S(2)}) copy-start(bf16[256,512]{1,0:T(8,128)(2,1)} %get-tuple-element.16.back_ref) | copy-start | bytes 786436

commit v6 on v5

--- a/solution.py
+++ b/solution.py
@@ -39,8 +39,8 @@
 
 
 FULL = 62_900_000
-UPPER = 61_000_000
-LEVEL = 58_600_000
+UPPER = 59_000_000
+LEVEL = 48_000_000
 SMALL = 16_000_000
 
 
@@ -257,41 +257,43 @@
     at = slice(HIGHS * LANES, (HIGHS + 1) * LANES)
     weights = total_ref[:, at] + start_ref[:, at]
     coarse = weights.astype(BF16).astype(F32)
-    fine = weights - coarse
     lane = iota((LOW, LANES), 1)
+    split = jnp.where(lane < HIGHS, coarse, weights - coarse)
+    diagonal = jnp.where(iota((16, LANES), 0) == iota((16, LANES), 1), 1.0, 0.0).astype(BF16)
+    across = dot_nt(diagonal, split.astype(BF16))
     tops = []
     for high in range(HIGHS):
         mass = (total_ref[:, lane_slice(high)] + start_ref[:, lane_slice(high)]).astype(BF16)
         for half in range(2):
             send_ref[2 * high + half, 0:256, :] = mass[half * 256 : (half + 1) * 256]
         right_ref[lane_slice(high, LOW), 0:LANES] = mass
-        right_ref[lane_slice(high, LOW), LANES:] = jnp.where(
-            lane == high, coarse, jnp.where(lane == high + 8, fine, 0.0)
-        ).astype(BF16)
+        right_ref[lane_slice(high, LOW), LANES:] = jnp.where((lane & 7) == high, split, 0.0).astype(BF16)
         for part in range(4):
             hit = iota((256, LANES), 0) == top_ref[high * 4 + part : high * 4 + part + 1, :]
             tops.append(jnp.where(hit, 1.0, 0.0).astype(BF16))
     tops = dot(jnp.concatenate(tops, axis=1), right_ref[...])
     top_mass = tops[:, :LANES].astype(BF16)
-    top_weight = jnp.sum(tops[:, LANES:].T[0:16], axis=0, keepdims=True)
+    first = jnp.where(iota((8, LANES), 1) < 16, 1.0, 0.0)
+    top_weight = lax.dot_general(
+        first,
+        tops[:, LANES:],
+        (((1,), (1,)), ((), ())),
+        precision=lax.Precision.HIGHEST,
+        preferred_element_type=F32,
+    )[0:1]
     top_coarse = top_weight.astype(BF16).astype(F32)
     top_fine = top_weight - top_coarse
-    coarse_t, fine_t = coarse.T, fine.T
+    top_rows = [part[:, lane_slice(half)] for part in (top_coarse, top_fine) for half in range(2)]
     stores = []
     for owner in range(send_ref.shape[0]):
         send_ref[owner, 256:272, :] = top_mass[owner * TOP : (owner + 1) * TOP]
-        high, from_lane = owner // 2, (owner % 2) * 256
-        rows = []
-        for source, line_at, lane_at in (
-            (coarse_t, high, from_lane),
-            (fine_t, high, from_lane),
-            (top_coarse, 0, 0),
-            (top_fine, 0, 0),
-        ):
-            for half in range(2):
-                first = lane_at + half * LANES
-                rows.append(source[line_at : line_at + 1, first : first + LANES])
-        send_ref[owner, 272:280, :] = jnp.concatenate(rows, axis=0).astype(BF16)
+        high = owner // 2
+        rows = [
+            across[line : line + 1, lane_slice(owner % 2 * 2 + half)]
+            for line in (high, high + HIGHS)
+            for half in range(2)
+        ]
+        send_ref[owner, 272:280, :] = jnp.concatenate(rows + top_rows, axis=0).astype(BF16)
         if owner % 4 == 3:
             part = pl.ds(owner - 3, 4)
             stores.append(

time: 105 us -> 101 us (0.962)
  waiting for transfers between devices: 19.7 us -> 15.2 us
  starting transfers between devices: 17 us -> 15.4 us
    all_to_all x2, waiting for transfers between devices: 19.7 us -> 15.2 us  [swap(): return lax.all_to_all(value, axes, split_axis=0, concat_axis=0, tiled=True)]
    all_to_all x2, starting transfers between devices: 17 us -> 15.4 us  [swap(): return lax.all_to_all(value, axes, split_axis=0, concat_axis=0, tiled=True)]
    pallas_call x1, Pallas kernels: 7.5 us -> 8.62 us  [on_device(): call(upper_kernel, shape((owners, 280, lanes), BF16), [VMEM, VMEM, VMEM,...]
  transfers between devices with their start and end apart: 2 -> 2, of which waited for: 2 -> 2; matrix products, arithmetic and copies ran while one was open for 1% -> 1% of each run, Pallas kernels for 18% -> 19%
where the time goes in v6:
time: 101 us; the launch traced here: 100 us
  Pallas kernels  33.4 us (33%)
  blocking collectives  31 us (31%)
  starting transfers between devices  15.4 us (15%)
  waiting for transfers between devices  15.2 us (15%)
  local copies, waits for them, and re-layouts  4.53 us (4%)
    all_to_all x1, blocking collectives, swap(): return lax.all_to_all(value, axes, split_axis=0, concat_axis=0, tiled=True)  31 us
    all_to_all x2, starting transfers between devices, swap(): return lax.all_to_all(value, axes, split_axis=0, concat_axis=0, tiled=True)  15.4 us
    all_to_all x2, waiting for transfers between devices, swap(): return lax.all_to_all(value, axes, split_axis=0, concat_axis=0, tiled=True)  15.2 us
    pallas_call x1, Pallas kernels, on_device(): call(level_kernel, (shape((block, lanes), F32), shape((devices, CAP + TOP...  9.42 us
    pallas_call x1, Pallas kernels, on_device(): call(parent_kernel, shape(total_dims, F32), [VMEM, VMEM], VMEM, FULL, [pl...  9.29 us
    pallas_call x1, Pallas kernels, on_device(): call(upper_kernel, shape((owners, 280, lanes), BF16), [VMEM, VMEM, VMEM,...  8.62 us
    unnamed x10, local copies, waits for them, and re-layouts  3.6 us
    pallas_call x1, Pallas kernels, on_device(): call(pack_kernel, (shape((groups, owners, rows, lanes), BF16), shape((cou...  3.19 us
  transfers between devices with their start and end apart: 2, of which 2 were waited for; matrix products, arithmetic and copies ran while one was open for 1% of the time, Pallas kernels for 19%

profile of v6, /device:TPU:1, one launch (start us, length us, event | category | flops | bytes accessed | tf_op | source)
XLA Modules:
  0.0 100.3 jit_solution(17124518612556395899)
XLA Ops:
  0.6 0.0 copy-start.4
  0.6 3.2 %shard_map.84 = (bf16[8,16,40,128]{3,2,1,0:T(8,128)(2,1)}, bf16[256,512]{1,0:T(8,128)(2,1)}) custom-call(s32[1,256]{1,0:T(1,128)} %bitcast.13, bf16[256,1024]{1,0:T(8,128)(2,1)} %points_hbm.1), custom_call_target="tpu_custom_call" | custom-call | flops 268435456 | bytes 4194304 | tf_op jit(solution)/shard_map/pallas_call | solution.py:455
  3.8 11.5 %all-to-all-start = ((bf16[128,40,128]{2,1,0:T(8,128)(2,1)}), bf16[128,40,128]{2,1,0:T(8,128)(2,1)S(1)}, u32[]{:S(2)}, u32[]{:S(2)}) async-start(bf16[128,40,128]{2,1,0:T(8,128)(2,1)} %bitcast.8), calls=%async_computation | async-start | bytes 2621440 | tf_op jit(solution)/shard_map/all_to_all | solution.py:441
  15.4 0.0 copy-done.4
  15.4 0.1 shift_right_logical.14
  15.5 0.1 copy.10
  15.5 0.1 and.14
  15.6 0.1 copy.11
  15.7 0.6 pad.5.table_ref
  16.3 9.3 %shard_map.86.start_hbm = f32[512,1152]{1,0:T(8,128)} custom-call(s32[32,128]{1,0:T(8,128)} %bitcast.11, bf16[4096,128]{1,0:T(8,128)(2,1)} %old_ref.1), custom_call_target="tpu_custom_call" | custom-call | flops 4831838208 | bytes 4194304 | tf_op jit(solution)/shard_map/pallas_call | solution.py:472
  25.6 11.1 %all-to-all-done.slab_ref = bf16[128,40,128]{2,1,0:T(8,128)(2,1)S(1)} async-done(((bf16[128,40,128]{2,1,0:T(8,128)(2,1)}), bf16[128,40,128]{2,1,0:T(8,128)(2,1)S(1)}, u32[]{:S(2)}, u32[]{:S(2)}) %all-to-all-start) | async-done | bytes 1310752 | tf_op jit(solution)/shard_map/all_to_all | solution.py:441
  36.7 0.0 copy-start
  36.7 1.1 %copy-done = bf16[128,40,128]{2,1,0:T(8,128)(2,1)} copy-done((bf16[128,40,128]{2,1,0:T(8,128)(2,1)}, bf16[128,40,128]{2,1,0:T(8,128)(2,1)S(1)}, u32[]{:S(2)}) %copy-start) | copy-done | bytes 1310744
  37.8 8.6 %shard_map.87 = bf16[16,280,128]{2,1,0:T(8,128)(2,1)} custom-call(bf16[128,40,128]{2,1,0:T(8,128)(2,1)} %copy-done, bf16[128,128]{1,0:T(8,128)(2,1)} %pad.5.table_ref, s32[32,128]{1,0:T(8,128)} %bitcast.12, f32[512,1152]{1,0:T(8,128)} %shard_map.86.start_hbm), custom_call_target="tpu_custom_call" | custom-call | flops 4831838208 | bytes 4194304 | tf_op jit(solution)/shard_map/pallas_call | solution.py:489
  46.4 3.9 %all-to-all-start.1 = ((bf16[16,280,128]{2,1,0:T(8,128)(2,1)}), bf16[16,280,128]{2,1,0:T(8,128)(2,1)S(1)}, u32[]{:S(2)}, u32[]{:S(2)}) async-start(bf16[16,280,128]{2,1,0:T(8,128)(2,1)} %shard_map.87), calls=%async_computation.1 | async-start | bytes 2293760 | tf_op jit(solution)/shard_map/all_to_all | solution.py:441
  50.3 0.0 copy-start.1
  50.3 1.3 %copy-done.1 = bf16[128,40,128]{2,1,0:T(8,128)(2,1)S(1)} copy-done((bf16[128,40,128]{2,1,0:T(8,128)(2,1)S(1)}, bf16[128,40,128]{2,1,0:T(8,128)(2,1)}, u32[]{:S(2)}) %copy-start.1) | copy-done | bytes 1310744
  51.6 0.0 copy-start.3
  51.6 1.2 %copy-done.3 = bf16[4096,128]{1,0:T(8,128)(2,1)S(1)} copy-done((bf16[4096,128]{1,0:T(8,128)(2,1)S(1)}, bf16[4096,128]{1,0:T(8,128)(2,1)}, u32[]{:S(2)}) %copy-start.3) | copy-done | bytes 1048600
  52.8 9.4 %shard_map.85 = (f32[4096,128]{1,0:T(8,128)}, bf16[128,48,128]{2,1,0:T(8,128)(2,1)S(1)}) custom-call(bf16[128,40,128]{2,1,0:T(8,128)(2,1)S(1)} %copy-done.1, bf16[4096,128]{1,0:T(8,128)(2,1)S(1)} %copy-done.3), custom_call_target="tpu_custom_call" | custom-call | flops 9663676416 | bytes 4194304 | tf_op jit(solution)/shard_map/pallas_call | solution.py:511
  62.3 4.1 %all-to-all-done.1.parts_ref = bf16[16,280,128]{2,1,0:T(8,128)(2,1)S(1)} async-done(((bf16[16,280,128]{2,1,0:T(8,128)(2,1)}), bf16[16,280,128]{2,1,0:T(8,128)(2,1)S(1)}, u32[]{:S(2)}, u32[]{:S(2)}) %all-to-all-start.1) | async-done | bytes 1146912 | tf_op jit(solution)/shard_map/all_to_all | solution.py:441
  66.4 1.3 %shard_map.88 = (f32[256,128]{1,0:T(8,128)}, bf16[128,48,128]{2,1,0:T(8,128)(2,1)S(1)}) custom-call(bf16[16,280,128]{2,1,0:T(8,128)(2,1)S(1)} %all-to-all-done.1.parts_ref, bf16[128,48,128]{2,1,0:T(8,128)(2,1)S(1)} %get-tuple-element.14.send_in), custom_call_target="tpu_custom_call", output_to_operand_aliasing={{1}: (1, {})} | custom-call | bytes 4194304 | tf_op jit(solution)/shard_map/pallas_call | solution.py:535
  67.6 0.0 copy-start.2
  67.7 31.0 %all_to_all.15 = bf16[128,48,128]{2,1,0:T(8,128)(2,1)S(1)} all-to-all(bf16[128,48,128]{2,1,0:T(8,128)(2,1)S(1)} %get-tuple-element.17), channel_id=1, replica_groups=mesh['dp'=8,'cent'=16] {'dp','cent'}, dimensions={0} | all-to-all | bytes 3145728 | tf_op jit(solution)/shard_map/all_to_all | solution.py:441
  98.7 0.0 copy-done.2
  98.7 1.6 %shard_map.89 = (bf16[256,1024]{1,0:T(8,128)(2,1)}, f32[256,1024]{1,0:T(8,128)}) custom-call(bf16[256,512]{1,0:T(8,128)(2,1)S(1)} %copy-done.2, bf16[8,16,48,128]{3,2,1,0:T(8,128)(2,1)S(1)} %bitcast.7), custom_call_target="tpu_custom_call" | custom-call | flops 268435456 | bytes 4194304 | tf_op jit(solution)/shard_map/pallas_call | solution.py:549
  (2 shorter events, 0.0 us)
Async XLA Ops:
  0.6 14.7 %copy-start.4 = (s32[4096]{0:T(1024)S(1)}, s32[4096]{0:T(1024)}, u32[]{:S(2)}) copy-start(s32[4096]{0:T(1024)} %param.7) | copy-start | bytes 49156
  3.8 32.9 %all-to-all-start = ((bf16[128,40,128]{2,1,0:T(8,128)(2,1)}), bf16[128,40,128]{2,1,0:T(8,128)(2,1)S(1)}, u32[]{:S(2)}, u32[]{:S(2)}) async-start(bf16[128,40,128]{2,1,0:T(8,128)(2,1)} %bitcast.8), calls=%async_computation | async-start | bytes 2621440 | tf_op jit(solution)/shard_map/all_to_all | solution.py:441
  36.7 1.1 %copy-start = (bf16[128,40,128]{2,1,0:T(8,128)(2,1)}, bf16[128,40,128]{2,1,0:T(8,128)(2,1)S(1)}, u32[]{:S(2)}) copy-start(bf16[128,40,128]{2,1,0:T(8,128)(2,1)S(1)} %all-to-all-done.slab_ref) | copy-start | bytes 3932164
  46.4 20.0 %all-to-all-start.1 = ((bf16[16,280,128]{2,1,0:T(8,128)(2,1)}), bf16[16,280,128]{2,1,0:T(8,128)(2,1)S(1)}, u32[]{:S(2)}, u32[]{:S(2)}) async-start(bf16[16,280,128]{2,1,0:T(8,128)(2,1)} %shard_map.87), calls=%async_computation.1 | async-start | bytes 2293760 | tf_op jit(solution)/shard_map/all_to_all | solution.py:441
  50.3 1.3 %copy-start.1 = (bf16[128,40,128]{2,1,0:T(8,128)(2,1)S(1)}, bf16[128,40,128]{2,1,0:T(8,128)(2,1)}, u32[]{:S(2)}) copy-start(bf16[128,40,128]{2,1,0:T(8,128)(2,1)} %copy-done) | copy-start | bytes 3932164
  51.6 1.2 %copy-start.3 = (bf16[4096,128]{1,0:T(8,128)(2,1)S(1)}, bf16[4096,128]{1,0:T(8,128)(2,1)}, u32[]{:S(2)}) copy-start(bf16[4096,128]{1,0:T(8,128)(2,1)} %old_ref.1) | copy-start | bytes 3145732
  67.6 31.0 %copy-start.2 = (bf16[256,512]{1,0:T(8,128)(2,1)S(1)}, bf16[256,512]{1,0:T(8,128)(2,1)}, u32[]{:S(2)}) copy-start(bf16[256,512]{1,0:T(8,128)(2,1)} %get-tuple-element.16.back_ref) | copy-start | bytes 786436

commit v7 on v6

--- a/solution.py
+++ b/solution.py
@@ -39,9 +39,10 @@
 
 
 FULL = 62_900_000
-UPPER = 59_000_000
+UPPER = 50_000_000
 LEVEL = 48_000_000
 SMALL = 16_000_000
+SPARE = 12
 
 
 def call(body, out_shape, ins, outs, vmem, scratch=(), flops=0, size=4 << 20, alias=None):
@@ -207,7 +208,7 @@
         live_ref[group] = jnp.where(most > 0.0, 1, 0)
 
 
-def parent_kernel(parent_ref, old_ref, total_ref, digits_ref, left_ref, high_ref):
+def parent_kernel(parent_ref, old_ref, total_hbm, digits_ref, left_ref, high_ref, total_ref, sem):
     parent = parent_ref[...]
     digits_ref[0:32, :] = (lax.shift_right_logical(parent, 6) + 1).astype(F32)
     digits_ref[32:64, :] = ((parent & 63) + 1).astype(F32)
@@ -219,6 +220,9 @@
         digits_ref,
         old_ref.shape[0] // 512,
     )
+    store = pltpu.make_async_copy(total_ref, total_hbm.at[0], sem)
+    store.start()
+    store.wait()
 
 
 def find_parents(digits_ref, parents_ref, table_ref, at, count):
@@ -234,9 +238,10 @@
 
 def upper_kernel(
     slab_ref, table_ref, top_ref, start_hbm, send_hbm,
-    digits_ref, parents_ref, total_ref, left_ref, high_ref, start_ref, send_ref, right_ref, live_ref, sems,
+    digits_ref, parents_ref, total_ref, left_ref, high_ref, start_ref, send_ref, right_ref, tail_ref, live_ref,
+    sems,
 ):
-    load = pltpu.make_async_copy(start_hbm, start_ref, sems.at[0])
+    load = pltpu.make_async_copy(start_hbm.at[0], start_ref, sems.at[0])
     load.start()
     slot_digits(slab_ref, digits_ref)
     mark_live(digits_ref, live_ref)
@@ -262,44 +267,40 @@
     diagonal = jnp.where(iota((16, LANES), 0) == iota((16, LANES), 1), 1.0, 0.0).astype(BF16)
     across = dot_nt(diagonal, split.astype(BF16))
     tops = []
+    stores = []
     for high in range(HIGHS):
         mass = (total_ref[:, lane_slice(high)] + start_ref[:, lane_slice(high)]).astype(BF16)
         for half in range(2):
-            send_ref[2 * high + half, 0:256, :] = mass[half * 256 : (half + 1) * 256]
+            send_ref[2 * high + half, 0:32] = mass[half * 256 : (half + 1) * 256].reshape(32, 8, LANES)
+        part = (pl.ds(2 * high, 2), pl.ds(0, 32))
+        stores.append(pltpu.make_async_copy(send_ref.at[part], send_hbm.at[part], sems.at[1 + high]))
+        stores[-1].start()
         right_ref[lane_slice(high, LOW), 0:LANES] = mass
         right_ref[lane_slice(high, LOW), LANES:] = jnp.where((lane & 7) == high, split, 0.0).astype(BF16)
         for part in range(4):
             hit = iota((256, LANES), 0) == top_ref[high * 4 + part : high * 4 + part + 1, :]
             tops.append(jnp.where(hit, 1.0, 0.0).astype(BF16))
+    for half in range(2):
+        for kind in range(2):
+            lines = slice(kind * HIGHS, (kind + 1) * HIGHS)
+            for side in range(2):
+                tail_ref[pl.ds(side, HIGHS, 2), 2 * kind + half, :] = across[lines, lane_slice(2 * side + half)]
     tops = dot(jnp.concatenate(tops, axis=1), right_ref[...])
-    top_mass = tops[:, :LANES].astype(BF16)
-    first = jnp.where(iota((8, LANES), 1) < 16, 1.0, 0.0)
-    top_weight = lax.dot_general(
-        first,
-        tops[:, LANES:],
-        (((1,), (1,)), ((), ())),
-        precision=lax.Precision.HIGHEST,
-        preferred_element_type=F32,
-    )[0:1]
+    owners = send_ref.shape[0]
+    send_ref[:, 32:34] = tops[:, :LANES].astype(BF16).reshape(owners, 2, 8, LANES)
+    first = jnp.where(iota((8, LANES), 1) < 16, 1.0, 0.0).astype(BF16)
+    heavy = tops[:, LANES:]
+    heavy_coarse = heavy.astype(BF16)
+    heavy_fine = (heavy - heavy_coarse.astype(F32)).astype(BF16)
+    top_weight = (dot_nt(first, heavy_coarse) + dot_nt(first, heavy_fine))[0:1]
     top_coarse = top_weight.astype(BF16).astype(F32)
-    top_fine = top_weight - top_coarse
-    top_rows = [part[:, lane_slice(half)] for part in (top_coarse, top_fine) for half in range(2)]
-    stores = []
-    for owner in range(send_ref.shape[0]):
-        send_ref[owner, 256:272, :] = top_mass[owner * TOP : (owner + 1) * TOP]
-        high = owner // 2
-        rows = [
-            across[line : line + 1, lane_slice(owner % 2 * 2 + half)]
-            for line in (high, high + HIGHS)
-            for half in range(2)
-        ]
-        send_ref[owner, 272:280, :] = jnp.concatenate(rows + top_rows, axis=0).astype(BF16)
-        if owner % 4 == 3:
-            part = pl.ds(owner - 3, 4)
-            stores.append(
-                pltpu.make_async_copy(send_ref.at[part], send_hbm.at[part], sems.at[1 + owner // 4])
-            )
-            stores[-1].start()
+    for kind, value in enumerate((top_coarse, top_weight - top_coarse)):
+        for half in range(2):
+            tail_ref[:, 4 + 2 * kind + half, :] = jnp.broadcast_to(value[:, lane_slice(half)], (owners, LANES))
+    send_ref[:, 34:35] = tail_ref[...].astype(BF16)[:, None]
+    part = (slice(None), pl.ds(32, 3))
+    stores.append(pltpu.make_async_copy(send_ref.at[part], send_hbm.at[part], sems.at[1 + HIGHS]))
+    stores[-1].start()
     for store in stores:
         store.wait()
 
@@ -401,6 +402,7 @@
     total = parts_ref[0].astype(F32)
     for source in range(1, parts_ref.shape[0]):
         total += parts_ref[source].astype(F32)
+    total = total.reshape(-1, LANES)
     tail = total[272:280].T
     me = lax.axis_index("cent")
     chosen = jnp.where(me < 8, tail[:, 4:5] + tail[:, 6:7], tail[:, 5:6] + tail[:, 7:8])
@@ -417,9 +419,13 @@
     store.wait()
 
 
-def unpack_kernel(back_ref, returned_ref, residual_ref, level_ref):
+def unpack_kernel(back_ref, returned_ref, residual_hbm, level_hbm, residual_ref, level_ref, sems):
     groups, owners, rows, lanes = returned_ref.shape
+    stores = []
     for pair in range(groups // 2):
+        for side in range(2):
+            top = returned_ref[2 * pair + side, :, CAP:rows, :].astype(F32)
+            level_ref[:, lane_slice(2 * pair + side)] = top.reshape(owners * TOP, lanes)
         right = jnp.concatenate(
             [
                 returned_ref[2 * pair + side, :, 0:CAP, :].reshape(owners * CAP, lanes)
@@ -427,10 +433,16 @@
             ],
             axis=1,
         )
-        residual_ref[:, lane_slice(pair, 2 * lanes)] = dot(back_ref[...], right).astype(BF16)
-    for group in range(groups):
-        top = returned_ref[group, :, CAP:rows, :].astype(F32)
-        level_ref[:, lane_slice(group)] = top.reshape(owners * TOP, lanes)
+        at = lane_slice(pair, 2 * lanes)
+        stores.append(pltpu.make_async_copy(level_ref.at[:, at], level_hbm.at[:, at], sems.at[2 * pair]))
+        stores[-1].start()
+        residual_ref[:, at] = dot(back_ref[...], right).astype(BF16)
+        stores.append(
+            pltpu.make_async_copy(residual_ref.at[:, at], residual_hbm.at[:, at], sems.at[2 * pair + 1])
+        )
+        stores[-1].start()
+    for store in stores:
+        store.wait()
 
 
 def shape(dims, kind):
@@ -471,14 +483,16 @@
 
     start = call(
         parent_kernel,
-        shape(total_dims, F32),
+        shape((SPARE, *total_dims), F32),
         [VMEM, VMEM],
-        VMEM,
+        HBM,
         FULL,
         [
             pltpu.VMEM((64, LANES), F32),
             pltpu.VMEM((LOW, block), BF16),
             pltpu.VMEM((block, LANES), I32),
+            pltpu.VMEM(total_dims, F32),
+            pltpu.SemaphoreType.DMA(()),
         ],
         flops=work,
     )(parent_one.reshape(block // LANES, LANES), old_level_one)
@@ -488,7 +502,7 @@
 
     share = call(
         upper_kernel,
-        shape((owners, 280, lanes), BF16),
+        shape((owners, 35, 8, lanes), BF16),
         [VMEM, VMEM, VMEM, HBM],
         HBM,
         UPPER,
@@ -499,10 +513,11 @@
             pltpu.VMEM((LOW, 2048), BF16),
             pltpu.VMEM((2048, LANES), I32),
             pltpu.VMEM(total_dims, F32),
-            pltpu.VMEM((owners, 280, lanes), BF16),
+            pltpu.VMEM((owners, 35, 8, lanes), BF16),
             pltpu.VMEM((HIGHS * LOW, 2 * LANES), BF16),
+            pltpu.VMEM((owners, 8, lanes), F32),
             pltpu.SMEM((groups,), I32),
-            pltpu.SemaphoreType.DMA((5,)),
+            pltpu.SemaphoreType.DMA((2 + HIGHS,)),
         ],
         flops=work,
     )(slab, table, parent_two.reshape(-1, LANES), start)
@@ -550,8 +565,13 @@
         unpack_kernel,
         (shape((count, width), BF16), shape((owners * TOP, width), F32)),
         [VMEM, VMEM],
-        (VMEM, VMEM),
+        (HBM, HBM),
         SMALL,
+        [
+            pltpu.VMEM((count, width), BF16),
+            pltpu.VMEM((owners * TOP, width), F32),
+            pltpu.SemaphoreType.DMA((groups,)),
+        ],
         flops=2 * slots * count * width,
     )(back, returned.reshape(groups, owners, CAP + TOP, lanes))
     return (level_one, level_two, level_three, residual)

time: 101 us -> 99 us (0.980)
  waiting for transfers between devices: 15.2 us -> 18.4 us
  local copies, waits for them, and re-layouts: 4.53 us -> 1.55 us
  Pallas kernels: 33.4 us -> 30.6 us
    all_to_all x2, waiting for transfers between devices: 15.2 us -> 18.4 us  [swap(): return lax.all_to_all(value, axes, split_axis=0, concat_axis=0, tiled=True)]
    pallas_call x2, Pallas kernels: 17.9 us -> 15.3 us  [the longest x1 9.31 us: on_device(): call(parent_kernel, shape((SPARE, *total_dims), F32), [VMEM, VMEM], HBM,...]
    unnamed x10 -> x8, local copies, waits for them, and re-layouts: 3.6 us -> 1.24 us
    pallas_call x1, Pallas kernels: 9.42 us -> 8.12 us  [on_device(): call(level_kernel, (shape((block, lanes), F32), shape((devices, CAP + TOP...]
    pallas_call x1, Pallas kernels: 1.28 us -> 2.54 us  [on_device(): call(finish_kernel, (shape((256, lanes), F32), shape((devices, CAP + TOP,...]
  transfers between devices with their start and end apart: 2 -> 2, of which waited for: 2 -> 2; matrix products, arithmetic and copies ran while one was open for 1% -> 0% of each run, Pallas kernels for 19% -> 18%
where the time goes in v7:
time: 99 us; the launch traced here: 98.6 us
  blocking collectives  31 us (31%)
  Pallas kernels  30.6 us (31%)
  waiting for transfers between devices  18.4 us (19%)
  starting transfers between devices  16.1 us (16%)
  local copies, waits for them, and re-layouts  1.55 us (2%)
    all_to_all x1, blocking collectives, swap(): return lax.all_to_all(value, axes, split_axis=0, concat_axis=0, tiled=True)  31 us
    all_to_all x2, waiting for transfers between devices, swap(): return lax.all_to_all(value, axes, split_axis=0, concat_axis=0, tiled=True)  18.4 us
    all_to_all x2, starting transfers between devices, swap(): return lax.all_to_all(value, axes, split_axis=0, concat_axis=0, tiled=True)  16.1 us
    pallas_call x1, Pallas kernels, on_device(): call(parent_kernel, shape((SPARE, *total_dims), F32), [VMEM, VMEM], HBM,...  9.31 us
    pallas_call x1, Pallas kernels, on_device(): call(level_kernel, (shape((block, lanes), F32), shape((devices, CAP + TOP...  8.12 us
    pallas_call x1, Pallas kernels, on_device(): call(upper_kernel, shape((owners, 35, 8, lanes), BF16), [VMEM, VMEM, VMEM...  6 us
    pallas_call x1, Pallas kernels, on_device(): call(pack_kernel, (shape((groups, owners, rows, lanes), BF16), shape((cou...  3.19 us
    pallas_call x1, Pallas kernels, on_device(): call(finish_kernel, (shape((256, lanes), F32), shape((devices, CAP + TOP,...  2.54 us
  transfers between devices with their start and end apart: 2, of which 2 were waited for; matrix products, arithmetic and copies ran while one was open for 0% of the time, Pallas kernels for 18%

profile of v7, /device:TPU:1, one launch (start us, length us, event | category | flops | bytes accessed | tf_op | source)
XLA Modules:
  0.0 98.6 jit_solution(15310176396123139079)
XLA Ops:
  0.6 0.0 copy-start.3
  0.6 3.2 %shard_map.84 = (bf16[8,16,40,128]{3,2,1,0:T(8,128)(2,1)}, bf16[256,512]{1,0:T(8,128)(2,1)}) custom-call(s32[1,256]{1,0:T(1,128)} %bitcast.13, bf16[256,1024]{1,0:T(8,128)(2,1)} %points_hbm.1), custom_call_target="tpu_custom_call" | custom-call | flops 268435456 | bytes 4194304 | tf_op jit(solution)/shard_map/pallas_call | solution.py:467
  3.8 11.5 %all-to-all-start = ((bf16[128,40,128]{2,1,0:T(8,128)(2,1)}), bf16[128,40,128]{2,1,0:T(8,128)(2,1)S(1)}, u32[]{:S(2)}, u32[]{:S(2)}) async-start(bf16[128,40,128]{2,1,0:T(8,128)(2,1)} %bitcast.9), calls=%async_computation | async-start | bytes 2621440 | tf_op jit(solution)/shard_map/all_to_all | solution.py:453
  15.4 0.0 copy-done.3
  15.4 0.1 shift_right_logical.14
  15.5 0.1 copy.10
  15.5 0.1 and.14
  15.6 0.1 copy.11
  15.7 0.0 copy-start.2
  15.8 9.3 %shard_map.86.start_hbm = f32[12,512,1152]{2,1,0:T(8,128)} custom-call(s32[32,128]{1,0:T(8,128)} %bitcast.12, bf16[4096,128]{1,0:T(8,128)(2,1)} %old_ref.1), custom_call_target="tpu_custom_call" | custom-call | flops 4831838208 | bytes 4194304 | tf_op jit(solution)/shard_map/pallas_call | solution.py:484
  25.1 11.6 %all-to-all-done.slab_ref = bf16[128,40,128]{2,1,0:T(8,128)(2,1)S(1)} async-done(((bf16[128,40,128]{2,1,0:T(8,128)(2,1)}), bf16[128,40,128]{2,1,0:T(8,128)(2,1)S(1)}, u32[]{:S(2)}, u32[]{:S(2)}) %all-to-all-start) | async-done | bytes 1310752 | tf_op jit(solution)/shard_map/all_to_all | solution.py:453
  36.7 0.0 copy-done.2
  36.7 6.0 %shard_map.87 = bf16[16,35,8,128]{3,2,1,0:T(8,128)(2,1)} custom-call(bf16[128,40,128]{2,1,0:T(8,128)(2,1)S(1)} %all-to-all-done.slab_ref, bf16[128,128]{1,0:T(8,128)(2,1)S(1)} %pad.5.table_ref, s32[32,128]{1,0:T(8,128)S(1)} %bitcast.8, f32[12,512,1152]{2,1,0:T(8,128)} %shard_map.86.start_hbm), custom_call_target="tpu_custom_call" | custom-call | flops 4831838208 | bytes 4194304 | tf_op jit(solution)/shard_map/pallas_call | solution.py:503
  42.7 4.6 %all-to-all-start.1 = ((bf16[16,35,8,128]{3,2,1,0:T(8,128)(2,1)}), bf16[16,35,8,128]{3,2,1,0:T(8,128)(2,1)}, u32[]{:S(2)}, u32[]{:S(2)}) async-start(bf16[16,35,8,128]{3,2,1,0:T(8,128)(2,1)} %shard_map.87), calls=%async_computation.1 | async-start | bytes 2293760 | tf_op jit(solution)/shard_map/all_to_all | solution.py:453
  47.3 0.0 copy-start
  47.3 1.2 %copy-done = bf16[4096,128]{1,0:T(8,128)(2,1)S(1)} copy-done((bf16[4096,128]{1,0:T(8,128)(2,1)S(1)}, bf16[4096,128]{1,0:T(8,128)(2,1)}, u32[]{:S(2)}) %copy-start) | copy-done | bytes 1048600
  48.5 8.1 %shard_map.85 = (f32[4096,128]{1,0:T(8,128)}, bf16[128,48,128]{2,1,0:T(8,128)(2,1)S(1)}) custom-call(bf16[128,40,128]{2,1,0:T(8,128)(2,1)S(1)} %all-to-all-done.slab_ref, bf16[4096,128]{1,0:T(8,128)(2,1)S(1)} %copy-done), custom_call_target="tpu_custom_call" | custom-call | flops 9663676416 | bytes 4194304 | tf_op jit(solution)/shard_map/pallas_call | solution.py:526
  56.7 6.8 %all-to-all-done.1.parts_ref = bf16[16,35,8,128]{3,2,1,0:T(8,128)(2,1)} async-done(((bf16[16,35,8,128]{3,2,1,0:T(8,128)(2,1)}), bf16[16,35,8,128]{3,2,1,0:T(8,128)(2,1)}, u32[]{:S(2)}, u32[]{:S(2)}) %all-to-all-start.1) | async-done | bytes 1146912 | tf_op jit(solution)/shard_map/all_to_all | solution.py:453
  63.4 2.5 %shard_map.88 = (f32[256,128]{1,0:T(8,128)}, bf16[128,48,128]{2,1,0:T(8,128)(2,1)S(1)}) custom-call(bf16[16,35,8,128]{3,2,1,0:T(8,128)(2,1)} %all-to-all-done.1.parts_ref, bf16[128,48,128]{2,1,0:T(8,128)(2,1)S(1)} %get-tuple-element.14.send_in), custom_call_target="tpu_custom_call", output_to_operand_aliasing={{1}: (1, {})} | custom-call | bytes 4194304 | tf_op jit(solution)/shard_map/pallas_call | solution.py:550
  66.0 0.0 copy-start.1
  66.0 31.0 %all_to_all.15 = bf16[128,48,128]{2,1,0:T(8,128)(2,1)S(1)} all-to-all(bf16[128,48,128]{2,1,0:T(8,128)(2,1)S(1)} %get-tuple-element.17), channel_id=1, replica_groups=mesh['dp'=8,'cent'=16] {'dp','cent'}, dimensions={0} | all-to-all | bytes 3145728 | tf_op jit(solution)/shard_map/all_to_all | solution.py:453
  97.0 0.0 copy-done.1
  97.0 1.4 %shard_map.89 = (bf16[256,1024]{1,0:T(8,128)(2,1)}, f32[256,1024]{1,0:T(8,128)}) custom-call(bf16[256,512]{1,0:T(8,128)(2,1)S(1)} %copy-done.1, bf16[8,16,48,128]{3,2,1,0:T(8,128)(2,1)S(1)} %bitcast.7), custom_call_target="tpu_custom_call" | custom-call | flops 268435456 | bytes 4194304 | tf_op jit(solution)/shard_map/pallas_call | solution.py:564
  (3 shorter events, 0.0 us)
Async XLA Ops:
  0.6 14.7 %copy-start.3 = (s32[4096]{0:T(1024)S(1)}, s32[4096]{0:T(1024)}, u32[]{:S(2)}) copy-start(s32[4096]{0:T(1024)} %param.7) | copy-start | bytes 49156
  3.8 32.9 %all-to-all-start = ((bf16[128,40,128]{2,1,0:T(8,128)(2,1)}), bf16[128,40,128]{2,1,0:T(8,128)(2,1)S(1)}, u32[]{:S(2)}, u32[]{:S(2)}) async-start(bf16[128,40,128]{2,1,0:T(8,128)(2,1)} %bitcast.9), calls=%async_computation | async-start | bytes 2621440 | tf_op jit(solution)/shard_map/all_to_all | solution.py:453
  15.7 21.0 %copy-start.2 = (s32[4096]{0:T(1024)S(1)}, s32[4096]{0:T(1024)}, u32[]{:S(2)}) copy-start(s32[4096]{0:T(1024)} %param.8) | copy-start | bytes 49156
  42.7 20.7 %all-to-all-start.1 = ((bf16[16,35,8,128]{3,2,1,0:T(8,128)(2,1)}), bf16[16,35,8,128]{3,2,1,0:T(8,128)(2,1)}, u32[]{:S(2)}, u32[]{:S(2)}) async-start(bf16[16,35,8,128]{3,2,1,0:T(8,128)(2,1)} %shard_map.87), calls=%async_computation.1 | async-start | bytes 2293760 | tf_op jit(solution)/shard_map/all_to_all | solution.py:453
  47.3 1.2 %copy-start = (bf16[4096,128]{1,0:T(8,128)(2,1)S(1)}, bf16[4096,128]{1,0:T(8,128)(2,1)}, u32[]{:S(2)}) copy-start(bf16[4096,128]{1,0:T(8,128)(2,1)} %old_ref.1) | copy-start | bytes 3145732
  66.0 31.0 %copy-start.1 = (bf16[256,512]{1,0:T(8,128)(2,1)S(1)}, bf16[256,512]{1,0:T(8,128)(2,1)}, u32[]{:S(2)}) copy-start(bf16[256,512]{1,0:T(8,128)(2,1)} %get-tuple-element.16.back_ref) | copy-start | bytes 786436

commit v8 on v7

--- a/solution.py
+++ b/solution.py
@@ -402,7 +402,6 @@
     total = parts_ref[0].astype(F32)
     for source in range(1, parts_ref.shape[0]):
         total += parts_ref[source].astype(F32)
-    total = total.reshape(-1, LANES)
     tail = total[272:280].T
     me = lax.axis_index("cent")
     chosen = jnp.where(me < 8, tail[:, 4:5] + tail[:, 6:7], tail[:, 5:6] + tail[:, 7:8])
@@ -559,7 +558,7 @@
             pltpu.SemaphoreType.DMA(()),
         ],
         alias={1: 1},
-    )(shares, answer)
+    )(shares.reshape(owners, -1, lanes), answer)
     returned = swap(answer, BOTH)
     residual, level_three = call(
         unpack_kernel,

time: 99 us -> 99.6 us (level)
  no operation moved by 1% of the time
where the time goes in v8:
time: 99.6 us; the launch traced here: 98.9 us
  Pallas kernels  30.6 us (31%)
  blocking collectives  30.5 us (31%)
  waiting for transfers between devices  18.8 us (19%)
  starting transfers between devices  16.4 us (16%)
  local copies, waits for them, and re-layouts  1.55 us (2%)
    all_to_all x1, blocking collectives, swap(): return lax.all_to_all(value, axes, split_axis=0, concat_axis=0, tiled=True)  30.5 us
    all_to_all x2, waiting for transfers between devices, swap(): return lax.all_to_all(value, axes, split_axis=0, concat_axis=0, tiled=True)  18.8 us
    all_to_all x2, starting transfers between devices, swap(): return lax.all_to_all(value, axes, split_axis=0, concat_axis=0, tiled=True)  16.4 us
    pallas_call x1, Pallas kernels, on_device(): call(parent_kernel, shape((SPARE, *total_dims), F32), [VMEM, VMEM], HBM,...  9.31 us
    pallas_call x1, Pallas kernels, on_device(): call(level_kernel, (shape((block, lanes), F32), shape((devices, CAP + TOP...  8.12 us
    pallas_call x1, Pallas kernels, on_device(): call(upper_kernel, shape((owners, 35, 8, lanes), BF16), [VMEM, VMEM, VMEM...  6 us
    pallas_call x1, Pallas kernels, on_device(): call(pack_kernel, (shape((groups, owners, rows, lanes), BF16), shape((cou...  3.19 us
    pallas_call x1, Pallas kernels, on_device(): call(finish_kernel, (shape((256, lanes), F32), shape((devices, CAP + TOP,...  2.54 us
  transfers between devices with their start and end apart: 2, of which 2 were waited for; matrix products, arithmetic and copies ran while one was open for 0% of the time, Pallas kernels for 18%

profile of v8, /device:TPU:1, one launch (start us, length us, event | category | flops | bytes accessed | tf_op | source)
XLA Modules:
  0.0 98.9 jit_solution(15310176396123139079)
XLA Ops:
  0.6 0.0 copy-start.3
  0.6 3.2 %shard_map.84 = (bf16[8,16,40,128]{3,2,1,0:T(8,128)(2,1)}, bf16[256,512]{1,0:T(8,128)(2,1)}) custom-call(s32[1,256]{1,0:T(1,128)} %bitcast.14, bf16[256,1024]{1,0:T(8,128)(2,1)} %points_hbm.1), custom_call_target="tpu_custom_call" | custom-call | flops 268435456 | bytes 4194304 | tf_op jit(solution)/shard_map/pallas_call | solution.py:466
  3.8 11.5 %all-to-all-start = ((bf16[128,40,128]{2,1,0:T(8,128)(2,1)}), bf16[128,40,128]{2,1,0:T(8,128)(2,1)S(1)}, u32[]{:S(2)}, u32[]{:S(2)}) async-start(bf16[128,40,128]{2,1,0:T(8,128)(2,1)} %bitcast.10), calls=%async_computation | async-start | bytes 2621440 | tf_op jit(solution)/shard_map/all_to_all | solution.py:452
  15.4 0.0 copy-done.3
  15.4 0.1 shift_right_logical.14
  15.5 0.1 copy.10
  15.5 0.1 and.14
  15.6 0.1 copy.11
  15.7 0.0 copy-start.2
  15.8 9.3 %shard_map.86.start_hbm = f32[12,512,1152]{2,1,0:T(8,128)} custom-call(s32[32,128]{1,0:T(8,128)} %bitcast.13, bf16[4096,128]{1,0:T(8,128)(2,1)} %old_ref.1), custom_call_target="tpu_custom_call" | custom-call | flops 4831838208 | bytes 4194304 | tf_op jit(solution)/shard_map/pallas_call | solution.py:483
  25.1 11.6 %all-to-all-done.slab_ref = bf16[128,40,128]{2,1,0:T(8,128)(2,1)S(1)} async-done(((bf16[128,40,128]{2,1,0:T(8,128)(2,1)}), bf16[128,40,128]{2,1,0:T(8,128)(2,1)S(1)}, u32[]{:S(2)}, u32[]{:S(2)}) %all-to-all-start) | async-done | bytes 1310752 | tf_op jit(solution)/shard_map/all_to_all | solution.py:452
  36.7 0.0 copy-done.2
  36.7 6.0 %shard_map.87 = bf16[16,35,8,128]{3,2,1,0:T(8,128)(2,1)} custom-call(bf16[128,40,128]{2,1,0:T(8,128)(2,1)S(1)} %all-to-all-done.slab_ref, bf16[128,128]{1,0:T(8,128)(2,1)S(1)} %pad.5.table_ref, s32[32,128]{1,0:T(8,128)S(1)} %bitcast.9, f32[12,512,1152]{2,1,0:T(8,128)} %shard_map.86.start_hbm), custom_call_target="tpu_custom_call" | custom-call | flops 4831838208 | bytes 4194304 | tf_op jit(solution)/shard_map/pallas_call | solution.py:502
  42.7 4.9 %all-to-all-start.1 = ((bf16[16,35,8,128]{3,2,1,0:T(8,128)(2,1)}), bf16[16,35,8,128]{3,2,1,0:T(8,128)(2,1)}, u32[]{:S(2)}, u32[]{:S(2)}) async-start(bf16[16,35,8,128]{3,2,1,0:T(8,128)(2,1)} %shard_map.87), calls=%async_computation.1 | async-start | bytes 2293760 | tf_op jit(solution)/shard_map/all_to_all | solution.py:452
  47.6 0.0 copy-start
  47.7 1.2 %copy-done = bf16[4096,128]{1,0:T(8,128)(2,1)S(1)} copy-done((bf16[4096,128]{1,0:T(8,128)(2,1)S(1)}, bf16[4096,128]{1,0:T(8,128)(2,1)}, u32[]{:S(2)}) %copy-start) | copy-done | bytes 1048600
  48.9 8.1 %shard_map.85 = (f32[4096,128]{1,0:T(8,128)}, bf16[128,48,128]{2,1,0:T(8,128)(2,1)S(1)}) custom-call(bf16[128,40,128]{2,1,0:T(8,128)(2,1)S(1)} %all-to-all-done.slab_ref, bf16[4096,128]{1,0:T(8,128)(2,1)S(1)} %copy-done), custom_call_target="tpu_custom_call" | custom-call | flops 9663676416 | bytes 4194304 | tf_op jit(solution)/shard_map/pallas_call | solution.py:525
  57.0 7.2 %all-to-all-done.1 = bf16[16,35,8,128]{3,2,1,0:T(8,128)(2,1)} async-done(((bf16[16,35,8,128]{3,2,1,0:T(8,128)(2,1)}), bf16[16,35,8,128]{3,2,1,0:T(8,128)(2,1)}, u32[]{:S(2)}, u32[]{:S(2)}) %all-to-all-start.1) | async-done | bytes 1146912 | tf_op jit(solution)/shard_map/all_to_all | solution.py:452
  64.2 2.5 %shard_map.88 = (f32[256,128]{1,0:T(8,128)}, bf16[128,48,128]{2,1,0:T(8,128)(2,1)S(1)}) custom-call(bf16[16,280,128]{2,1,0:T(8,128)(2,1)} %bitcast.6.parts_ref, bf16[128,48,128]{2,1,0:T(8,128)(2,1)S(1)} %get-tuple-element.14.send_in), custom_call_target="tpu_custom_call", output_to_operand_aliasing={{1}: (1, {})} | custom-call | bytes 4194304 | tf_op jit(solution)/shard_map/pallas_call | solution.py:549
  66.7 0.0 copy-start.1
  66.7 30.5 %all_to_all.15 = bf16[128,48,128]{2,1,0:T(8,128)(2,1)S(1)} all-to-all(bf16[128,48,128]{2,1,0:T(8,128)(2,1)S(1)} %get-tuple-element.17), channel_id=1, replica_groups=mesh['dp'=8,'cent'=16] {'dp','cent'}, dimensions={0} | all-to-all | bytes 3145728 | tf_op jit(solution)/shard_map/all_to_all | solution.py:452
  97.3 0.0 copy-done.1
  97.3 1.4 %shard_map.89 = (bf16[256,1024]{1,0:T(8,128)(2,1)}, f32[256,1024]{1,0:T(8,128)}) custom-call(bf16[256,512]{1,0:T(8,128)(2,1)S(1)} %copy-done.1, bf16[8,16,48,128]{3,2,1,0:T(8,128)(2,1)S(1)} %bitcast.8), custom_call_target="tpu_custom_call" | custom-call | flops 268435456 | bytes 4194304 | tf_op jit(solution)/shard_map/pallas_call | solution.py:563
  (3 shorter events, 0.0 us)
Async XLA Ops:
  0.6 14.7 %copy-start.3 = (s32[4096]{0:T(1024)S(1)}, s32[4096]{0:T(1024)}, u32[]{:S(2)}) copy-start(s32[4096]{0:T(1024)} %param.7) | copy-start | bytes 49156
  3.8 32.9 %all-to-all-start = ((bf16[128,40,128]{2,1,0:T(8,128)(2,1)}), bf16[128,40,128]{2,1,0:T(8,128)(2,1)S(1)}, u32[]{:S(2)}, u32[]{:S(2)}) async-start(bf16[128,40,128]{2,1,0:T(8,128)(2,1)} %bitcast.10), calls=%async_computation | async-start | bytes 2621440 | tf_op jit(solution)/shard_map/all_to_all | solution.py:452
  15.7 21.0 %copy-start.2 = (s32[4096]{0:T(1024)S(1)}, s32[4096]{0:T(1024)}, u32[]{:S(2)}) copy-start(s32[4096]{0:T(1024)} %param.8) | copy-start | bytes 49156
  42.7 21.5 %all-to-all-start.1 = ((bf16[16,35,8,128]{3,2,1,0:T(8,128)(2,1)}), bf16[16,35,8,128]{3,2,1,0:T(8,128)(2,1)}, u32[]{:S(2)}, u32[]{:S(2)}) async-start(bf16[16,35,8,128]{3,2,1,0:T(8,128)(2,1)} %shard_map.87), calls=%async_computation.1 | async-start | bytes 2293760 | tf_op jit(solution)/shard_map/all_to_all | solution.py:452
  47.6 1.2 %copy-start = (bf16[4096,128]{1,0:T(8,128)(2,1)S(1)}, bf16[4096,128]{1,0:T(8,128)(2,1)}, u32[]{:S(2)}) copy-start(bf16[4096,128]{1,0:T(8,128)(2,1)} %old_ref.1) | copy-start | bytes 3145732
  66.7 30.5 %copy-start.1 = (bf16[256,512]{1,0:T(8,128)(2,1)S(1)}, bf16[256,512]{1,0:T(8,128)(2,1)}, u32[]{:S(2)}) copy-start(bf16[256,512]{1,0:T(8,128)(2,1)} %get-tuple-element.16.back_ref) | copy-start | bytes 786436

commit v9 on v8

--- a/solution.py
+++ b/solution.py
@@ -359,30 +359,31 @@
 
     for step in range(4):
         sources = lane_slice(step, 32)
-        residual_ref[sources, 0:HALF, :] = subtract(
+        residual_ref[sources, 0 : HALF // 8] = subtract(
             4 * step, 4, lower_rows(slab_ref, step)
-        ).reshape(32, HALF, LANES)
-        part = (sources, slice(0, HALF))
+        ).reshape(32, HALF // 8, 8, LANES)
+        part = (sources, slice(0, HALF // 8))
         stores.append(
             pltpu.make_async_copy(residual_ref.at[part], residual_hbm.at[part], low_sems.at[step])
         )
         stores[-1].start()
 
     def upper_copy(group):
-        part = (pl.ds(group * 16, 16), pl.ds(HALF, HALF))
+        part = (pl.ds(group * 16, 16), pl.ds(HALF // 8, HALF // 8))
         return pltpu.make_async_copy(residual_ref.at[part], residual_hbm.at[part], up_sems.at[group])
 
     def finish(group, carry):
         sources = pl.ds(group * 16, 16)
         @pl.when(live_ref[group] > 0)
         def _():
-            residual_ref[sources, HALF:CAP, :] = subtract(
+            residual_ref[sources, HALF // 8 : CAP // 8] = subtract(
                 16 + 2 * group, 2, upper_rows(slab_ref, group)
-            ).reshape(16, HALF, LANES)
+            ).reshape(16, HALF // 8, 8, LANES)
 
         @pl.when(live_ref[group] == 0)
         def _():
-            residual_ref[sources, HALF:CAP, :] = slab_ref[sources, HALF:CAP, :]
+            empty = slab_ref[sources, HALF:CAP, :]
+            residual_ref[sources, HALF // 8 : CAP // 8] = empty.reshape(16, HALF // 8, 8, LANES)
 
         upper_copy(group).start()
         return carry
@@ -404,12 +405,16 @@
         total += parts_ref[source].astype(F32)
     tail = total[272:280].T
     me = lax.axis_index("cent")
+    owners = parts_ref.shape[0]
     chosen = jnp.where(me < 8, tail[:, 4:5] + tail[:, 6:7], tail[:, 5:6] + tail[:, 7:8])
     column_ref[...] = jnp.broadcast_to(chosen, (LANES, LANES))
     weight = column_ref[pl.ds(pl.multiple_of((me % 8) * TOP, TOP), TOP), :]
     top = (total[256:272] / weight).astype(BF16)
-    top_ref[...] = jnp.broadcast_to(top[None], top_ref.shape)
-    store = pltpu.make_async_copy(top_ref, send_hbm.at[:, pl.ds(CAP, TOP), :], sem)
+    for group in range(top_ref.shape[0] // owners):
+        first = group % 2 * (TOP // 2)
+        part = jnp.broadcast_to(top[first : first + TOP // 2][None, None], (owners, 1, TOP // 2, LANES))
+        top_ref[group * owners : (group + 1) * owners] = part
+    store = pltpu.make_async_copy(top_ref, send_hbm.at[:, pl.ds(CAP // 8, 1)], sem)
     store.start()
     for half in range(2):
         weight = tail[:, half : half + 1] + tail[:, half + 2 : half + 3]
@@ -420,11 +425,12 @@
 
 def unpack_kernel(back_ref, returned_ref, residual_hbm, level_hbm, residual_ref, level_ref, sems):
     groups, owners, rows, lanes = returned_ref.shape
+    core = lax.axis_index("dp") % 2
     stores = []
     for pair in range(groups // 2):
         for side in range(2):
             top = returned_ref[2 * pair + side, :, CAP:rows, :].astype(F32)
-            level_ref[:, lane_slice(2 * pair + side)] = top.reshape(owners * TOP, lanes)
+            level_ref[:, 0, :, lane_slice(2 * pair + side)] = top
         right = jnp.concatenate(
             [
                 returned_ref[2 * pair + side, :, 0:CAP, :].reshape(owners * CAP, lanes)
@@ -433,15 +439,22 @@
             axis=1,
         )
         at = lane_slice(pair, 2 * lanes)
-        stores.append(pltpu.make_async_copy(level_ref.at[:, at], level_hbm.at[:, at], sems.at[2 * pair]))
+        residual_ref[:, at] = dot(back_ref[...], right).astype(BF16)
+        stores.append(pltpu.make_async_copy(residual_ref.at[:, at], residual_hbm.at[:, at], sems.at[pair]))
         stores[-1].start()
-        residual_ref[:, at] = dot(back_ref[...], right).astype(BF16)
-        stores.append(
-            pltpu.make_async_copy(residual_ref.at[:, at], residual_hbm.at[:, at], sems.at[2 * pair + 1])
-        )
-        stores[-1].start()
+    stores.append(pltpu.make_async_copy(level_ref, level_hbm.at[:, pl.ds(core, 1)], sems.at[groups // 2]))
+    stores[-1].start()
     for store in stores:
         store.wait()
+
+
+def other_kernel(parts_ref, level_in, level_hbm, level_ref, sem):
+    core = lax.axis_index("dp") % 2
+    for group in range(parts_ref.shape[0]):
+        level_ref[:, 0, :, lane_slice(group)] = parts_ref[group].astype(F32)
+    store = pltpu.make_async_copy(level_ref, level_hbm.at[:, pl.ds(1 - core, 1)], sem)
+    store.start()
+    store.wait()
 
 
 def shape(dims, kind):
@@ -461,6 +474,7 @@
     slots = owners * CAP
     rows = CAP + EXTRA
     total_dims = (LOW, (HIGHS + 1) * LANES)
+    answer_dims = (devices, (CAP + TOP // 2) // 8, 8, lanes)
     work = 2 * LOW * block * (HIGHS + 1) * LANES
 
     send, back = call(
@@ -524,7 +538,7 @@
 
     level_one, answer = call(
         level_kernel,
-        (shape((block, lanes), F32), shape((devices, CAP + TOP, lanes), BF16)),
+        (shape((block, lanes), F32), shape(answer_dims, BF16)),
         [VMEM, HBM],
         (HBM, HBM),
         LEVEL,
@@ -536,7 +550,7 @@
             pltpu.VMEM((2048, LANES), I32),
             pltpu.VMEM((block, lanes), BF16),
             pltpu.VMEM((block, lanes), F32),
-            pltpu.VMEM((devices, CAP, lanes), BF16),
+            pltpu.VMEM((devices, CAP // 8, 8, lanes), BF16),
             pltpu.SMEM((groups,), I32),
             pltpu.SemaphoreType.DMA(()),
             pltpu.SemaphoreType.DMA((HIGHS,)),
@@ -548,31 +562,44 @@
 
     level_two, answer = call(
         finish_kernel,
-        (shape((256, lanes), F32), shape((devices, CAP + TOP, lanes), BF16)),
+        (shape((256, lanes), F32), shape(answer_dims, BF16)),
         [VMEM, HBM],
         (VMEM, HBM),
         SMALL,
         [
             pltpu.VMEM((LANES, LANES), F32),
-            pltpu.VMEM((devices, TOP, lanes), BF16),
+            pltpu.VMEM((devices, 1, TOP // 2, lanes), BF16),
             pltpu.SemaphoreType.DMA(()),
         ],
         alias={1: 1},
     )(shares.reshape(owners, -1, lanes), answer)
     returned = swap(answer, BOTH)
+    half = returned[:, CAP // 8]
+    half = lax.ppermute(half, "dp", [(group, group ^ 1) for group in range(groups)])
+    top_dims = (owners, 2, TOP // 2, width)
     residual, level_three = call(
         unpack_kernel,
-        (shape((count, width), BF16), shape((owners * TOP, width), F32)),
+        (shape((count, width), BF16), shape(top_dims, F32)),
         [VMEM, VMEM],
         (HBM, HBM),
         SMALL,
         [
             pltpu.VMEM((count, width), BF16),
-            pltpu.VMEM((owners * TOP, width), F32),
-            pltpu.SemaphoreType.DMA((groups,)),
+            pltpu.VMEM((owners, 1, TOP // 2, width), F32),
+            pltpu.SemaphoreType.DMA((1 + groups // 2,)),
         ],
         flops=2 * slots * count * width,
-    )(back, returned.reshape(groups, owners, CAP + TOP, lanes))
+    )(back, returned.reshape(groups, owners, CAP + TOP // 2, lanes))
+    level_three = call(
+        other_kernel,
+        shape(top_dims, F32),
+        [VMEM, HBM],
+        HBM,
+        SMALL,
+        [pltpu.VMEM((owners, 1, TOP // 2, width), F32), pltpu.SemaphoreType.DMA(())],
+        alias={1: 0},
+    )(half.reshape(groups, owners, TOP // 2, lanes), level_three)
+    level_three = level_three.reshape(owners * TOP, width)
     return (level_one, level_two, level_three, residual)
 
 

time: 99.6 us -> 99.7 us (level)
  Pallas kernels: 30.6 us -> 33.5 us
  blocking collectives: 30.5 us -> 28.3 us
  waiting for transfers between devices: 18.8 us -> 17.1 us
  starting transfers between devices: 16.4 us -> 17.6 us
    all_to_all x1, blocking collectives: 30.5 us -> 28.3 us  [swap(): return lax.all_to_all(value, axes, split_axis=0, concat_axis=0, tiled=True)]
    pallas_call x3 -> x4, Pallas kernels: 12.1 us -> 14.2 us  [the longest x1 9.39 us: on_device(): call(level_kernel, (shape((block, lanes), F32), shape(answer_dims, BF16))...]
    all_to_all x2, waiting for transfers between devices: 18.8 us -> 17.1 us  [swap(): return lax.all_to_all(value, axes, split_axis=0, concat_axis=0, tiled=True)]
    ppermute x0 -> x1, starting transfers between devices: none -> 1.57 us  [on_device(): lax.ppermute(half, 'dp', [(group, group ^ 1) for group in range(groups)])]
  transfers between devices with their start and end apart: 2 -> 3, of which waited for: 2 -> 2; matrix products, arithmetic and copies ran while one was open for 0% -> 0% of each run, Pallas kernels for 18% -> 20%
where the time goes in v9:
time: 99.7 us; the launch traced here: 99.1 us
  Pallas kernels  33.5 us (34%)
  blocking collectives  28.3 us (28%)
  starting transfers between devices  17.6 us (18%)
  waiting for transfers between devices  17.1 us (17%)
  local copies, waits for them, and re-layouts  1.56 us (2%)
    all_to_all x1, blocking collectives, swap(): return lax.all_to_all(value, axes, split_axis=0, concat_axis=0, tiled=True)  28.3 us
    all_to_all x2, waiting for transfers between devices, swap(): return lax.all_to_all(value, axes, split_axis=0, concat_axis=0, tiled=True)  17.1 us
    all_to_all x2, starting transfers between devices, swap(): return lax.all_to_all(value, axes, split_axis=0, concat_axis=0, tiled=True)  16.1 us
    pallas_call x1, Pallas kernels, on_device(): call(level_kernel, (shape((block, lanes), F32), shape(answer_dims, BF16))...  9.39 us
    pallas_call x1, Pallas kernels, on_device(): call(parent_kernel, shape((SPARE, *total_dims), F32), [VMEM, VMEM], HBM,...  9.31 us
    pallas_call x1, Pallas kernels, on_device(): call(upper_kernel, shape((owners, 35, 8, lanes), BF16), [VMEM, VMEM, VMEM...  6.85 us
    pallas_call x1, Pallas kernels, on_device(): call(pack_kernel, (shape((groups, owners, rows, lanes), BF16), shape((cou...  3.19 us
    pallas_call x1, Pallas kernels, on_device(): call(finish_kernel, (shape((256, lanes), F32), shape(answer_dims, BF16)),...  2.54 us
  transfers between devices with their start and end apart: 3, of which 2 were waited for; matrix products, arithmetic and copies ran while one was open for 0% of the time, Pallas kernels for 20%

profile of v9, /device:TPU:1, one launch (start us, length us, event | category | flops | bytes accessed | tf_op | source)
XLA Modules:
  0.0 99.1 jit_solution(4711776636568671955)
XLA Ops:
  0.6 3.2 %shard_map.84 = (bf16[8,16,40,128]{3,2,1,0:T(8,128)(2,1)}, bf16[256,512]{1,0:T(8,128)(2,1)}) custom-call(s32[1,256]{1,0:T(1,128)} %bitcast.20, bf16[256,1024]{1,0:T(8,128)(2,1)} %points_hbm.1), custom_call_target="tpu_custom_call" | custom-call | flops 268435456 | bytes 4194304 | tf_op jit(solution)/shard_map/pallas_call | solution.py:480
  3.8 0.0 copy-start.3
  3.8 11.5 %all-to-all-start = ((bf16[128,40,128]{2,1,0:T(8,128)(2,1)}), bf16[128,40,128]{2,1,0:T(8,128)(2,1)S(1)}, u32[]{:S(2)}, u32[]{:S(2)}) async-start(bf16[128,40,128]{2,1,0:T(8,128)(2,1)} %bitcast.15), calls=%async_computation | async-start | bytes 2621440 | tf_op jit(solution)/shard_map/all_to_all | solution.py:465
  15.4 0.0 copy-done.3
  15.4 0.1 shift_right_logical.14
  15.4 0.1 copy.11
  15.5 0.1 and.14
  15.6 0.1 copy.12
  15.7 0.0 copy-start.2
  15.7 9.3 %shard_map.86.start_hbm = f32[12,512,1152]{2,1,0:T(8,128)} custom-call(s32[32,128]{1,0:T(8,128)} %bitcast.19, bf16[4096,128]{1,0:T(8,128)(2,1)} %old_ref.1), custom_call_target="tpu_custom_call" | custom-call | flops 4831838208 | bytes 4194304 | tf_op jit(solution)/shard_map/pallas_call | solution.py:497
  25.1 11.6 %all-to-all-done.slab_ref = bf16[128,40,128]{2,1,0:T(8,128)(2,1)S(1)} async-done(((bf16[128,40,128]{2,1,0:T(8,128)(2,1)}), bf16[128,40,128]{2,1,0:T(8,128)(2,1)S(1)}, u32[]{:S(2)}, u32[]{:S(2)}) %all-to-all-start) | async-done | bytes 1310752 | tf_op jit(solution)/shard_map/all_to_all | solution.py:465
  36.7 0.0 copy-done.2
  36.7 6.8 %shard_map.87 = bf16[16,35,8,128]{3,2,1,0:T(8,128)(2,1)} custom-call(bf16[128,40,128]{2,1,0:T(8,128)(2,1)S(1)} %all-to-all-done.slab_ref, bf16[128,128]{1,0:T(8,128)(2,1)S(1)} %pad.5.table_ref, s32[32,128]{1,0:T(8,128)S(1)} %bitcast.14, f32[12,512,1152]{2,1,0:T(8,128)} %shard_map.86.start_hbm), custom_call_target="tpu_custom_call" | custom-call | flops 4831838208 | bytes 4194304 | tf_op jit(solution)/shard_map/pallas_call | solution.py:516
  43.6 4.6 %all-to-all-start.1 = ((bf16[16,35,8,128]{3,2,1,0:T(8,128)(2,1)}), bf16[16,35,8,128]{3,2,1,0:T(8,128)(2,1)}, u32[]{:S(2)}, u32[]{:S(2)}) async-start(bf16[16,35,8,128]{3,2,1,0:T(8,128)(2,1)} %shard_map.87), calls=%async_computation.1 | async-start | bytes 2293760 | tf_op jit(solution)/shard_map/all_to_all | solution.py:465
  48.1 0.0 copy-start
  48.1 1.2 %copy-done = bf16[4096,128]{1,0:T(8,128)(2,1)S(1)} copy-done((bf16[4096,128]{1,0:T(8,128)(2,1)S(1)}, bf16[4096,128]{1,0:T(8,128)(2,1)}, u32[]{:S(2)}) %copy-start) | copy-done | bytes 1048600
  49.4 9.4 %shard_map.85 = (f32[4096,128]{1,0:T(8,128)}, bf16[128,5,8,128]{3,2,1,0:T(8,128)(2,1)S(1)}) custom-call(bf16[128,40,128]{2,1,0:T(8,128)(2,1)S(1)} %all-to-all-done.slab_ref, bf16[4096,128]{1,0:T(8,128)(2,1)S(1)} %copy-done), custom_call_target="tpu_custom_call" | custom-call | flops 9663676416 | bytes 4194304 | tf_op jit(solution)/shard_map/pallas_call | solution.py:539
  58.8 5.5 %all-to-all-done.1 = bf16[16,35,8,128]{3,2,1,0:T(8,128)(2,1)} async-done(((bf16[16,35,8,128]{3,2,1,0:T(8,128)(2,1)}), bf16[16,35,8,128]{3,2,1,0:T(8,128)(2,1)}, u32[]{:S(2)}, u32[]{:S(2)}) %all-to-all-start.1) | async-done | bytes 1146912 | tf_op jit(solution)/shard_map/all_to_all | solution.py:465
  64.2 2.5 %shard_map.88 = (f32[256,128]{1,0:T(8,128)}, bf16[128,5,8,128]{3,2,1,0:T(8,128)(2,1)S(1)}) custom-call(bf16[16,280,128]{2,1,0:T(8,128)(2,1)} %bitcast.6.parts_ref, bf16[128,5,8,128]{3,2,1,0:T(8,128)(2,1)S(1)} %get-tuple-element.14.send_in), custom_call_target="tpu_custom_call", output_to_operand_aliasing={{1}: (1, {})} | custom-call | bytes 4194304 | tf_op jit(solution)/shard_map/pallas_call | solution.py:563
  66.8 0.0 copy-start.1
  66.8 28.3 %all_to_all.15 = bf16[128,5,8,128]{3,2,1,0:T(8,128)(2,1)S(1)} all-to-all(bf16[128,5,8,128]{3,2,1,0:T(8,128)(2,1)S(1)} %get-tuple-element.16), channel_id=1, replica_groups=mesh['dp'=8,'cent'=16] {'dp','cent'}, dimensions={0} | all-to-all | bytes 2621440 | tf_op jit(solution)/shard_map/all_to_all | solution.py:465
  95.1 1.6 %collective-permute-start = (bf16[128,8,128]{2,1,0:T(8,128)(2,1)S(1)}, bf16[128,8,128]{2,1,0:T(8,128)(2,1)S(1)}, u32[]{:S(2)}, u32[]{:S(2)}) collective-permute-start(bf16[128,8,128]{2,1,0:T(8,128)(2,1)S(1)} %slice_bitcast_fusion), channel_id=1, source_target_pairs={{0,16},{16,0},{32,48},{48,32},{64,80},{80,64},{96,112},{112,96},{1... | collective-permute-start | bytes 786440 | tf_op jit(solution)/shard_map/ppermute | solution.py:578
  96.7 0.0 copy-done.1
  96.7 1.4 %shard_map.89 = (bf16[256,1024]{1,0:T(8,128)(2,1)}, f32[16,2,8,1024]{3,2,1,0:T(8,128)}) custom-call(bf16[256,512]{1,0:T(8,128)(2,1)S(1)} %copy-done.1, bf16[8,16,40,128]{3,2,1,0:T(8,128)(2,1)S(1)} %bitcast.12), custom_call_target="tpu_custom_call" | custom-call | flops 268435456 | bytes 4194304 | tf_op jit(solution)/shard_map/pallas_call | solution.py:580
  98.1 0.0 collective-permute-done
  98.1 0.9 shard_map.90
  (4 shorter events, 0.1 us)
Async XLA Ops:
  3.8 11.5 %copy-start.3 = (s32[4096]{0:T(1024)S(1)}, s32[4096]{0:T(1024)}, u32[]{:S(2)}) copy-start(s32[4096]{0:T(1024)} %param.7) | copy-start | bytes 49156
  3.8 32.9 %all-to-all-start = ((bf16[128,40,128]{2,1,0:T(8,128)(2,1)}), bf16[128,40,128]{2,1,0:T(8,128)(2,1)S(1)}, u32[]{:S(2)}, u32[]{:S(2)}) async-start(bf16[128,40,128]{2,1,0:T(8,128)(2,1)} %bitcast.15), calls=%async_computation | async-start | bytes 2621440 | tf_op jit(solution)/shard_map/all_to_all | solution.py:465
  15.7 21.0 %copy-start.2 = (s32[4096]{0:T(1024)S(1)}, s32[4096]{0:T(1024)}, u32[]{:S(2)}) copy-start(s32[4096]{0:T(1024)} %param.8) | copy-start | bytes 49156
  43.6 20.7 %all-to-all-start.1 = ((bf16[16,35,8,128]{3,2,1,0:T(8,128)(2,1)}), bf16[16,35,8,128]{3,2,1,0:T(8,128)(2,1)}, u32[]{:S(2)}, u32[]{:S(2)}) async-start(bf16[16,35,8,128]{3,2,1,0:T(8,128)(2,1)} %shard_map.87), calls=%async_computation.1 | async-start | bytes 2293760 | tf_op jit(solution)/shard_map/all_to_all | solution.py:465
  48.1 1.2 %copy-start = (bf16[4096,128]{1,0:T(8,128)(2,1)S(1)}, bf16[4096,128]{1,0:T(8,128)(2,1)}, u32[]{:S(2)}) copy-start(bf16[4096,128]{1,0:T(8,128)(2,1)} %old_ref.1) | copy-start | bytes 3145732
  66.8 29.9 %copy-start.1 = (bf16[256,512]{1,0:T(8,128)(2,1)S(1)}, bf16[256,512]{1,0:T(8,128)(2,1)}, u32[]{:S(2)}) copy-start(bf16[256,512]{1,0:T(8,128)(2,1)} %get-tuple-element.17.back_ref) | copy-start | bytes 786436
  95.1 3.0 %collective-permute-start = (bf16[128,8,128]{2,1,0:T(8,128)(2,1)S(1)}, bf16[128,8,128]{2,1,0:T(8,128)(2,1)S(1)}, u32[]{:S(2)}, u32[]{:S(2)}) collective-permute-start(bf16[128,8,128]{2,1,0:T(8,128)(2,1)S(1)} %slice_bitcast_fusion), channel_id=1, source_target_pairs={{0,16},{16,0},{32,48},{48,32},{64,80},{80,64},{96,112},{112,96},{1... | collective-permute-start | bytes 786440 | tf_op jit(solution)/shard_map/ppermute | solution.py:578

commit v10 on v9

--- a/solution.py
+++ b/solution.py
@@ -39,10 +39,9 @@
 
 
 FULL = 62_900_000
-UPPER = 50_000_000
+UPPER = 48_000_000
 LEVEL = 48_000_000
 SMALL = 16_000_000
-SPARE = 12
 
 
 def call(body, out_shape, ins, outs, vmem, scratch=(), flops=0, size=4 << 20, alias=None):
@@ -220,7 +219,7 @@
         digits_ref,
         old_ref.shape[0] // 512,
     )
-    store = pltpu.make_async_copy(total_ref, total_hbm.at[0], sem)
+    store = pltpu.make_async_copy(total_ref, total_hbm, sem)
     store.start()
     store.wait()
 
@@ -237,12 +236,14 @@
 
 
 def upper_kernel(
-    slab_ref, table_ref, top_ref, start_hbm, send_hbm,
+    slab_ref, table_ref, top_ref, start_hbm, send_hbm, slab_hbm,
     digits_ref, parents_ref, total_ref, left_ref, high_ref, start_ref, send_ref, right_ref, tail_ref, live_ref,
     sems,
 ):
-    load = pltpu.make_async_copy(start_hbm.at[0], start_ref, sems.at[0])
+    load = pltpu.make_async_copy(start_hbm, start_ref, sems.at[0])
     load.start()
+    keep = pltpu.make_async_copy(slab_ref, slab_hbm, sems.at[2 + HIGHS])
+    keep.start()
     slot_digits(slab_ref, digits_ref)
     mark_live(digits_ref, live_ref)
     for step in range(4):
@@ -267,7 +268,7 @@
     diagonal = jnp.where(iota((16, LANES), 0) == iota((16, LANES), 1), 1.0, 0.0).astype(BF16)
     across = dot_nt(diagonal, split.astype(BF16))
     tops = []
-    stores = []
+    stores = [keep]
     for high in range(HIGHS):
         mass = (total_ref[:, lane_slice(high)] + start_ref[:, lane_slice(high)]).astype(BF16)
         for half in range(2):
@@ -306,12 +307,15 @@
 
 
 def level_kernel(
-    slab_ref, old_hbm, level_hbm, residual_hbm,
-    digits_ref, total_ref, table_ref, left_ref, high_ref, old_ref, level_ref, residual_ref, live_ref,
-    load_sem, level_sems, low_sems, up_sems,
+    slab_hbm, old_hbm, level_hbm, residual_hbm,
+    slab_ref, digits_ref, total_ref, table_ref, left_ref, high_ref, old_ref, level_ref, residual_ref, live_ref,
+    load_sem, slab_sem, level_sems, low_sems, up_sems,
 ):
+    fetch = pltpu.make_async_copy(slab_hbm, slab_ref, slab_sem)
+    fetch.start()
     load = pltpu.make_async_copy(old_hbm, old_ref, load_sem)
     load.start()
+    fetch.wait()
     slot_digits(slab_ref, digits_ref)
     mark_live(digits_ref, live_ref)
     segments(total_ref, left_ref, high_ref, lambda step: lower_rows(slab_ref, step), digits_ref, 4)
@@ -461,6 +465,10 @@
     return jax.ShapeDtypeStruct(dims, kind)
 
 
+def in_hbm(value):
+    return pltpu.with_memory_space_constraint(value, pltpu.HBM)
+
+
 def swap(value, axes):
     return lax.all_to_all(value, axes, split_axis=0, concat_axis=0, tiled=True)
 
@@ -496,7 +504,7 @@
 
     start = call(
         parent_kernel,
-        shape((SPARE, *total_dims), F32),
+        pltpu.HBM(total_dims, F32),
         [VMEM, VMEM],
         HBM,
         FULL,
@@ -513,11 +521,11 @@
     table = jnp.concatenate([lax.shift_right_logical(grid, 6), grid & 63], axis=0) + 1
     table = jnp.pad(table, ((0, 0), (0, 64))).astype(BF16)
 
-    share = call(
+    share, slab_kept = call(
         upper_kernel,
-        shape((owners, 35, 8, lanes), BF16),
+        (pltpu.HBM((owners, 35, 8, lanes), BF16), pltpu.HBM((devices, rows, lanes), BF16)),
         [VMEM, VMEM, VMEM, HBM],
-        HBM,
+        (HBM, HBM),
         UPPER,
         [
             pltpu.VMEM((64, LANES), F32),
@@ -530,19 +538,20 @@
             pltpu.VMEM((HIGHS * LOW, 2 * LANES), BF16),
             pltpu.VMEM((owners, 8, lanes), F32),
             pltpu.SMEM((groups,), I32),
-            pltpu.SemaphoreType.DMA((2 + HIGHS,)),
+            pltpu.SemaphoreType.DMA((3 + HIGHS,)),
         ],
         flops=work,
-    )(slab, table, parent_two.reshape(-1, LANES), start)
+    )(slab, table, parent_two.reshape(-1, LANES), in_hbm(start))
     shares = swap(share, "cent")
 
     level_one, answer = call(
         level_kernel,
         (shape((block, lanes), F32), shape(answer_dims, BF16)),
-        [VMEM, HBM],
+        [HBM, HBM],
         (HBM, HBM),
         LEVEL,
         [
+            pltpu.VMEM((devices, rows, lanes), BF16),
             pltpu.VMEM((64, LANES), F32),
             pltpu.VMEM(total_dims, F32),
             pltpu.VMEM((LOW, HIGHS * LANES), BF16),
@@ -553,12 +562,13 @@
             pltpu.VMEM((devices, CAP // 8, 8, lanes), BF16),
             pltpu.SMEM((groups,), I32),
             pltpu.SemaphoreType.DMA(()),
+            pltpu.SemaphoreType.DMA(()),
             pltpu.SemaphoreType.DMA((HIGHS,)),
             pltpu.SemaphoreType.DMA((4,)),
             pltpu.SemaphoreType.DMA((groups,)),
         ],
         flops=2 * work,
-    )(slab, old_level_one)
+    )(in_hbm(slab_kept), in_hbm(old_level_one))
 
     level_two, answer = call(
         finish_kernel,

time: 99.7 us -> 98.4 us (0.987)
  local copies, waits for them, and re-layouts: 1.56 us -> 0.34 us
    pallas_call x1, Pallas kernels: 9.39 us -> 10.7 us  [on_device(): call(level_kernel, (shape((block, lanes), F32), shape(answer_dims, BF16))...]
    pallas_call x1, Pallas kernels: 2.54 us -> 1.28 us  [on_device(): call(finish_kernel, (shape((256, lanes), F32), shape(answer_dims, BF16)),...]
    unnamed x8 -> x6, local copies, waits for them, and re-layouts: 1.24 us -> 0.02 us
  transfers between devices with their start and end apart: 3 -> 3, of which waited for: 2 -> 2; matrix products, arithmetic and copies ran while one was open for 0% -> 0% of each run, Pallas kernels for 20% -> 22%
where the time goes in v10:
time: 98.4 us; the launch traced here: 97.2 us
  Pallas kernels  33.6 us (34%)
  blocking collectives  28.3 us (29%)
  starting transfers between devices  17 us (17%)
  waiting for transfers between devices  17 us (17%)
    all_to_all x1, blocking collectives, swap(): return lax.all_to_all(value, axes, split_axis=0, concat_axis=0, tiled=True)  28.3 us
    all_to_all x2, waiting for transfers between devices, swap(): return lax.all_to_all(value, axes, split_axis=0, concat_axis=0, tiled=True)  17 us
    all_to_all x2, starting transfers between devices, swap(): return lax.all_to_all(value, axes, split_axis=0, concat_axis=0, tiled=True)  15.4 us
    pallas_call x1, Pallas kernels, on_device(): call(level_kernel, (shape((block, lanes), F32), shape(answer_dims, BF16))...  10.7 us
    pallas_call x1, Pallas kernels, on_device(): call(parent_kernel, pltpu.HBM(total_dims, F32), [VMEM, VMEM], HBM, FULL,...  9.31 us
    pallas_call x1, Pallas kernels, on_device(): call(upper_kernel, (pltpu.HBM((owners, 35, 8, lanes), BF16), pltpu.HBM((d...  6.88 us
    pallas_call x1, Pallas kernels, on_device(): call(pack_kernel, (shape((groups, owners, rows, lanes), BF16), shape((cou...  3.19 us
  transfers between devices with their start and end apart: 3, of which 2 were waited for; matrix products, arithmetic and copies ran while one was open for 0% of the time, Pallas kernels for 22%

profile of v10, /device:TPU:1, one launch (start us, length us, event | category | flops | bytes accessed | tf_op | source)
XLA Modules:
  0.0 97.2 jit_solution(17868895102075141519)
XLA Ops:
  0.6 3.2 %shard_map.84 = (bf16[8,16,40,128]{3,2,1,0:T(8,128)(2,1)}, bf16[256,512]{1,0:T(8,128)(2,1)}) custom-call(s32[1,256]{1,0:T(1,128)} %bitcast.21, bf16[256,1024]{1,0:T(8,128)(2,1)} %points_hbm.1), custom_call_target="tpu_custom_call" | custom-call | flops 268435456 | bytes 4194304 | tf_op jit(solution)/shard_map/pallas_call | solution.py:488
  3.8 0.0 copy-start.2
  3.8 11.5 %all-to-all-start = ((bf16[128,40,128]{2,1,0:T(8,128)(2,1)}), bf16[128,40,128]{2,1,0:T(8,128)(2,1)S(1)}, u32[]{:S(2)}, u32[]{:S(2)}) async-start(bf16[128,40,128]{2,1,0:T(8,128)(2,1)} %bitcast.16), calls=%async_computation | async-start | bytes 2621440 | tf_op jit(solution)/shard_map/all_to_all | solution.py:473
  15.4 0.0 copy-done.2
  15.4 0.1 shift_right_logical.14
  15.4 0.1 copy.11
  15.5 0.1 and.14
  15.6 0.1 copy.12
  15.7 0.0 copy-start.1
  15.7 9.3 %shard_map.85.start_hbm = f32[512,1152]{1,0:T(8,128)} custom-call(s32[32,128]{1,0:T(8,128)} %bitcast.20, bf16[4096,128]{1,0:T(8,128)(2,1)} %old_hbm.1), custom_call_target="tpu_custom_call" | custom-call | flops 4831838208 | bytes 4194304 | tf_op jit(solution)/shard_map/pallas_call | solution.py:505
  25.1 11.6 %all-to-all-done.slab_ref = bf16[128,40,128]{2,1,0:T(8,128)(2,1)S(1)} async-done(((bf16[128,40,128]{2,1,0:T(8,128)(2,1)}), bf16[128,40,128]{2,1,0:T(8,128)(2,1)S(1)}, u32[]{:S(2)}, u32[]{:S(2)}) %all-to-all-start) | async-done | bytes 1310752 | tf_op jit(solution)/shard_map/all_to_all | solution.py:473
  36.7 0.0 copy-done.1
  36.7 6.9 %shard_map.86 = (bf16[16,35,8,128]{3,2,1,0:T(8,128)(2,1)}, bf16[128,40,128]{2,1,0:T(8,128)(2,1)}) custom-call(bf16[128,40,128]{2,1,0:T(8,128)(2,1)S(1)} %all-to-all-done.slab_ref, bf16[128,128]{1,0:T(8,128)(2,1)S(1)} %pad.5.table_ref, s32[32,128]{1,0:T(8,128)S(1)} %bitcast.15, f32[512,1152]{1,0:T(8,128)} %shard_map.85.start_hbm), custom_call_target="tpu_custom_call" | custom-call | flops 4831838208 | bytes 4194304 | tf_op jit(solution)/shard_map/pallas_call | solution.py:524
  43.6 3.9 %all-to-all-start.1 = ((bf16[16,35,8,128]{3,2,1,0:T(8,128)(2,1)}), bf16[16,35,8,128]{3,2,1,0:T(8,128)(2,1)S(1)}, u32[]{:S(2)}, u32[]{:S(2)}) async-start(bf16[16,35,8,128]{3,2,1,0:T(8,128)(2,1)} %get-tuple-element.17), calls=%async_computation.1 | async-start | bytes 2293760 | tf_op jit(solution)/shard_map/all_to_all | solution.py:473
  47.5 10.7 %shard_map.87 = (f32[4096,128]{1,0:T(8,128)}, bf16[128,5,8,128]{3,2,1,0:T(8,128)(2,1)S(1)}) custom-call(bf16[128,40,128]{2,1,0:T(8,128)(2,1)} %get-tuple-element.15.slab_hbm, bf16[4096,128]{1,0:T(8,128)(2,1)} %old_hbm.1), custom_call_target="tpu_custom_call" | custom-call | flops 9663676416 | bytes 4194304 | tf_op jit(solution)/shard_map/pallas_call | solution.py:547
  58.2 5.4 %all-to-all-done.1 = bf16[16,35,8,128]{3,2,1,0:T(8,128)(2,1)S(1)} async-done(((bf16[16,35,8,128]{3,2,1,0:T(8,128)(2,1)}), bf16[16,35,8,128]{3,2,1,0:T(8,128)(2,1)S(1)}, u32[]{:S(2)}, u32[]{:S(2)}) %all-to-all-start.1) | async-done | bytes 1146912 | tf_op jit(solution)/shard_map/all_to_all | solution.py:473
  63.6 1.3 %shard_map.88 = (f32[256,128]{1,0:T(8,128)}, bf16[128,5,8,128]{3,2,1,0:T(8,128)(2,1)S(1)}) custom-call(bf16[16,280,128]{2,1,0:T(8,128)(2,1)S(1)} %bitcast.13, bf16[128,5,8,128]{3,2,1,0:T(8,128)(2,1)S(1)} %get-tuple-element.18.send_in), custom_call_target="tpu_custom_call", output_to_operand_aliasing={{1}: (1, {})} | custom-call | bytes 4194304 | tf_op jit(solution)/shard_map/pallas_call | solution.py:573
  64.8 0.0 copy-start
  64.8 28.3 %all_to_all.15 = bf16[128,5,8,128]{3,2,1,0:T(8,128)(2,1)S(1)} all-to-all(bf16[128,5,8,128]{3,2,1,0:T(8,128)(2,1)S(1)} %get-tuple-element.20), channel_id=1, replica_groups=mesh['dp'=8,'cent'=16] {'dp','cent'}, dimensions={0} | all-to-all | bytes 2621440 | tf_op jit(solution)/shard_map/all_to_all | solution.py:473
  93.2 1.6 %collective-permute-start = (bf16[128,8,128]{2,1,0:T(8,128)(2,1)S(1)}, bf16[128,8,128]{2,1,0:T(8,128)(2,1)S(1)}, u32[]{:S(2)}, u32[]{:S(2)}) collective-permute-start(bf16[128,8,128]{2,1,0:T(8,128)(2,1)S(1)} %slice_bitcast_fusion), channel_id=1, source_target_pairs={{0,16},{16,0},{32,48},{48,32},{64,80},{80,64},{96,112},{112,96},{1... | collective-permute-start | bytes 786440 | tf_op jit(solution)/shard_map/ppermute | solution.py:588
  94.7 0.0 copy-done
  94.7 1.4 %shard_map.89 = (bf16[256,1024]{1,0:T(8,128)(2,1)}, f32[16,2,8,1024]{3,2,1,0:T(8,128)}) custom-call(bf16[256,512]{1,0:T(8,128)(2,1)S(1)} %copy-done, bf16[8,16,40,128]{3,2,1,0:T(8,128)(2,1)S(1)} %bitcast.12), custom_call_target="tpu_custom_call" | custom-call | flops 268435456 | bytes 4194304 | tf_op jit(solution)/shard_map/pallas_call | solution.py:590
  96.1 0.0 collective-permute-done
  96.1 0.9 shard_map.90
  (4 shorter events, 0.1 us)
Async XLA Ops:
  3.8 11.5 %copy-start.2 = (s32[4096]{0:T(1024)S(1)}, s32[4096]{0:T(1024)}, u32[]{:S(2)}) copy-start(s32[4096]{0:T(1024)} %param.7) | copy-start | bytes 49156
  3.8 32.9 %all-to-all-start = ((bf16[128,40,128]{2,1,0:T(8,128)(2,1)}), bf16[128,40,128]{2,1,0:T(8,128)(2,1)S(1)}, u32[]{:S(2)}, u32[]{:S(2)}) async-start(bf16[128,40,128]{2,1,0:T(8,128)(2,1)} %bitcast.16), calls=%async_computation | async-start | bytes 2621440 | tf_op jit(solution)/shard_map/all_to_all | solution.py:473
  15.7 21.0 %copy-start.1 = (s32[4096]{0:T(1024)S(1)}, s32[4096]{0:T(1024)}, u32[]{:S(2)}) copy-start(s32[4096]{0:T(1024)} %param.8) | copy-start | bytes 49156
  43.6 20.0 %all-to-all-start.1 = ((bf16[16,35,8,128]{3,2,1,0:T(8,128)(2,1)}), bf16[16,35,8,128]{3,2,1,0:T(8,128)(2,1)S(1)}, u32[]{:S(2)}, u32[]{:S(2)}) async-start(bf16[16,35,8,128]{3,2,1,0:T(8,128)(2,1)} %get-tuple-element.17), calls=%async_computation.1 | async-start | bytes 2293760 | tf_op jit(solution)/shard_map/all_to_all | solution.py:473
  64.8 29.9 %copy-start = (bf16[256,512]{1,0:T(8,128)(2,1)S(1)}, bf16[256,512]{1,0:T(8,128)(2,1)}, u32[]{:S(2)}) copy-start(bf16[256,512]{1,0:T(8,128)(2,1)} %get-tuple-element.21.back_ref) | copy-start | bytes 786436
  93.2 3.0 %collective-permute-start = (bf16[128,8,128]{2,1,0:T(8,128)(2,1)S(1)}, bf16[128,8,128]{2,1,0:T(8,128)(2,1)S(1)}, u32[]{:S(2)}, u32[]{:S(2)}) collective-permute-start(bf16[128,8,128]{2,1,0:T(8,128)(2,1)S(1)} %slice_bitcast_fusion), channel_id=1, source_target_pairs={{0,16},{16,0},{32,48},{48,32},{64,80},{80,64},{96,112},{112,96},{1... | collective-permute-start | bytes 786440 | tf_op jit(solution)/shard_map/ppermute | solution.py:588

commit v11 on v10

--- a/solution.py
+++ b/solution.py
@@ -57,12 +57,22 @@
     )
 
 
-def pack_kernel(
-    assign_hbm, points_hbm, send_hbm, back_hbm, assign_ref, points_ref, send_ref, back_ref, sems
-):
+def owner_slots(label, owners):
+    count = label.shape[1]
+    owner = lax.shift_right_logical(label, 12)
+    mine = jnp.where(iota((owners, count), 0) == owner, 1.0, 0.0)
+    before = jnp.where(iota((count, count), 0) <= iota((count, count), 1), 1.0, 0.0).astype(BF16)
+    place = jnp.sum(dot(mine.astype(BF16), before) * mine, axis=0, keepdims=True).astype(I32) - 1
+    return mine, place, owner * CAP + place
+
+
+def slot_table(slot, slots):
+    return jnp.where(iota((slots, slot.shape[1]), 0) == slot, 1.0, 0.0).astype(BF16)
+
+
+def pack_kernel(assign_hbm, points_hbm, send_hbm, assign_ref, points_ref, send_ref, sems):
     owners = send_ref.shape[1]
     parts = send_ref.shape[0]
-    count = points_ref.shape[0]
     load = pltpu.make_async_copy(assign_hbm, assign_ref, sems.at[0])
     load.start()
     loads = []
@@ -72,23 +82,16 @@
             pltpu.make_async_copy(points_hbm.at[:, at], points_ref.at[:, at], sems.at[1 + pair])
         )
         loads[-1].start()
-    before = jnp.where(iota((count, count), 0) <= iota((count, count), 1), 1.0, 0.0).astype(BF16)
-    same = jnp.where(iota((count, count), 0) == iota((count, count), 1), 1.0, 0.0).astype(BF16)
     load.wait()
     label = assign_ref[...]
-    owner = lax.shift_right_logical(label, 12)
+    mine, place, slot = owner_slots(label, owners)
     local = label & 4095
-    mine = iota((owners, count), 0) == owner
-    mine_f = jnp.where(mine, 1.0, 0.0)
-    running = dot(mine_f.astype(BF16), before)
-    place = jnp.sum(running * mine_f, axis=0, keepdims=True).astype(I32) - 1
-    slot = owner * CAP + place
-    table = jnp.where(iota((owners * CAP, count), 0) == slot, 1.0, 0.0).astype(BF16)
+    table = slot_table(slot, owners * CAP)
     shift = (lax.axis_index("cent") % 8) * HALF
-    line = iota((LANES, count), 0)
+    line = iota((LANES, points_ref.shape[0]), 0)
     row = iota((owners, EXTRA, LANES), 1)
     digits = [(lax.shift_right_logical(local, 6) + 1).astype(F32), ((local & 63) + 1).astype(F32)]
-    digits = [(mine_f * digit).astype(BF16) for digit in digits]
+    digits = [(mine * digit).astype(BF16) for digit in digits]
     extra = jnp.zeros((owners, EXTRA, LANES), F32)
     for half in range(2):
         first = half * HALF
@@ -111,10 +114,6 @@
             pltpu.make_async_copy(send_ref.at[part], send_hbm.at[part], sems.at[1 + parts // 2 + part])
         )
         stores[-1].start()
-        if part == 0:
-            back_ref[...] = dot_nt(same, table).astype(BF16)
-            stores.append(pltpu.make_async_copy(back_ref, back_hbm, sems.at[1 + parts // 2 + parts]))
-            stores[-1].start()
     for store in stores:
         store.wait()
 
@@ -207,7 +206,13 @@
         live_ref[group] = jnp.where(most > 0.0, 1, 0)
 
 
-def parent_kernel(parent_ref, old_ref, total_hbm, digits_ref, left_ref, high_ref, total_ref, sem):
+def parent_kernel(
+    parent_ref, old_ref, assign_ref, total_hbm, back_ref, digits_ref, left_ref, high_ref, total_ref, sem
+):
+    count, slots = back_ref.shape
+    unused, unused, slot = owner_slots(assign_ref[...], slots // CAP)
+    same = jnp.where(iota((count, count), 0) == iota((count, count), 1), 1.0, 0.0).astype(BF16)
+    back_ref[...] = dot_nt(same, slot_table(slot, slots)).astype(BF16)
     parent = parent_ref[...]
     digits_ref[0:32, :] = (lax.shift_right_logical(parent, 6) + 1).astype(F32)
     digits_ref[32:64, :] = ((parent & 63) + 1).astype(F32)
@@ -237,8 +242,8 @@
 
 def upper_kernel(
     slab_ref, table_ref, top_ref, start_hbm, send_hbm, slab_hbm,
-    digits_ref, parents_ref, total_ref, left_ref, high_ref, start_ref, send_ref, right_ref, tail_ref, live_ref,
-    sems,
+    digits_ref, parents_ref, total_ref, left_ref, high_ref, start_ref, send_ref, right_ref, hits_ref, tail_ref,
+    live_ref, sems,
 ):
     load = pltpu.make_async_copy(start_hbm, start_ref, sems.at[0])
     load.start()
@@ -246,6 +251,9 @@
     keep.start()
     slot_digits(slab_ref, digits_ref)
     mark_live(digits_ref, live_ref)
+    for part in range(HIGHS * 4):
+        hit = iota((256, LANES), 0) == top_ref[part : part + 1, :]
+        hits_ref[:, lane_slice(part)] = jnp.where(hit, 1.0, 0.0).astype(BF16)
     for step in range(4):
         find_parents(digits_ref, parents_ref, table_ref, 4 * step, 4)
     segments(total_ref, left_ref, high_ref, lambda step: lower_rows(slab_ref, step), parents_ref, 4)
@@ -267,7 +275,6 @@
     split = jnp.where(lane < HIGHS, coarse, weights - coarse)
     diagonal = jnp.where(iota((16, LANES), 0) == iota((16, LANES), 1), 1.0, 0.0).astype(BF16)
     across = dot_nt(diagonal, split.astype(BF16))
-    tops = []
     stores = [keep]
     for high in range(HIGHS):
         mass = (total_ref[:, lane_slice(high)] + start_ref[:, lane_slice(high)]).astype(BF16)
@@ -278,15 +285,12 @@
         stores[-1].start()
         right_ref[lane_slice(high, LOW), 0:LANES] = mass
         right_ref[lane_slice(high, LOW), LANES:] = jnp.where((lane & 7) == high, split, 0.0).astype(BF16)
-        for part in range(4):
-            hit = iota((256, LANES), 0) == top_ref[high * 4 + part : high * 4 + part + 1, :]
-            tops.append(jnp.where(hit, 1.0, 0.0).astype(BF16))
     for half in range(2):
         for kind in range(2):
             lines = slice(kind * HIGHS, (kind + 1) * HIGHS)
             for side in range(2):
                 tail_ref[pl.ds(side, HIGHS, 2), 2 * kind + half, :] = across[lines, lane_slice(2 * side + half)]
-    tops = dot(jnp.concatenate(tops, axis=1), right_ref[...])
+    tops = dot(hits_ref[...], right_ref[...])
     owners = send_ref.shape[0]
     send_ref[:, 32:34] = tops[:, :LANES].astype(BF16).reshape(owners, 2, 8, LANES)
     first = jnp.where(iota((8, LANES), 1) < 16, 1.0, 0.0).astype(BF16)
@@ -403,27 +407,36 @@
     lax.fori_loop(0, groups, settle, 0)
 
 
-def finish_kernel(parts_ref, send_in, level_ref, send_hbm, column_ref, top_ref, sem):
-    total = parts_ref[0].astype(F32)
+def add_parts(parts_ref, lines):
+    total = parts_ref[0, lines].astype(F32)
     for source in range(1, parts_ref.shape[0]):
-        total += parts_ref[source].astype(F32)
-    tail = total[272:280].T
+        total += parts_ref[source, lines].astype(F32)
+    return total
+
+
+def middle_kernel(parts_ref, level_ref):
+    tail = add_parts(parts_ref, slice(272, 280)).T
+    for half in range(2):
+        weight = tail[:, half : half + 1] + tail[:, half + 2 : half + 3]
+        lines = slice(half * LANES, (half + 1) * LANES)
+        level_ref[lines, :] = add_parts(parts_ref, lines) / jnp.broadcast_to(weight, (LANES, LANES))
+
+
+def top_kernel(parts_ref, send_in, send_hbm, column_ref, top_ref, sem):
+    owners = parts_ref.shape[0]
+    total = add_parts(parts_ref, slice(256, 280))
+    tail = total[16:24].T
     me = lax.axis_index("cent")
-    owners = parts_ref.shape[0]
     chosen = jnp.where(me < 8, tail[:, 4:5] + tail[:, 6:7], tail[:, 5:6] + tail[:, 7:8])
     column_ref[...] = jnp.broadcast_to(chosen, (LANES, LANES))
     weight = column_ref[pl.ds(pl.multiple_of((me % 8) * TOP, TOP), TOP), :]
-    top = (total[256:272] / weight).astype(BF16)
+    top = (total[0:TOP] / weight).astype(BF16)
     for group in range(top_ref.shape[0] // owners):
         first = group % 2 * (TOP // 2)
         part = jnp.broadcast_to(top[first : first + TOP // 2][None, None], (owners, 1, TOP // 2, LANES))
         top_ref[group * owners : (group + 1) * owners] = part
     store = pltpu.make_async_copy(top_ref, send_hbm.at[:, pl.ds(CAP // 8, 1)], sem)
     store.start()
-    for half in range(2):
-        weight = tail[:, half : half + 1] + tail[:, half + 2 : half + 3]
-        lines = slice(half * LANES, (half + 1) * LANES)
-        level_ref[lines, :] = total[lines] / jnp.broadcast_to(weight, (LANES, LANES))
     store.wait()
 
 
@@ -485,28 +498,28 @@
     answer_dims = (devices, (CAP + TOP // 2) // 8, 8, lanes)
     work = 2 * LOW * block * (HIGHS + 1) * LANES
 
-    send, back = call(
+    labels = assign.reshape(1, count)
+    send = call(
         pack_kernel,
-        (shape((groups, owners, rows, lanes), BF16), shape((count, slots), BF16)),
+        pltpu.HBM((groups, owners, rows, lanes), BF16),
         [HBM, HBM],
-        (HBM, HBM),
+        HBM,
         FULL,
         [
             pltpu.VMEM((1, count), I32),
             pltpu.VMEM((count, width), BF16),
             pltpu.VMEM((groups, owners, rows, lanes), BF16),
-            pltpu.VMEM((count, slots), BF16),
-            pltpu.SemaphoreType.DMA((2 + groups // 2 + groups,)),
+            pltpu.SemaphoreType.DMA((1 + groups // 2 + groups,)),
         ],
         flops=2 * slots * count * width,
-    )(assign.reshape(1, count), points)
+    )(labels, points)
     slab = swap(send.reshape(devices, rows, lanes), BOTH)
 
-    start = call(
+    start, back = call(
         parent_kernel,
-        pltpu.HBM(total_dims, F32),
-        [VMEM, VMEM],
-        HBM,
+        (pltpu.HBM(total_dims, F32), shape((count, slots), BF16)),
+        [VMEM, VMEM, VMEM],
+        (HBM, VMEM),
         FULL,
         [
             pltpu.VMEM((64, LANES), F32),
@@ -516,7 +529,7 @@
             pltpu.SemaphoreType.DMA(()),
         ],
         flops=work,
-    )(parent_one.reshape(block // LANES, LANES), old_level_one)
+    )(parent_one.reshape(block // LANES, LANES), old_level_one, labels)
     grid = parent_one.reshape(64, 64).T
     table = jnp.concatenate([lax.shift_right_logical(grid, 6), grid & 63], axis=0) + 1
     table = jnp.pad(table, ((0, 0), (0, 64))).astype(BF16)
@@ -536,6 +549,7 @@
             pltpu.VMEM(total_dims, F32),
             pltpu.VMEM((owners, 35, 8, lanes), BF16),
             pltpu.VMEM((HIGHS * LOW, 2 * LANES), BF16),
+            pltpu.VMEM((256, HIGHS * LOW), BF16),
             pltpu.VMEM((owners, 8, lanes), F32),
             pltpu.SMEM((groups,), I32),
             pltpu.SemaphoreType.DMA((3 + HIGHS,)),
@@ -570,20 +584,23 @@
         flops=2 * work,
     )(in_hbm(slab_kept), in_hbm(old_level_one))
 
-    level_two, answer = call(
-        finish_kernel,
-        (shape((256, lanes), F32), shape(answer_dims, BF16)),
+    shares = shares.reshape(owners, -1, lanes)
+    answer = call(
+        top_kernel,
+        shape(answer_dims, BF16),
         [VMEM, HBM],
-        (VMEM, HBM),
+        HBM,
         SMALL,
         [
             pltpu.VMEM((LANES, LANES), F32),
             pltpu.VMEM((devices, 1, TOP // 2, lanes), BF16),
             pltpu.SemaphoreType.DMA(()),
         ],
-        alias={1: 1},
-    )(shares.reshape(owners, -1, lanes), answer)
+        alias={1: 0},
+    )(shares, answer)
+    level_two = call(middle_kernel, shape((256, lanes), F32), [VMEM], VMEM, SMALL, flops=work)(shares)
     returned = swap(answer, BOTH)
+    returned, level_two = lax.optimization_barrier((returned, level_two))
     half = returned[:, CAP // 8]
     half = lax.ppermute(half, "dp", [(group, group ^ 1) for group in range(groups)])
     top_dims = (owners, 2, TOP // 2, width)

time: 98.4 us -> 98.3 us (level); the launches traced: 97.2 us -> 98.2 us
  blocking collectives: 28.3 us -> 0 us
  waiting for transfers between devices: 17 us -> 36.5 us
  starting transfers between devices: 17 us -> 24.5 us
  Pallas kernels: 33.6 us -> 35.9 us
    all_to_all x1 -> x0, blocking collectives: 28.3 us -> none  [swap(): return lax.all_to_all(value, axes, split_axis=0, concat_axis=0, tiled=True)]
    all_to_all x2 -> x3, waiting for transfers between devices: 17 us -> 36.5 us  [swap(): return lax.all_to_all(value, axes, split_axis=0, concat_axis=0, tiled=True)]
    all_to_all x2 -> x3, starting transfers between devices: 15.4 us -> 22.9 us  [swap(): return lax.all_to_all(value, axes, split_axis=0, concat_axis=0, tiled=True)]
    pallas_call x3 -> x4, Pallas kernels: 13.8 us -> 15.4 us  [the longest x1 10.3 us: on_device(): call(parent_kernel, (pltpu.HBM(total_dims, F32), shape((count, slots), BF...]
  transfers between devices with their start and end apart: 3 -> 4, of which waited for: 2 -> 3; matrix products, arithmetic and copies ran while one was open for 0% -> 0% of each run, Pallas kernels for 22% -> 24%
where the time goes in v11:
time: 98.3 us; the launch traced here: 98.2 us
  waiting for transfers between devices  36.5 us (37%)
  Pallas kernels  35.9 us (37%)
  starting transfers between devices  24.5 us (25%)
    all_to_all x3, waiting for transfers between devices, swap(): return lax.all_to_all(value, axes, split_axis=0, concat_axis=0, tiled=True)  36.5 us
    all_to_all x3, starting transfers between devices, swap(): return lax.all_to_all(value, axes, split_axis=0, concat_axis=0, tiled=True)  22.9 us
    pallas_call x1, Pallas kernels, on_device(): call(level_kernel, (shape((block, lanes), F32), shape(answer_dims, BF16))...  10.8 us
    pallas_call x1, Pallas kernels, on_device(): call(parent_kernel, (pltpu.HBM(total_dims, F32), shape((count, slots), BF...  10.3 us
    pallas_call x1, Pallas kernels, on_device(): call(upper_kernel, (pltpu.HBM((owners, 35, 8, lanes), BF16), pltpu.HBM((d...  7.45 us
    pallas_call x1, Pallas kernels, on_device(): call(pack_kernel, pltpu.HBM((groups, owners, rows, lanes), BF16), [HBM, H...  3.11 us
  transfers between devices with their start and end apart: 4, of which 3 were waited for; matrix products, arithmetic and copies ran while one was open for 0% of the time, Pallas kernels for 24%

profile of v11, /device:TPU:1, one launch (start us, length us, event | category | flops | bytes accessed | tf_op | source)
XLA Modules:
  0.0 98.2 jit_solution(4418584974759299154)
XLA Ops:
  0.6 3.1 %shard_map.84 = bf16[8,16,40,128]{3,2,1,0:T(8,128)(2,1)} custom-call(s32[1,256]{1,0:T(1,128)} %bitcast.22, bf16[256,1024]{1,0:T(8,128)(2,1)} %points_hbm.1), custom_call_target="tpu_custom_call" | custom-call | flops 268435456 | bytes 4194304 | tf_op jit(solution)/shard_map/pallas_call | solution.py:502
  3.7 0.0 copy-start.2
  3.8 11.5 %all-to-all-start = ((bf16[128,40,128]{2,1,0:T(8,128)(2,1)}), bf16[128,40,128]{2,1,0:T(8,128)(2,1)S(1)}, u32[]{:S(2)}, u32[]{:S(2)}) async-start(bf16[128,40,128]{2,1,0:T(8,128)(2,1)} %bitcast.17), calls=%async_computation | async-start | bytes 2621440 | tf_op jit(solution)/shard_map/all_to_all | solution.py:486
  15.3 0.0 copy-done.2
  15.3 0.1 shift_right_logical.14
  15.4 0.1 copy.11
  15.4 0.1 and.14
  15.5 0.1 copy.12
  15.6 0.0 copy-start.1
  15.7 10.3 %shard_map.85 = (f32[512,1152]{1,0:T(8,128)}, bf16[256,512]{1,0:T(8,128)(2,1)}) custom-call(s32[32,128]{1,0:T(8,128)} %bitcast.21, bf16[4096,128]{1,0:T(8,128)(2,1)} %old_hbm.1, s32[1,256]{1,0:T(1,128)} %bitcast.23), custom_call_target="tpu_custom_call" | custom-call | flops 4831838208 | bytes 4194304 | tf_op jit(solution)/shard_map/pallas_call | solution.py:518
  25.9 10.7 %all-to-all-done.slab_ref = bf16[128,40,128]{2,1,0:T(8,128)(2,1)S(1)} async-done(((bf16[128,40,128]{2,1,0:T(8,128)(2,1)}), bf16[128,40,128]{2,1,0:T(8,128)(2,1)S(1)}, u32[]{:S(2)}, u32[]{:S(2)}) %all-to-all-start) | async-done | bytes 1310752 | tf_op jit(solution)/shard_map/all_to_all | solution.py:486
  36.6 0.0 copy-done.1
  36.6 7.5 %shard_map.86 = (bf16[16,35,8,128]{3,2,1,0:T(8,128)(2,1)}, bf16[128,40,128]{2,1,0:T(8,128)(2,1)}) custom-call(bf16[128,40,128]{2,1,0:T(8,128)(2,1)S(1)} %all-to-all-done.slab_ref, bf16[128,128]{1,0:T(8,128)(2,1)S(1)} %pad.5.table_ref, s32[32,128]{1,0:T(8,128)S(1)} %bitcast.16, f32[512,1152]{1,0:T(8,128)} %get-tuple-element.14.start_hbm), custom_call_target="tpu_custom_call" | custom-call | flops 4831838208 | bytes 4194304 | tf_op jit(solution)/shard_map/pallas_call | solution.py:537
  44.1 4.1 %all-to-all-start.1 = ((bf16[16,35,8,128]{3,2,1,0:T(8,128)(2,1)}), bf16[16,35,8,128]{3,2,1,0:T(8,128)(2,1)S(1)}, u32[]{:S(2)}, u32[]{:S(2)}) async-start(bf16[16,35,8,128]{3,2,1,0:T(8,128)(2,1)} %get-tuple-element.17), calls=%async_computation.1 | async-start | bytes 2293760 | tf_op jit(solution)/shard_map/all_to_all | solution.py:486
  48.1 10.8 %shard_map.87 = (f32[4096,128]{1,0:T(8,128)}, bf16[128,5,8,128]{3,2,1,0:T(8,128)(2,1)}) custom-call(bf16[128,40,128]{2,1,0:T(8,128)(2,1)} %get-tuple-element.15.slab_hbm, bf16[4096,128]{1,0:T(8,128)(2,1)} %old_hbm.1), custom_call_target="tpu_custom_call" | custom-call | flops 9663676416 | bytes 4194304 | tf_op jit(solution)/shard_map/pallas_call | solution.py:561
  59.0 5.4 %all-to-all-done.1 = bf16[16,35,8,128]{3,2,1,0:T(8,128)(2,1)S(1)} async-done(((bf16[16,35,8,128]{3,2,1,0:T(8,128)(2,1)}), bf16[16,35,8,128]{3,2,1,0:T(8,128)(2,1)S(1)}, u32[]{:S(2)}, u32[]{:S(2)}) %all-to-all-start.1) | async-done | bytes 1146912 | tf_op jit(solution)/shard_map/all_to_all | solution.py:486
  64.4 1.1 %shard_map.88 = bf16[128,5,8,128]{3,2,1,0:T(8,128)(2,1)} custom-call(bf16[16,280,128]{2,1,0:T(8,128)(2,1)S(1)} %bitcast.13, bf16[128,5,8,128]{3,2,1,0:T(8,128)(2,1)} %get-tuple-element.18.send_in), custom_call_target="tpu_custom_call", output_to_operand_aliasing={{}: (1, {})} | custom-call | bytes 4194304 | tf_op jit(solution)/shard_map/pallas_call | solution.py:588
  65.5 7.3 %all-to-all-start.2 = ((bf16[128,5,8,128]{3,2,1,0:T(8,128)(2,1)}), bf16[128,5,8,128]{3,2,1,0:T(8,128)(2,1)S(1)}, u32[]{:S(2)}, u32[]{:S(2)}) async-start(bf16[128,5,8,128]{3,2,1,0:T(8,128)(2,1)} %shard_map.88), calls=%async_computation.2 | async-start | bytes 2621440 | tf_op jit(solution)/shard_map/all_to_all | solution.py:486
  72.8 0.0 copy-start
  72.9 1.0 shard_map.89
  73.8 20.4 %all-to-all-done.2 = bf16[128,5,8,128]{3,2,1,0:T(8,128)(2,1)S(1)} async-done(((bf16[128,5,8,128]{3,2,1,0:T(8,128)(2,1)}), bf16[128,5,8,128]{3,2,1,0:T(8,128)(2,1)S(1)}, u32[]{:S(2)}, u32[]{:S(2)}) %all-to-all-start.2) | async-done | bytes 1310752 | tf_op jit(solution)/shard_map/all_to_all | solution.py:486
  94.2 1.6 %collective-permute-start = (bf16[128,8,128]{2,1,0:T(8,128)(2,1)S(1)}, bf16[128,8,128]{2,1,0:T(8,128)(2,1)S(1)}, u32[]{:S(2)}, u32[]{:S(2)}) collective-permute-start(bf16[128,8,128]{2,1,0:T(8,128)(2,1)S(1)} %slice_bitcast_fusion), channel_id=1, source_target_pairs={{0,16},{16,0},{32,48},{48,32},{64,80},{80,64},{96,112},{112,96},{1... | collective-permute-start | bytes 786440 | tf_op jit(solution)/shard_map/ppermute | solution.py:605
  95.8 0.0 copy-done
  95.8 1.4 %shard_map.90 = (bf16[256,1024]{1,0:T(8,128)(2,1)}, f32[16,2,8,1024]{3,2,1,0:T(8,128)}) custom-call(bf16[256,512]{1,0:T(8,128)(2,1)S(1)} %copy-done, bf16[8,16,40,128]{3,2,1,0:T(8,128)(2,1)S(1)} %bitcast.12), custom_call_target="tpu_custom_call" | custom-call | flops 268435456 | bytes 4194304 | tf_op jit(solution)/shard_map/pallas_call | solution.py:607
  97.2 0.0 collective-permute-done
  97.2 0.9 shard_map.91
  (4 shorter events, 0.1 us)
Async XLA Ops:
  3.7 11.5 %copy-start.2 = (s32[4096]{0:T(1024)S(1)}, s32[4096]{0:T(1024)}, u32[]{:S(2)}) copy-start(s32[4096]{0:T(1024)} %param.7) | copy-start | bytes 49156
  3.8 32.9 %all-to-all-start = ((bf16[128,40,128]{2,1,0:T(8,128)(2,1)}), bf16[128,40,128]{2,1,0:T(8,128)(2,1)S(1)}, u32[]{:S(2)}, u32[]{:S(2)}) async-start(bf16[128,40,128]{2,1,0:T(8,128)(2,1)} %bitcast.17), calls=%async_computation | async-start | bytes 2621440 | tf_op jit(solution)/shard_map/all_to_all | solution.py:486
  15.6 21.0 %copy-start.1 = (s32[4096]{0:T(1024)S(1)}, s32[4096]{0:T(1024)}, u32[]{:S(2)}) copy-start(s32[4096]{0:T(1024)} %param.8) | copy-start | bytes 49156
  44.1 20.3 %all-to-all-start.1 = ((bf16[16,35,8,128]{3,2,1,0:T(8,128)(2,1)}), bf16[16,35,8,128]{3,2,1,0:T(8,128)(2,1)S(1)}, u32[]{:S(2)}, u32[]{:S(2)}) async-start(bf16[16,35,8,128]{3,2,1,0:T(8,128)(2,1)} %get-tuple-element.17), calls=%async_computation.1 | async-start | bytes 2293760 | tf_op jit(solution)/shard_map/all_to_all | solution.py:486
  65.5 28.7 %all-to-all-start.2 = ((bf16[128,5,8,128]{3,2,1,0:T(8,128)(2,1)}), bf16[128,5,8,128]{3,2,1,0:T(8,128)(2,1)S(1)}, u32[]{:S(2)}, u32[]{:S(2)}) async-start(bf16[128,5,8,128]{3,2,1,0:T(8,128)(2,1)} %shard_map.88), calls=%async_computation.2 | async-start | bytes 2621440 | tf_op jit(solution)/shard_map/all_to_all | solution.py:486
  72.8 22.9 %copy-start = (bf16[256,512]{1,0:T(8,128)(2,1)S(1)}, bf16[256,512]{1,0:T(8,128)(2,1)}, u32[]{:S(2)}) copy-start(bf16[256,512]{1,0:T(8,128)(2,1)} %get-tuple-element.21.back_ref) | copy-start | bytes 786436
  94.2 3.0 %collective-permute-start = (bf16[128,8,128]{2,1,0:T(8,128)(2,1)S(1)}, bf16[128,8,128]{2,1,0:T(8,128)(2,1)S(1)}, u32[]{:S(2)}, u32[]{:S(2)}) collective-permute-start(bf16[128,8,128]{2,1,0:T(8,128)(2,1)S(1)} %slice_bitcast_fusion), channel_id=1, source_target_pairs={{0,16},{16,0},{32,48},{48,32},{64,80},{80,64},{96,112},{112,96},{1... | collective-permute-start | bytes 786440 | tf_op jit(solution)/shard_map/ppermute | solution.py:605

commit v12 on v11

--- a/solution.py
+++ b/solution.py
@@ -242,8 +242,8 @@
 
 def upper_kernel(
     slab_ref, table_ref, top_ref, start_hbm, send_hbm, slab_hbm,
-    digits_ref, parents_ref, total_ref, left_ref, high_ref, start_ref, send_ref, right_ref, hits_ref, tail_ref,
-    live_ref, sems,
+    digits_ref, parents_ref, total_ref, left_ref, high_ref, start_ref, send_ref, right_ref, tail_ref, live_ref,
+    sems,
 ):
     load = pltpu.make_async_copy(start_hbm, start_ref, sems.at[0])
     load.start()
@@ -251,9 +251,6 @@
     keep.start()
     slot_digits(slab_ref, digits_ref)
     mark_live(digits_ref, live_ref)
-    for part in range(HIGHS * 4):
-        hit = iota((256, LANES), 0) == top_ref[part : part + 1, :]
-        hits_ref[:, lane_slice(part)] = jnp.where(hit, 1.0, 0.0).astype(BF16)
     for step in range(4):
         find_parents(digits_ref, parents_ref, table_ref, 4 * step, 4)
     segments(total_ref, left_ref, high_ref, lambda step: lower_rows(slab_ref, step), parents_ref, 4)
@@ -275,6 +272,7 @@
     split = jnp.where(lane < HIGHS, coarse, weights - coarse)
     diagonal = jnp.where(iota((16, LANES), 0) == iota((16, LANES), 1), 1.0, 0.0).astype(BF16)
     across = dot_nt(diagonal, split.astype(BF16))
+    tops = []
     stores = [keep]
     for high in range(HIGHS):
         mass = (total_ref[:, lane_slice(high)] + start_ref[:, lane_slice(high)]).astype(BF16)
@@ -285,12 +283,15 @@
         stores[-1].start()
         right_ref[lane_slice(high, LOW), 0:LANES] = mass
         right_ref[lane_slice(high, LOW), LANES:] = jnp.where((lane & 7) == high, split, 0.0).astype(BF16)
+        for part in range(4):
+            hit = iota((256, LANES), 0) == top_ref[high * 4 + part : high * 4 + part + 1, :]
+            tops.append(jnp.where(hit, 1.0, 0.0).astype(BF16))
     for half in range(2):
         for kind in range(2):
             lines = slice(kind * HIGHS, (kind + 1) * HIGHS)
             for side in range(2):
                 tail_ref[pl.ds(side, HIGHS, 2), 2 * kind + half, :] = across[lines, lane_slice(2 * side + half)]
-    tops = dot(hits_ref[...], right_ref[...])
+    tops = dot(jnp.concatenate(tops, axis=1), right_ref[...])
     owners = send_ref.shape[0]
     send_ref[:, 32:34] = tops[:, :LANES].astype(BF16).reshape(owners, 2, 8, LANES)
     first = jnp.where(iota((8, LANES), 1) < 16, 1.0, 0.0).astype(BF16)
@@ -407,47 +408,41 @@
     lax.fori_loop(0, groups, settle, 0)
 
 
-def add_parts(parts_ref, lines):
-    total = parts_ref[0, lines].astype(F32)
+def finish_kernel(parts_ref, send_in, level_hbm, send_hbm, column_ref, top_ref, level_ref, sem, level_sem):
+    total = parts_ref[0].astype(F32)
     for source in range(1, parts_ref.shape[0]):
-        total += parts_ref[source, lines].astype(F32)
-    return total
-
-
-def middle_kernel(parts_ref, level_ref):
-    tail = add_parts(parts_ref, slice(272, 280)).T
-    for half in range(2):
-        weight = tail[:, half : half + 1] + tail[:, half + 2 : half + 3]
-        lines = slice(half * LANES, (half + 1) * LANES)
-        level_ref[lines, :] = add_parts(parts_ref, lines) / jnp.broadcast_to(weight, (LANES, LANES))
-
-
-def top_kernel(parts_ref, send_in, send_hbm, column_ref, top_ref, sem):
+        total += parts_ref[source].astype(F32)
+    tail = total[272:280].T
+    me = lax.axis_index("cent")
     owners = parts_ref.shape[0]
-    total = add_parts(parts_ref, slice(256, 280))
-    tail = total[16:24].T
-    me = lax.axis_index("cent")
     chosen = jnp.where(me < 8, tail[:, 4:5] + tail[:, 6:7], tail[:, 5:6] + tail[:, 7:8])
     column_ref[...] = jnp.broadcast_to(chosen, (LANES, LANES))
     weight = column_ref[pl.ds(pl.multiple_of((me % 8) * TOP, TOP), TOP), :]
-    top = (total[0:TOP] / weight).astype(BF16)
+    top = (total[256:272] / weight).astype(BF16)
     for group in range(top_ref.shape[0] // owners):
         first = group % 2 * (TOP // 2)
         part = jnp.broadcast_to(top[first : first + TOP // 2][None, None], (owners, 1, TOP // 2, LANES))
         top_ref[group * owners : (group + 1) * owners] = part
     store = pltpu.make_async_copy(top_ref, send_hbm.at[:, pl.ds(CAP // 8, 1)], sem)
     store.start()
+    for half in range(2):
+        weight = tail[:, half : half + 1] + tail[:, half + 2 : half + 3]
+        lines = slice(half * LANES, (half + 1) * LANES)
+        level_ref[lines, :] = total[lines] / jnp.broadcast_to(weight, (LANES, LANES))
+    level_store = pltpu.make_async_copy(level_ref, level_hbm, level_sem)
+    level_store.start()
     store.wait()
+    level_store.wait()
 
 
 def unpack_kernel(back_ref, returned_ref, residual_hbm, level_hbm, residual_ref, level_ref, sems):
     groups, owners, rows, lanes = returned_ref.shape
     core = lax.axis_index("dp") % 2
-    stores = []
+    for group in range(groups):
+        level_ref[:, 0, :, lane_slice(group)] = returned_ref[group, :, CAP:rows, :].astype(F32)
+    stores = [pltpu.make_async_copy(level_ref, level_hbm.at[:, pl.ds(core, 1)], sems.at[groups // 2])]
+    stores[-1].start()
     for pair in range(groups // 2):
-        for side in range(2):
-            top = returned_ref[2 * pair + side, :, CAP:rows, :].astype(F32)
-            level_ref[:, 0, :, lane_slice(2 * pair + side)] = top
         right = jnp.concatenate(
             [
                 returned_ref[2 * pair + side, :, 0:CAP, :].reshape(owners * CAP, lanes)
@@ -459,8 +454,6 @@
         residual_ref[:, at] = dot(back_ref[...], right).astype(BF16)
         stores.append(pltpu.make_async_copy(residual_ref.at[:, at], residual_hbm.at[:, at], sems.at[pair]))
         stores[-1].start()
-    stores.append(pltpu.make_async_copy(level_ref, level_hbm.at[:, pl.ds(core, 1)], sems.at[groups // 2]))
-    stores[-1].start()
     for store in stores:
         store.wait()
 
@@ -549,7 +542,6 @@
             pltpu.VMEM(total_dims, F32),
             pltpu.VMEM((owners, 35, 8, lanes), BF16),
             pltpu.VMEM((HIGHS * LOW, 2 * LANES), BF16),
-            pltpu.VMEM((256, HIGHS * LOW), BF16),
             pltpu.VMEM((owners, 8, lanes), F32),
             pltpu.SMEM((groups,), I32),
             pltpu.SemaphoreType.DMA((3 + HIGHS,)),
@@ -584,23 +576,22 @@
         flops=2 * work,
     )(in_hbm(slab_kept), in_hbm(old_level_one))
 
-    shares = shares.reshape(owners, -1, lanes)
-    answer = call(
-        top_kernel,
-        shape(answer_dims, BF16),
+    level_two, answer = call(
+        finish_kernel,
+        (shape((256, lanes), F32), shape(answer_dims, BF16)),
         [VMEM, HBM],
-        HBM,
+        (HBM, HBM),
         SMALL,
         [
             pltpu.VMEM((LANES, LANES), F32),
             pltpu.VMEM((devices, 1, TOP // 2, lanes), BF16),
+            pltpu.VMEM((256, lanes), F32),
+            pltpu.SemaphoreType.DMA(()),
             pltpu.SemaphoreType.DMA(()),
         ],
-        alias={1: 0},
-    )(shares, answer)
-    level_two = call(middle_kernel, shape((256, lanes), F32), [VMEM], VMEM, SMALL, flops=work)(shares)
+        alias={1: 1},
+    )(shares.reshape(owners, -1, lanes), answer)
     returned = swap(answer, BOTH)
-    returned, level_two = lax.optimization_barrier((returned, level_two))
     half = returned[:, CAP // 8]
     half = lax.ppermute(half, "dp", [(group, group ^ 1) for group in range(groups)])
     top_dims = (owners, 2, TOP // 2, width)

time: 98.3 us -> 98.5 us (level)
  blocking collectives: 0 us -> 28.6 us
  waiting for transfers between devices: 36.5 us -> 17.9 us
  starting transfers between devices: 24.5 us -> 18.2 us
  Pallas kernels: 35.9 us -> 32.1 us
    all_to_all x0 -> x1, blocking collectives: none -> 28.6 us  [swap(): return lax.all_to_all(value, axes, split_axis=0, concat_axis=0, tiled=True)]
    all_to_all x3 -> x2, waiting for transfers between devices: 36.5 us -> 17.9 us  [swap(): return lax.all_to_all(value, axes, split_axis=0, concat_axis=0, tiled=True)]
    all_to_all x3 -> x2, starting transfers between devices: 22.9 us -> 16.6 us  [swap(): return lax.all_to_all(value, axes, split_axis=0, concat_axis=0, tiled=True)]
    pallas_call x1, Pallas kernels: 7.45 us -> 5.99 us  [on_device(): call(upper_kernel, (pltpu.HBM((owners, 35, 8, lanes), BF16), pltpu.HBM((d...]
    pallas_call x1, Pallas kernels: 10.8 us -> 9.38 us  [on_device(): call(level_kernel, (shape((block, lanes), F32), shape(answer_dims, BF16))...]
    pallas_call x2 -> x1, Pallas kernels: 2.03 us -> 1.28 us  [on_device(): call(finish_kernel, (shape((256, lanes), F32), shape(answer_dims, BF16)),...]
  transfers between devices with their start and end apart: 4 -> 3, of which waited for: 3 -> 2; matrix products, arithmetic and copies ran while one was open for 0% -> 0% of each run, Pallas kernels for 24% -> 21%
where the time goes in v12:
time: 98.5 us; the launch traced here: 98.2 us
  Pallas kernels  32.1 us (33%)
  blocking collectives  28.6 us (29%)
  starting transfers between devices  18.2 us (18%)
  waiting for transfers between devices  17.9 us (18%)
    all_to_all x1, blocking collectives, swap(): return lax.all_to_all(value, axes, split_axis=0, concat_axis=0, tiled=True)  28.6 us
    all_to_all x2, waiting for transfers between devices, swap(): return lax.all_to_all(value, axes, split_axis=0, concat_axis=0, tiled=True)  17.9 us
    all_to_all x2, starting transfers between devices, swap(): return lax.all_to_all(value, axes, split_axis=0, concat_axis=0, tiled=True)  16.6 us
    pallas_call x1, Pallas kernels, on_device(): call(parent_kernel, (pltpu.HBM(total_dims, F32), shape((count, slots), BF...  10.3 us
    pallas_call x1, Pallas kernels, on_device(): call(level_kernel, (shape((block, lanes), F32), shape(answer_dims, BF16))...  9.38 us
    pallas_call x1, Pallas kernels, on_device(): call(upper_kernel, (pltpu.HBM((owners, 35, 8, lanes), BF16), pltpu.HBM((d...  5.99 us
    pallas_call x1, Pallas kernels, on_device(): call(pack_kernel, pltpu.HBM((groups, owners, rows, lanes), BF16), [HBM, H...  3.11 us
  transfers between devices with their start and end apart: 3, of which 2 were waited for; matrix products, arithmetic and copies ran while one was open for 0% of the time, Pallas kernels for 21%

profile of v12, /device:TPU:1, one launch (start us, length us, event | category | flops | bytes accessed | tf_op | source)
XLA Modules:
  0.0 98.2 jit_solution(11097131130230337803)
XLA Ops:
  0.6 3.1 %shard_map.84 = bf16[8,16,40,128]{3,2,1,0:T(8,128)(2,1)} custom-call(s32[1,256]{1,0:T(1,128)} %bitcast.21, bf16[256,1024]{1,0:T(8,128)(2,1)} %points_hbm.1), custom_call_target="tpu_custom_call" | custom-call | flops 268435456 | bytes 4194304 | tf_op jit(solution)/shard_map/pallas_call | solution.py:495
  3.7 0.0 copy-start.2
  3.8 11.5 %all-to-all-start = ((bf16[128,40,128]{2,1,0:T(8,128)(2,1)}), bf16[128,40,128]{2,1,0:T(8,128)(2,1)S(1)}, u32[]{:S(2)}, u32[]{:S(2)}) async-start(bf16[128,40,128]{2,1,0:T(8,128)(2,1)} %bitcast.16), calls=%async_computation | async-start | bytes 2621440 | tf_op jit(solution)/shard_map/all_to_all | solution.py:479
  15.3 0.0 copy-done.2
  15.3 0.1 shift_right_logical.14
  15.4 0.1 copy.11
  15.4 0.1 and.14
  15.5 0.1 copy.12
  15.6 0.0 copy-start.1
  15.7 10.3 %shard_map.85 = (f32[512,1152]{1,0:T(8,128)}, bf16[256,512]{1,0:T(8,128)(2,1)}) custom-call(s32[32,128]{1,0:T(8,128)} %bitcast.20, bf16[4096,128]{1,0:T(8,128)(2,1)} %old_hbm.1, s32[1,256]{1,0:T(1,128)} %bitcast.22), custom_call_target="tpu_custom_call" | custom-call | flops 4831838208 | bytes 4194304 | tf_op jit(solution)/shard_map/pallas_call | solution.py:511
  25.9 10.7 %all-to-all-done.slab_ref = bf16[128,40,128]{2,1,0:T(8,128)(2,1)S(1)} async-done(((bf16[128,40,128]{2,1,0:T(8,128)(2,1)}), bf16[128,40,128]{2,1,0:T(8,128)(2,1)S(1)}, u32[]{:S(2)}, u32[]{:S(2)}) %all-to-all-start) | async-done | bytes 1310752 | tf_op jit(solution)/shard_map/all_to_all | solution.py:479
  36.6 0.0 copy-done.1
  36.6 6.0 %shard_map.86 = (bf16[16,35,8,128]{3,2,1,0:T(8,128)(2,1)}, bf16[128,40,128]{2,1,0:T(8,128)(2,1)}) custom-call(bf16[128,40,128]{2,1,0:T(8,128)(2,1)S(1)} %all-to-all-done.slab_ref, bf16[128,128]{1,0:T(8,128)(2,1)S(1)} %pad.5.table_ref, s32[32,128]{1,0:T(8,128)S(1)} %bitcast.15, f32[512,1152]{1,0:T(8,128)} %get-tuple-element.14.start_hbm), custom_call_target="tpu_custom_call" | custom-call | flops 4831838208 | bytes 4194304 | tf_op jit(solution)/shard_map/pallas_call | solution.py:530
  42.6 5.1 %all-to-all-start.1 = ((bf16[16,35,8,128]{3,2,1,0:T(8,128)(2,1)}), bf16[16,35,8,128]{3,2,1,0:T(8,128)(2,1)S(1)}, u32[]{:S(2)}, u32[]{:S(2)}) async-start(bf16[16,35,8,128]{3,2,1,0:T(8,128)(2,1)} %get-tuple-element.17), calls=%async_computation.1 | async-start | bytes 2293760 | tf_op jit(solution)/shard_map/all_to_all | solution.py:479
  47.8 9.4 %shard_map.87 = (f32[4096,128]{1,0:T(8,128)}, bf16[128,5,8,128]{3,2,1,0:T(8,128)(2,1)S(1)}) custom-call(bf16[128,40,128]{2,1,0:T(8,128)(2,1)} %get-tuple-element.15.slab_hbm, bf16[4096,128]{1,0:T(8,128)(2,1)} %old_hbm.1), custom_call_target="tpu_custom_call" | custom-call | flops 9663676416 | bytes 4194304 | tf_op jit(solution)/shard_map/pallas_call | solution.py:553
  57.2 7.2 %all-to-all-done.1 = bf16[16,35,8,128]{3,2,1,0:T(8,128)(2,1)S(1)} async-done(((bf16[16,35,8,128]{3,2,1,0:T(8,128)(2,1)}), bf16[16,35,8,128]{3,2,1,0:T(8,128)(2,1)S(1)}, u32[]{:S(2)}, u32[]{:S(2)}) %all-to-all-start.1) | async-done | bytes 1146912 | tf_op jit(solution)/shard_map/all_to_all | solution.py:479
  64.4 1.3 %shard_map.88 = (f32[256,128]{1,0:T(8,128)}, bf16[128,5,8,128]{3,2,1,0:T(8,128)(2,1)S(1)}) custom-call(bf16[16,280,128]{2,1,0:T(8,128)(2,1)S(1)} %bitcast.13, bf16[128,5,8,128]{3,2,1,0:T(8,128)(2,1)S(1)} %get-tuple-element.18.send_in), custom_call_target="tpu_custom_call", output_to_operand_aliasing={{1}: (1, {})} | custom-call | bytes 4194304 | tf_op jit(solution)/shard_map/pallas_call | solution.py:579
  65.7 0.0 copy-start
  65.7 28.6 %all_to_all.15 = bf16[128,5,8,128]{3,2,1,0:T(8,128)(2,1)S(1)} all-to-all(bf16[128,5,8,128]{3,2,1,0:T(8,128)(2,1)S(1)} %get-tuple-element.20), channel_id=1, replica_groups=mesh['dp'=8,'cent'=16] {'dp','cent'}, dimensions={0} | all-to-all | bytes 2621440 | tf_op jit(solution)/shard_map/all_to_all | solution.py:479
  94.3 1.6 %collective-permute-start = (bf16[128,8,128]{2,1,0:T(8,128)(2,1)S(1)}, bf16[128,8,128]{2,1,0:T(8,128)(2,1)S(1)}, u32[]{:S(2)}, u32[]{:S(2)}) collective-permute-start(bf16[128,8,128]{2,1,0:T(8,128)(2,1)S(1)} %slice_bitcast_fusion), channel_id=1, source_target_pairs={{0,16},{16,0},{32,48},{48,32},{64,80},{80,64},{96,112},{112,96},{1... | collective-permute-start | bytes 786440 | tf_op jit(solution)/shard_map/ppermute | solution.py:596
  95.9 0.0 copy-done
  95.9 1.3 %shard_map.89 = (bf16[256,1024]{1,0:T(8,128)(2,1)}, f32[16,2,8,1024]{3,2,1,0:T(8,128)}) custom-call(bf16[256,512]{1,0:T(8,128)(2,1)S(1)} %copy-done, bf16[8,16,40,128]{3,2,1,0:T(8,128)(2,1)S(1)} %bitcast.12), custom_call_target="tpu_custom_call" | custom-call | flops 268435456 | bytes 4194304 | tf_op jit(solution)/shard_map/pallas_call | solution.py:598
  97.1 0.0 collective-permute-done
  97.1 0.9 shard_map.90
  (4 shorter events, 0.1 us)
Async XLA Ops:
  3.7 11.5 %copy-start.2 = (s32[4096]{0:T(1024)S(1)}, s32[4096]{0:T(1024)}, u32[]{:S(2)}) copy-start(s32[4096]{0:T(1024)} %param.7) | copy-start | bytes 49156
  3.8 32.9 %all-to-all-start = ((bf16[128,40,128]{2,1,0:T(8,128)(2,1)}), bf16[128,40,128]{2,1,0:T(8,128)(2,1)S(1)}, u32[]{:S(2)}, u32[]{:S(2)}) async-start(bf16[128,40,128]{2,1,0:T(8,128)(2,1)} %bitcast.16), calls=%async_computation | async-start | bytes 2621440 | tf_op jit(solution)/shard_map/all_to_all | solution.py:479
  15.6 21.0 %copy-start.1 = (s32[4096]{0:T(1024)S(1)}, s32[4096]{0:T(1024)}, u32[]{:S(2)}) copy-start(s32[4096]{0:T(1024)} %param.8) | copy-start | bytes 49156
  42.6 21.7 %all-to-all-start.1 = ((bf16[16,35,8,128]{3,2,1,0:T(8,128)(2,1)}), bf16[16,35,8,128]{3,2,1,0:T(8,128)(2,1)S(1)}, u32[]{:S(2)}, u32[]{:S(2)}) async-start(bf16[16,35,8,128]{3,2,1,0:T(8,128)(2,1)} %get-tuple-element.17), calls=%async_computation.1 | async-start | bytes 2293760 | tf_op jit(solution)/shard_map/all_to_all | solution.py:479
  65.7 30.2 %copy-start = (bf16[256,512]{1,0:T(8,128)(2,1)S(1)}, bf16[256,512]{1,0:T(8,128)(2,1)}, u32[]{:S(2)}) copy-start(bf16[256,512]{1,0:T(8,128)(2,1)} %get-tuple-element.21.back_ref) | copy-start | bytes 786436
  94.3 2.8 %collective-permute-start = (bf16[128,8,128]{2,1,0:T(8,128)(2,1)S(1)}, bf16[128,8,128]{2,1,0:T(8,128)(2,1)S(1)}, u32[]{:S(2)}, u32[]{:S(2)}) collective-permute-start(bf16[128,8,128]{2,1,0:T(8,128)(2,1)S(1)} %slice_bitcast_fusion), channel_id=1, source_target_pairs={{0,16},{16,0},{32,48},{48,32},{64,80},{80,64},{96,112},{112,96},{1... | collective-permute-start | bytes 786440 | tf_op jit(solution)/shard_map/ppermute | solution.py:596

commit v13 on v12

--- a/solution.py
+++ b/solution.py
@@ -128,22 +128,23 @@
     digits_ref[...] = dot(jnp.where(pick, 1.0, 0.0).astype(BF16), rows)
 
 
-def across_lanes(digits_ref, at, count):
-    found = []
-    for part in range(count):
-        high, low = digits_ref[pl.ds(at + part, 1), :], digits_ref[pl.ds(at + part + 32, 1), :]
-        found.append((high * 64.0 + low).astype(I32) - 65)
-    return found
-
-
-def down_rows(digits_ref, at, count):
+def label_rows(digits_ref, at, count):
+    return [
+        (digits_ref[pl.ds(at + part, 1), :], digits_ref[pl.ds(at + part + 32, 1), :])
+        for part in range(count)
+    ]
+
+
+def across_lanes(pairs):
+    return [(high * 64.0 + low).astype(I32) - 65 for high, low in pairs]
+
+
+def down_rows(pairs):
     same = iota((LANES, LANES), 0) == iota((LANES, LANES), 1)
-    parts = []
-    for part in range(count):
-        high, low = digits_ref[pl.ds(at + part, 1), :], digits_ref[pl.ds(at + part + 32, 1), :]
-        parts.append(
-            jnp.concatenate([jnp.where(same, high, 0.0), jnp.where(same, low, 0.0)], axis=1)
-        )
+    parts = [
+        jnp.concatenate([jnp.where(same, high, 0.0), jnp.where(same, low, 0.0)], axis=1)
+        for high, low in pairs
+    ]
     left = jnp.concatenate(parts, axis=0).astype(BF16)
     right = jnp.where(iota((2 * LANES, LANES), 0) < LANES, 64.0, 1.0).astype(BF16)
     return dot(left, right).astype(I32) - 65
@@ -167,10 +168,9 @@
 
 def segments(total_ref, left_ref, high_ref, rows_of, digits_ref, steps):
     for step in range(steps):
-        left_ref[:, lane_slice(step, 512)] = low_table(across_lanes(digits_ref, 4 * step, 4))
-        high_ref[lane_slice(step, 512), :] = lax.shift_right_arithmetic(
-            down_rows(digits_ref, 4 * step, 4), 9
-        )
+        pairs = label_rows(digits_ref, 4 * step, 4)
+        left_ref[:, lane_slice(step, 512)] = low_table(across_lanes(pairs))
+        high_ref[lane_slice(step, 512), :] = lax.shift_right_arithmetic(down_rows(pairs), 9)
     left = left_ref[:, 0 : steps * 512]
     for pair in range(HIGHS // 2):
         right = []
@@ -183,9 +183,9 @@
     total_ref[:, HIGHS * LANES :] = dot(left, counting(high_ref[0 : steps * 512, :]))
 
 
-def add_segments(total_ref, digits_ref, at, rows):
-    left = low_table(across_lanes(digits_ref, at, 2))
-    high = lax.shift_right_arithmetic(down_rows(digits_ref, at, 2), 9)
+def add_segments(total_ref, pairs, rows):
+    left = low_table(across_lanes(pairs))
+    high = lax.shift_right_arithmetic(down_rows(pairs), 9)
     for pair in range(HIGHS // 2):
         right = jnp.concatenate([masked(rows, high, 2 * pair + side) for side in range(2)], axis=1)
         total_ref[:, lane_slice(pair, 2 * LANES)] += dot(left, right)
@@ -200,10 +200,17 @@
     return slab_ref[pl.ds(group * 16, 16), HALF:CAP, :].reshape(256, LANES).astype(F32)
 
 
-def mark_live(digits_ref, live_ref):
-    for group in range(live_ref.shape[0]):
-        most = jnp.max(digits_ref[16 + 2 * group : 18 + 2 * group, :])
-        live_ref[group] = jnp.where(most > 0.0, 1, 0)
+def mark_live(digits_ref, live_ref, order_ref):
+    groups = live_ref.shape[0]
+    count, dead = 0, 0
+    for group in range(groups):
+        live = jnp.where(jnp.max(digits_ref[16 + 2 * group : 18 + 2 * group, :]) > 0.0, 1, 0)
+        live_ref[group] = live
+        order_ref[count] = group
+        count = count + live
+        dead = jnp.where(live > 0, dead, group)
+    order_ref[count] = dead
+    return lax.shift_right_logical(count + 1, 1)
 
 
 def parent_kernel(
@@ -229,20 +236,32 @@
     store.wait()
 
 
-def find_parents(digits_ref, parents_ref, table_ref, at, count):
+def find_parents(rows, table_ref):
     line = iota((LANES, LANES), 0)
-    rows = [(digits_ref[pl.ds(at + n, 1), :], digits_ref[pl.ds(at + n + 32, 1), :]) for n in range(count)]
     left = [jnp.where(line == high.astype(I32) - 1, 1.0, 0.0).astype(BF16) for high, _ in rows]
     found = dot(table_ref[...], jnp.concatenate(left, axis=1))
-    for n in range(count):
-        chosen = jnp.where((line & 63) == rows[n][1].astype(I32) - 1, found[:, lane_slice(n)], 0.0)
-        parents_ref[pl.ds(at + n, 1), :] = jnp.sum(chosen[0:64], axis=0, keepdims=True)
-        parents_ref[pl.ds(at + n + 32, 1), :] = jnp.sum(chosen[64:128], axis=0, keepdims=True)
+    parents = []
+    for n, (_, low) in enumerate(rows):
+        chosen = jnp.where((line & 63) == low.astype(I32) - 1, found[:, lane_slice(n)], 0.0)
+        parents.append(
+            (
+                jnp.sum(chosen[0:64], axis=0, keepdims=True),
+                jnp.sum(chosen[64:128], axis=0, keepdims=True),
+            )
+        )
+    return parents
+
+
+def two_groups(slab_ref, digits_ref, order_ref, pair):
+    groups = [order_ref[2 * pair + side] for side in range(2)]
+    labels = [row for group in groups for row in label_rows(digits_ref, 16 + 2 * group, 2)]
+    return labels, jnp.concatenate([upper_rows(slab_ref, group) for group in groups], axis=0)
 
 
 def upper_kernel(
     slab_ref, table_ref, top_ref, start_hbm, send_hbm, slab_hbm,
-    digits_ref, parents_ref, total_ref, left_ref, high_ref, start_ref, send_ref, right_ref, tail_ref, live_ref,
+    digits_ref, parents_ref, total_ref, left_ref, high_ref, start_ref, send_ref, right_ref, tail_ref,
+    live_ref, order_ref,
     sems,
 ):
     load = pltpu.make_async_copy(start_hbm, start_ref, sems.at[0])
@@ -250,20 +269,19 @@
     keep = pltpu.make_async_copy(slab_ref, slab_hbm, sems.at[2 + HIGHS])
     keep.start()
     slot_digits(slab_ref, digits_ref)
-    mark_live(digits_ref, live_ref)
+    pairs_live = mark_live(digits_ref, live_ref, order_ref)
     for step in range(4):
-        find_parents(digits_ref, parents_ref, table_ref, 4 * step, 4)
+        for n, (high, low) in enumerate(find_parents(label_rows(digits_ref, 4 * step, 4), table_ref)):
+            parents_ref[4 * step + n : 4 * step + n + 1, :] = high
+            parents_ref[4 * step + n + 32 : 4 * step + n + 33, :] = low
     segments(total_ref, left_ref, high_ref, lambda step: lower_rows(slab_ref, step), parents_ref, 4)
 
-    def more(group, carry):
-        @pl.when(live_ref[group] > 0)
-        def _():
-            find_parents(digits_ref, parents_ref, table_ref, 16 + 2 * group, 2)
-            add_segments(total_ref, parents_ref, 16 + 2 * group, upper_rows(slab_ref, group))
-
+    def more(pair, carry):
+        labels, rows = two_groups(slab_ref, digits_ref, order_ref, pair)
+        add_segments(total_ref, find_parents(labels, table_ref), rows)
         return carry
 
-    lax.fori_loop(0, slab_ref.shape[0] // 16, more, 0)
+    lax.fori_loop(0, pairs_live, more, 0)
     load.wait()
     at = slice(HIGHS * LANES, (HIGHS + 1) * LANES)
     weights = total_ref[:, at] + start_ref[:, at]
@@ -313,7 +331,7 @@
 
 def level_kernel(
     slab_hbm, old_hbm, level_hbm, residual_hbm,
-    slab_ref, digits_ref, total_ref, table_ref, left_ref, high_ref, old_ref, level_ref, residual_ref, live_ref,
+    slab_ref, digits_ref, total_ref, table_ref, left_ref, high_ref, old_ref, level_ref, residual_ref, live_ref, order_ref,
     load_sem, slab_sem, level_sems, low_sems, up_sems,
 ):
     fetch = pltpu.make_async_copy(slab_hbm, slab_ref, slab_sem)
@@ -322,18 +340,16 @@
     load.start()
     fetch.wait()
     slot_digits(slab_ref, digits_ref)
-    mark_live(digits_ref, live_ref)
+    pairs_live = mark_live(digits_ref, live_ref, order_ref)
     segments(total_ref, left_ref, high_ref, lambda step: lower_rows(slab_ref, step), digits_ref, 4)
     groups = slab_ref.shape[0] // 16
 
-    def more(group, carry):
-        @pl.when(live_ref[group] > 0)
-        def _():
-            add_segments(total_ref, digits_ref, 16 + 2 * group, upper_rows(slab_ref, group))
-
+    def more(pair, carry):
+        labels, rows = two_groups(slab_ref, digits_ref, order_ref, pair)
+        add_segments(total_ref, labels, rows)
         return carry
 
-    lax.fori_loop(0, groups, more, 0)
+    lax.fori_loop(0, pairs_live, more, 0)
     load.wait()
     inverse = 1.0 / (total_ref[:, HIGHS * LANES :] + 1.0)
     stores = []
@@ -349,7 +365,7 @@
         stores[-1].start()
 
     def subtract(at, count, rows):
-        label = down_rows(digits_ref, at, count)
+        label = down_rows(label_rows(digits_ref, at, count))
         low = label & (LOW - 1)
         high = lax.shift_right_arithmetic(label, 9)
         lane = iota(label.shape, 1)
@@ -544,6 +560,7 @@
             pltpu.VMEM((HIGHS * LOW, 2 * LANES), BF16),
             pltpu.VMEM((owners, 8, lanes), F32),
             pltpu.SMEM((groups,), I32),
+            pltpu.SMEM((groups + 1,), I32),
             pltpu.SemaphoreType.DMA((3 + HIGHS,)),
         ],
         flops=work,
@@ -567,6 +584,7 @@
             pltpu.VMEM((block, lanes), F32),
             pltpu.VMEM((devices, CAP // 8, 8, lanes), BF16),
             pltpu.SMEM((groups,), I32),
+            pltpu.SMEM((groups + 1,), I32),
             pltpu.SemaphoreType.DMA(()),
             pltpu.SemaphoreType.DMA(()),
             pltpu.SemaphoreType.DMA((HIGHS,)),

time: 98.5 us -> 97.8 us (level)
  Pallas kernels: 32.1 us -> 35.6 us
  waiting for transfers between devices: 17.9 us -> 15.5 us
  starting transfers between devices: 18.2 us -> 16.8 us
    all_to_all x2, waiting for transfers between devices: 17.9 us -> 15.4 us  [swap(): return lax.all_to_all(value, axes, split_axis=0, concat_axis=0, tiled=True)]
    pallas_call x1, Pallas kernels: 9.38 us -> 11.5 us  [on_device(): call(level_kernel, (shape((block, lanes), F32), shape(answer_dims, BF16))...]
    all_to_all x2, starting transfers between devices: 16.6 us -> 15.2 us  [swap(): return lax.all_to_all(value, axes, split_axis=0, concat_axis=0, tiled=True)]
    pallas_call x1, Pallas kernels: 5.99 us -> 7.32 us  [on_device(): call(upper_kernel, (pltpu.HBM((owners, 35, 8, lanes), BF16), pltpu.HBM((d...]
  transfers between devices with their start and end apart: 3 -> 3, of which waited for: 2 -> 2; matrix products, arithmetic and copies ran while one was open for 0% -> 0% of each run, Pallas kernels for 21% -> 24%
where the time goes in v13:
time: 97.8 us; the launch traced here: 97.4 us
  Pallas kernels  35.6 us (36%)
  blocking collectives  28.3 us (29%)
  starting transfers between devices  16.8 us (17%)
  waiting for transfers between devices  15.5 us (16%)
    all_to_all x1, blocking collectives, swap(): return lax.all_to_all(value, axes, split_axis=0, concat_axis=0, tiled=True)  28.3 us
    all_to_all x2, waiting for transfers between devices, swap(): return lax.all_to_all(value, axes, split_axis=0, concat_axis=0, tiled=True)  15.4 us
    all_to_all x2, starting transfers between devices, swap(): return lax.all_to_all(value, axes, split_axis=0, concat_axis=0, tiled=True)  15.2 us
    pallas_call x1, Pallas kernels, on_device(): call(level_kernel, (shape((block, lanes), F32), shape(answer_dims, BF16))...  11.5 us
    pallas_call x1, Pallas kernels, on_device(): call(parent_kernel, (pltpu.HBM(total_dims, F32), shape((count, slots), BF...  10.3 us
    pallas_call x1, Pallas kernels, on_device(): call(upper_kernel, (pltpu.HBM((owners, 35, 8, lanes), BF16), pltpu.HBM((d...  7.32 us
    pallas_call x1, Pallas kernels, on_device(): call(pack_kernel, pltpu.HBM((groups, owners, rows, lanes), BF16), [HBM, H...  3.11 us
  transfers between devices with their start and end apart: 3, of which 2 were waited for; matrix products, arithmetic and copies ran while one was open for 0% of the time, Pallas kernels for 24%

profile of v13, /device:TPU:1, one launch (start us, length us, event | category | flops | bytes accessed | tf_op | source)
XLA Modules:
  0.0 97.4 jit_solution(2691317626870702113)
XLA Ops:
  0.6 3.1 %shard_map.84 = bf16[8,16,40,128]{3,2,1,0:T(8,128)(2,1)} custom-call(s32[1,256]{1,0:T(1,128)} %bitcast.21, bf16[256,1024]{1,0:T(8,128)(2,1)} %points_hbm.1), custom_call_target="tpu_custom_call" | custom-call | flops 268435456 | bytes 4194304 | tf_op jit(solution)/shard_map/pallas_call | solution.py:511
  3.7 0.0 copy-start.2
  3.8 11.5 %all-to-all-start = ((bf16[128,40,128]{2,1,0:T(8,128)(2,1)}), bf16[128,40,128]{2,1,0:T(8,128)(2,1)S(1)}, u32[]{:S(2)}, u32[]{:S(2)}) async-start(bf16[128,40,128]{2,1,0:T(8,128)(2,1)} %bitcast.16), calls=%async_computation | async-start | bytes 2621440 | tf_op jit(solution)/shard_map/all_to_all | solution.py:495
  15.3 0.0 copy-done.2
  15.3 0.1 shift_right_logical.14
  15.4 0.1 copy.11
  15.4 0.1 and.14
  15.5 0.1 copy.12
  15.6 0.0 copy-start.1
  15.7 10.3 %shard_map.85 = (f32[512,1152]{1,0:T(8,128)}, bf16[256,512]{1,0:T(8,128)(2,1)}) custom-call(s32[32,128]{1,0:T(8,128)} %bitcast.20, bf16[4096,128]{1,0:T(8,128)(2,1)} %old_hbm.1, s32[1,256]{1,0:T(1,128)} %bitcast.22), custom_call_target="tpu_custom_call" | custom-call | flops 4831838208 | bytes 4194304 | tf_op jit(solution)/shard_map/pallas_call | solution.py:527
  25.9 10.7 %all-to-all-done.slab_ref = bf16[128,40,128]{2,1,0:T(8,128)(2,1)S(1)} async-done(((bf16[128,40,128]{2,1,0:T(8,128)(2,1)}), bf16[128,40,128]{2,1,0:T(8,128)(2,1)S(1)}, u32[]{:S(2)}, u32[]{:S(2)}) %all-to-all-start) | async-done | bytes 1310752 | tf_op jit(solution)/shard_map/all_to_all | solution.py:495
  36.6 0.0 copy-done.1
  36.6 7.3 %shard_map.86 = (bf16[16,35,8,128]{3,2,1,0:T(8,128)(2,1)}, bf16[128,40,128]{2,1,0:T(8,128)(2,1)}) custom-call(bf16[128,40,128]{2,1,0:T(8,128)(2,1)S(1)} %all-to-all-done.slab_ref, bf16[128,128]{1,0:T(8,128)(2,1)S(1)} %pad.5.table_ref, s32[32,128]{1,0:T(8,128)S(1)} %bitcast.15, f32[512,1152]{1,0:T(8,128)} %get-tuple-element.14.start_hbm), custom_call_target="tpu_custom_call" | custom-call | flops 4831838208 | bytes 4194304 | tf_op jit(solution)/shard_map/pallas_call | solution.py:546
  43.9 3.7 %all-to-all-start.1 = ((bf16[16,35,8,128]{3,2,1,0:T(8,128)(2,1)}), bf16[16,35,8,128]{3,2,1,0:T(8,128)(2,1)S(1)}, u32[]{:S(2)}, u32[]{:S(2)}) async-start(bf16[16,35,8,128]{3,2,1,0:T(8,128)(2,1)} %get-tuple-element.17), calls=%async_computation.1 | async-start | bytes 2293760 | tf_op jit(solution)/shard_map/all_to_all | solution.py:495
  47.7 11.5 %shard_map.87 = (f32[4096,128]{1,0:T(8,128)}, bf16[128,5,8,128]{3,2,1,0:T(8,128)(2,1)S(1)}) custom-call(bf16[128,40,128]{2,1,0:T(8,128)(2,1)} %get-tuple-element.15.slab_hbm, bf16[4096,128]{1,0:T(8,128)(2,1)} %old_hbm.1), custom_call_target="tpu_custom_call" | custom-call | flops 9663676416 | bytes 4194304 | tf_op jit(solution)/shard_map/pallas_call | solution.py:570
  59.2 4.8 %all-to-all-done.1 = bf16[16,35,8,128]{3,2,1,0:T(8,128)(2,1)S(1)} async-done(((bf16[16,35,8,128]{3,2,1,0:T(8,128)(2,1)}), bf16[16,35,8,128]{3,2,1,0:T(8,128)(2,1)S(1)}, u32[]{:S(2)}, u32[]{:S(2)}) %all-to-all-start.1) | async-done | bytes 1146912 | tf_op jit(solution)/shard_map/all_to_all | solution.py:495
  63.9 1.3 %shard_map.88 = (f32[256,128]{1,0:T(8,128)}, bf16[128,5,8,128]{3,2,1,0:T(8,128)(2,1)S(1)}) custom-call(bf16[16,280,128]{2,1,0:T(8,128)(2,1)S(1)} %bitcast.13, bf16[128,5,8,128]{3,2,1,0:T(8,128)(2,1)S(1)} %get-tuple-element.18.send_in), custom_call_target="tpu_custom_call", output_to_operand_aliasing={{1}: (1, {})} | custom-call | bytes 4194304 | tf_op jit(solution)/shard_map/pallas_call | solution.py:597
  65.2 0.0 copy-start
  65.2 28.3 %all_to_all.15 = bf16[128,5,8,128]{3,2,1,0:T(8,128)(2,1)S(1)} all-to-all(bf16[128,5,8,128]{3,2,1,0:T(8,128)(2,1)S(1)} %get-tuple-element.20), channel_id=1, replica_groups=mesh['dp'=8,'cent'=16] {'dp','cent'}, dimensions={0} | all-to-all | bytes 2621440 | tf_op jit(solution)/shard_map/all_to_all | solution.py:495
  93.5 1.6 %collective-permute-start = (bf16[128,8,128]{2,1,0:T(8,128)(2,1)S(1)}, bf16[128,8,128]{2,1,0:T(8,128)(2,1)S(1)}, u32[]{:S(2)}, u32[]{:S(2)}) collective-permute-start(bf16[128,8,128]{2,1,0:T(8,128)(2,1)S(1)} %slice_bitcast_fusion), channel_id=1, source_target_pairs={{0,16},{16,0},{32,48},{48,32},{64,80},{80,64},{96,112},{112,96},{1... | collective-permute-start | bytes 786440 | tf_op jit(solution)/shard_map/ppermute | solution.py:614
  95.1 0.0 copy-done
  95.1 1.3 %shard_map.89 = (bf16[256,1024]{1,0:T(8,128)(2,1)}, f32[16,2,8,1024]{3,2,1,0:T(8,128)}) custom-call(bf16[256,512]{1,0:T(8,128)(2,1)S(1)} %copy-done, bf16[8,16,40,128]{3,2,1,0:T(8,128)(2,1)S(1)} %bitcast.12), custom_call_target="tpu_custom_call" | custom-call | flops 268435456 | bytes 4194304 | tf_op jit(solution)/shard_map/pallas_call | solution.py:616
  96.4 0.0 collective-permute-done
  96.4 0.9 shard_map.90
  (4 shorter events, 0.1 us)
Async XLA Ops:
  3.7 11.5 %copy-start.2 = (s32[4096]{0:T(1024)S(1)}, s32[4096]{0:T(1024)}, u32[]{:S(2)}) copy-start(s32[4096]{0:T(1024)} %param.7) | copy-start | bytes 49156
  3.8 32.9 %all-to-all-start = ((bf16[128,40,128]{2,1,0:T(8,128)(2,1)}), bf16[128,40,128]{2,1,0:T(8,128)(2,1)S(1)}, u32[]{:S(2)}, u32[]{:S(2)}) async-start(bf16[128,40,128]{2,1,0:T(8,128)(2,1)} %bitcast.16), calls=%async_computation | async-start | bytes 2621440 | tf_op jit(solution)/shard_map/all_to_all | solution.py:495
  15.6 21.0 %copy-start.1 = (s32[4096]{0:T(1024)S(1)}, s32[4096]{0:T(1024)}, u32[]{:S(2)}) copy-start(s32[4096]{0:T(1024)} %param.8) | copy-start | bytes 49156
  43.9 20.0 %all-to-all-start.1 = ((bf16[16,35,8,128]{3,2,1,0:T(8,128)(2,1)}), bf16[16,35,8,128]{3,2,1,0:T(8,128)(2,1)S(1)}, u32[]{:S(2)}, u32[]{:S(2)}) async-start(bf16[16,35,8,128]{3,2,1,0:T(8,128)(2,1)} %get-tuple-element.17), calls=%async_computation.1 | async-start | bytes 2293760 | tf_op jit(solution)/shard_map/all_to_all | solution.py:495
  65.2 29.9 %copy-start = (bf16[256,512]{1,0:T(8,128)(2,1)S(1)}, bf16[256,512]{1,0:T(8,128)(2,1)}, u32[]{:S(2)}) copy-start(bf16[256,512]{1,0:T(8,128)(2,1)} %get-tuple-element.21.back_ref) | copy-start | bytes 786436
  93.5 2.8 %collective-permute-start = (bf16[128,8,128]{2,1,0:T(8,128)(2,1)S(1)}, bf16[128,8,128]{2,1,0:T(8,128)(2,1)S(1)}, u32[]{:S(2)}, u32[]{:S(2)}) collective-permute-start(bf16[128,8,128]{2,1,0:T(8,128)(2,1)S(1)} %slice_bitcast_fusion), channel_id=1, source_target_pairs={{0,16},{16,0},{32,48},{48,32},{64,80},{80,64},{96,112},{112,96},{1... | collective-permute-start | bytes 786440 | tf_op jit(solution)/shard_map/ppermute | solution.py:614
